TPU v7x, 256 devices: a whole 4x4x8 slice. The times are simulated.
256 devices in a mesh: walker: 16 (over x, y), param: 16 (over z, core).
Axes of the slice: x: 4, y: 4, z: 8, core: 2. Of those that a mesh axis runs over, the one named last changes fastest.
Arguments:
- occupation: int32 [16, 4096], P(None, 'walker'), may hold values from 0 to 1023
- inverse_slater: float32 [16, 16, 4096], P(None, None, 'walker'), may hold values from -1.5 to 1.5
- orbitals: float32 [1024, 512], replicated, may hold values from -6 to 6
- hop_orbitals: float32 [1024, 512], replicated, may hold values from -6 to 6
- local_energy: float32 [4096], P('walker'), may hold values from -6 to 6
- excitations: int32 [4, 65536], P(None, 'param'), may hold values from 0 to 511, as said below
- initial_block: float32 [65536, 8], P('param'), may hold values from -6 to 6
Outputs:
- basis_scaled: float32 [65536, 32], P('param')
- proj_h: float32 [32, 32], replicated
- proj_s: float32 [32, 32], replicated
Inputs may be any that keep to these rules, and one draw needn't show every extreme that they name: `excitations`: rows 0 and 1 name two different electrons below 16; rows 2 and 3 name two different orbitals.
All inputs are finite; a program needn't handle non-finite values.
Results may differ from a plain program's by a relative error of at most 0.025.
Values may be sent and summed in bfloat16 or wider, within the bound.
No kernel may reach another device: no remote copies, remote signals or barrier semaphores. Data moves between devices by JAX's collectives and lax.ppermute only.
A program may use at most 128 MiB of HBM per device.

v0:
```python
import math

import jax
import jax.numpy as jnp
from jax import lax
from jax.sharding import PartitionSpec as P

ITERS = 3


EPS_SHIFT = 0.001
ENERGY_SHIFT = 0.5


def as_sent(array):
    return jax.tree.map(lambda a: a.astype(jnp.bfloat16) if a.dtype == jnp.float32 else a, array)


def orthonormal(vectors, gram_matrix):
    lower_factor = jnp.linalg.cholesky(gram_matrix)
    return jax.scipy.linalg.solve_triangular(lower_factor, vectors.T, lower=True).T


def dot_sums(values):
    return lax.psum(values, ("walker", "param"))


def on_device(
    occupation, inverse_slater, orbitals, hop_orbitals, local_energy, excitations, initial_block
):
    highest = lax.Precision.HIGHEST
    orbital_count = orbitals.shape[1]
    electrons = occupation.shape[0]
    local_walkers = local_energy.shape[0]
    walkers = local_walkers * lax.axis_size("walker")
    block_rows = excitations.shape[1]
    columns = initial_block.shape[1]
    params = block_rows * lax.axis_size("param")
    owned_rows = block_rows // lax.axis_size("walker")
    orbital_rows = jnp.take(orbitals, occupation, axis=0)
    hopped_rows = jnp.take(hop_orbitals, occupation, axis=0)
    ratios = jnp.einsum("ikw,kwa->iaw", inverse_slater, orbital_rows, precision=highest).reshape(
        electrons * orbital_count, local_walkers
    )
    energy_ratios = jnp.einsum(
        "ikw,kwa->iaw", inverse_slater, hopped_rows, precision=highest
    ).reshape(electrons * orbital_count, local_walkers)
    first = excitations[0] * orbital_count + excitations[2]
    second = excitations[1] * orbital_count + excitations[3]
    cross_one = excitations[0] * orbital_count + excitations[3]
    cross_two = excitations[1] * orbital_count + excitations[2]
    ratio_ia = jnp.take(ratios, first, axis=0)
    ratio_jb = jnp.take(ratios, second, axis=0)
    ratio_ib = jnp.take(ratios, cross_one, axis=0)
    ratio_ja = jnp.take(ratios, cross_two, axis=0)
    energy_ia = jnp.take(energy_ratios, first, axis=0)
    energy_jb = jnp.take(energy_ratios, second, axis=0)
    energy_ib = jnp.take(energy_ratios, cross_one, axis=0)
    energy_ja = jnp.take(energy_ratios, cross_two, axis=0)
    raw = ratio_ia * ratio_jb - ratio_ib * ratio_ja
    energy_raw = (
        local_energy[None, :] * raw
        + energy_ia * ratio_jb
        + ratio_ia * energy_jb
        - energy_ib * ratio_ja
        - ratio_ib * energy_ja
    )
    derivs = raw.astype(jnp.bfloat16)
    energy_derivs = energy_raw.astype(jnp.bfloat16)
    wide = derivs.astype(jnp.float32)
    local_sums = jnp.stack(
        [
            jnp.sum(wide, axis=1),
            jnp.sum(wide * wide, axis=1),
            jnp.sum(energy_derivs.astype(jnp.float32), axis=1),
        ]
    )
    column_sums = lax.psum(local_sums.astype(jnp.bfloat16), "walker").astype(jnp.float32)
    mean_o = column_sums[0] / walkers
    mean_h = column_sums[2] / walkers
    diagonal_block = column_sums[1] / walkers - mean_o * mean_o + EPS_SHIFT
    contract = (((0,), (0,)), ((), ()))
    offset = lax.axis_index("walker") * owned_rows
    block = lax.dynamic_slice_in_dim(initial_block, offset, owned_rows, 0)
    s_diagonal = lax.dynamic_slice_in_dim(diagonal_block, offset, owned_rows, 0)
    block = orthonormal(block, dot_sums(jnp.dot(block.T, block, precision=highest)))
    basis_list = []
    s_images = []
    h_images = []
    for iteration in range(ITERS + 1):
        block_b = block.astype(jnp.bfloat16)
        fold_piece = lax.all_gather(block_b, "walker", axis=0, tiled=True)
        totals = jnp.concatenate(
            [
                lax.dot_general(derivs, fold_piece, contract, preferred_element_type=jnp.float32),
                lax.dot_general(
                    energy_derivs, fold_piece, contract, preferred_element_type=jnp.float32
                ),
            ],
            axis=1,
        )
        piece_wide = fold_piece.astype(jnp.float32)
        centering = jnp.concatenate(
            [
                jnp.dot(mean_o, piece_wide, precision=highest),
                jnp.dot(mean_h, piece_wide, precision=highest),
            ]
        )
        partial_value = totals - centering[None, :]
        row_images = lax.psum(partial_value, "param").astype(jnp.bfloat16)
        images = lax.psum_scatter(
            jnp.dot(derivs, row_images, preferred_element_type=jnp.float32).astype(jnp.bfloat16),
            "walker",
            scatter_dimension=0,
            tiled=True,
        ).astype(jnp.float32)
        s_image = images[:, :columns] / walkers + EPS_SHIFT * block
        h_image = images[:, columns:] / walkers + ENERGY_SHIFT * block
        s_image, h_image = (s_image, h_image)
        basis_list.append(block)
        s_images.append(s_image)
        h_images.append(h_image)
        if iteration < ITERS:
            a_matrix, b_matrix = dot_sums(
                (
                    jnp.dot(block.T, s_image, precision=highest),
                    jnp.dot(block.T, h_image, precision=highest),
                )
            )
            rayleigh = jax.scipy.linalg.cho_solve((jnp.linalg.cholesky(a_matrix), True), b_matrix)
            residual = h_image - jnp.dot(s_image, rayleigh, precision=highest)
            correction = residual / s_diagonal[:, None]
            earlier = jnp.concatenate(basis_list, axis=1)
            correlation = dot_sums(jnp.dot(earlier.T, correction, precision=highest))
            correction = correction - jnp.dot(earlier, correlation, precision=highest)
            gram_matrix = dot_sums(jnp.dot(correction.T, correction, precision=highest))
            block = orthonormal(correction, gram_matrix)
    whole_basis = jnp.concatenate(basis_list, axis=1)
    proj_s, proj_h = dot_sums(
        (
            jnp.dot(whole_basis.T, jnp.concatenate(s_images, axis=1), precision=highest),
            jnp.dot(whole_basis.T, jnp.concatenate(h_images, axis=1), precision=highest),
        )
    )
    whole_basis = lax.all_gather(as_sent(whole_basis), "walker", axis=0, tiled=True).astype(
        whole_basis.dtype
    )
    return (math.sqrt(params) * whole_basis, proj_h, proj_s)


def solution(mesh):
    placed = (
        P(None, "walker"),
        P(None, None, "walker"),
        P(),
        P(),
        P("walker"),
        P(None, "param"),
        P("param", None),
    )
    return jax.shard_map(
        on_device,
        mesh=mesh,
        in_specs=placed,
        out_specs=(P("param", None), P(), P()),
        check_vma=False,
    )
```

profile of v0, /device:TPU:1, one launch (start us, length us, event | category | flops | bytes accessed | tf_op | source)
XLA Modules:
  0.0 1803.4 jit_solution(7476823142489259958)
XLA Ops:
  57.4 19.5 %gather_fusion.9 = f32[4096,256]{1,0:T(8,128)} fusion(f32[8192,256]{1,0:T(8,128)} %bitcast.248, s32[4096]{0:T(1024)S(1)} %fusion.44), kind=kCustom, calls=%fused_computation.9.clone | custom fusion | bytes 8404992 | tf_op jit(solution)/shard_map/jit(_take)/gather | solution.py:59
  76.9 19.6 %gather_fusion.8 = f32[4096,256]{1,0:T(8,128)} fusion(f32[8192,256]{1,0:T(8,128)} %bitcast.249, s32[4096]{0:T(1024)S(1)} %fusion.43), kind=kCustom, calls=%fused_computation.8.clone | custom fusion | bytes 8404992 | tf_op jit(solution)/shard_map/jit(_take)/gather | solution.py:58
  160.1 19.5 %gather_fusion.3 = f32[4096,256]{1,0:T(8,128)} fusion(f32[8192,256]{1,0:T(8,128)} %bitcast.253, s32[4096]{0:T(1024)S(1)} %fusion.43), kind=kCustom, calls=%fused_computation.4.clone | custom fusion | bytes 8404992 | tf_op jit(solution)/shard_map/jit(_take)/gather | solution.py:54
  218.5 19.5 %gather_fusion.6 = f32[4096,256]{1,0:T(8,128)} fusion(f32[8192,256]{1,0:T(8,128)} %bitcast.251, s32[4096]{0:T(1024)S(1)} %fusion.41), kind=kCustom, calls=%fused_computation.6.clone | custom fusion | bytes 8404992 | tf_op jit(solution)/shard_map/jit(_take)/gather | solution.py:56
  258.3 81.4 %psum.140 = f32[8,8]{0,1:T(8,128)S(1)} all-reduce(f32[8,8]{0,1:T(8,128)S(1)} %fusion.65), channel_id=1, replica_groups=mesh['walker'=16,'param'=16] {'walker','param'}, use_global_device_ids=true, to_apply=%region_0.1 | all-reduce | flops 64 | bytes 512 | tf_op jit(solution)/shard_map/psum | solution.py:25
  373.3 58.2 %psum.141 = bf16[3,4096]{1,0:T(4,128)(2,1)S(1)} all-reduce(bf16[3,4096]{1,0:T(4,128)(2,1)S(1)} %pad_maximum_fusion), channel_id=1, replica_groups=mesh['walker'=16,'param'=16] {'walker'}, use_global_device_ids=true, to_apply=%region_6.0 | all-reduce | flops 12288 | bytes 49152 | tf_op jit(solution)/shard_map/psum | solution.py:78
  434.2 62.2 %psum.142 = bf16[256,16]{0,1:T(8,128)(2,1)S(1)} all-reduce(f32[256,16]{0,1:T(8,128)S(1)} %maximum_subtract_fusion), channel_id=1, replica_groups=mesh['walker'=16,'param'=16] {'param'}, use_global_device_ids=true, to_apply=%region_7.12 | all-reduce | flops 4096 | bytes 24576 | tf_op jit(solution)/shard_map/psum | solution.py:110
  497.9 69.7 %reduce-scatter.5.cloned.1.call-done = bf16[256,16]{0,1:T(8,128)(2,1)} async-done(((bf16[4096,16]{0,1:T(8,128)(2,1)}), bf16[256,16]{0,1:T(8,128)(2,1)}) %reduce-scatter.5.cloned.1.call-update) | async-done | bytes 8208 | tf_op jit(solution)/shard_map/reduce_scatter | solution.py:111
  568.6 77.5 %all-reduce.3 = (f32[8,8]{1,0:T(8,128)S(1)}, f32[8,8]{0,1:T(8,128)S(1)}) all-reduce(f32[8,8]{1,0:T(8,128)S(1)} %fusion.121, f32[8,8]{0,1:T(8,128)S(1)} %fusion.120), channel_id=1, replica_groups=mesh['walker'=16,'param'=16] {'walker','param'}, use_global_device_ids=true, to_apply=%region_10.15 | all-reduce | flops 128 | bytes 1024 | tf_op jit(solution)/shard_map/psum | solution.py:25
  649.5 73.3 %psum.145 = f32[8,8]{1,0:T(8,128)S(1)} all-reduce(f32[8,8]{1,0:T(8,128)S(1)} %fusion.122), channel_id=1, replica_groups=mesh['walker'=16,'param'=16] {'walker','param'}, use_global_device_ids=true, to_apply=%region_11.17 | all-reduce | flops 64 | bytes 512 | tf_op jit(solution)/shard_map/psum | solution.py:25
  723.2 73.0 %psum.146 = f32[8,8]{0,1:T(8,128)S(1)} all-reduce(f32[8,8]{0,1:T(8,128)S(1)} %fusion.123), channel_id=1, replica_groups=mesh['walker'=16,'param'=16] {'walker','param'}, use_global_device_ids=true, to_apply=%region_12.18 | all-reduce | flops 64 | bytes 512 | tf_op jit(solution)/shard_map/psum | solution.py:25
  819.7 48.2 %psum.147 = bf16[256,16]{0,1:T(8,128)(2,1)S(1)} all-reduce(f32[256,16]{0,1:T(8,128)S(1)} %maximum_subtract_fusion.1), channel_id=1, replica_groups=mesh['walker'=16,'param'=16] {'param'}, use_global_device_ids=true, to_apply=%region_13.19 | all-reduce | flops 4096 | bytes 24576 | tf_op jit(solution)/shard_map/psum | solution.py:110
  869.3 73.0 %reduce-scatter.7.cloned.1.call-done = bf16[256,16]{0,1:T(8,128)(2,1)} async-done(((bf16[4096,16]{0,1:T(8,128)(2,1)}), bf16[256,16]{0,1:T(8,128)(2,1)}) %reduce-scatter.7.cloned.1.call-update) | async-done | bytes 8208 | tf_op jit(solution)/shard_map/reduce_scatter | solution.py:111
  943.3 77.6 %all-reduce.2 = (f32[8,8]{1,0:T(8,128)S(1)}, f32[8,8]{0,1:T(8,128)S(1)}) all-reduce(f32[8,8]{1,0:T(8,128)S(1)} %fusion.127, f32[8,8]{0,1:T(8,128)S(1)} %fusion.126), channel_id=1, replica_groups=mesh['walker'=16,'param'=16] {'walker','param'}, use_global_device_ids=true, to_apply=%region_16.22 | all-reduce | flops 128 | bytes 1024 | tf_op jit(solution)/shard_map/psum | solution.py:25
  1024.2 73.4 %psum.150 = f32[16,8]{1,0:T(8,128)S(1)} all-reduce(f32[16,8]{1,0:T(8,128)S(1)} %fusion.39), channel_id=1, replica_groups=mesh['walker'=16,'param'=16] {'walker','param'}, use_global_device_ids=true, to_apply=%region_17.23 | all-reduce | flops 128 | bytes 1024 | tf_op jit(solution)/shard_map/psum | solution.py:25
  1097.9 73.0 %psum.151 = f32[8,8]{0,1:T(8,128)S(1)} all-reduce(f32[8,8]{0,1:T(8,128)S(1)} %fusion.128), channel_id=1, replica_groups=mesh['walker'=16,'param'=16] {'walker','param'}, use_global_device_ids=true, to_apply=%region_18.24 | all-reduce | flops 64 | bytes 512 | tf_op jit(solution)/shard_map/psum | solution.py:25
  1194.7 48.3 %psum.152 = bf16[256,16]{0,1:T(8,128)(2,1)S(1)} all-reduce(f32[256,16]{0,1:T(8,128)S(1)} %maximum_subtract_fusion.2), channel_id=1, replica_groups=mesh['walker'=16,'param'=16] {'param'}, use_global_device_ids=true, to_apply=%region_19.25 | all-reduce | flops 4096 | bytes 24576 | tf_op jit(solution)/shard_map/psum | solution.py:110
  1244.3 73.0 %reduce-scatter.9.cloned.1.call-done = bf16[256,16]{0,1:T(8,128)(2,1)} async-done(((bf16[4096,16]{0,1:T(8,128)(2,1)}), bf16[256,16]{0,1:T(8,128)(2,1)}) %reduce-scatter.9.cloned.1.call-update) | async-done | bytes 8208 | tf_op jit(solution)/shard_map/reduce_scatter | solution.py:111
  1318.3 77.5 %all-reduce.1 = (f32[8,8]{1,0:T(8,128)S(1)}, f32[8,8]{0,1:T(8,128)S(1)}) all-reduce(f32[8,8]{1,0:T(8,128)S(1)} %fusion.132, f32[8,8]{0,1:T(8,128)S(1)} %fusion.131), channel_id=1, replica_groups=mesh['walker'=16,'param'=16] {'walker','param'}, use_global_device_ids=true, to_apply=%region_22.28 | all-reduce | flops 128 | bytes 1024 | tf_op jit(solution)/shard_map/psum | solution.py:25
  1399.2 73.8 %psum.155 = f32[24,8]{1,0:T(8,128)S(1)} all-reduce(f32[24,8]{1,0:T(8,128)S(1)} %fusion.33), channel_id=1, replica_groups=mesh['walker'=16,'param'=16] {'walker','param'}, use_global_device_ids=true, to_apply=%region_23.29 | all-reduce | flops 192 | bytes 1536 | tf_op jit(solution)/shard_map/psum | solution.py:25
  1473.3 72.7 %psum.156 = f32[8,8]{0,1:T(8,128)S(1)} all-reduce(f32[8,8]{0,1:T(8,128)S(1)} %fusion.133), channel_id=1, replica_groups=mesh['walker'=16,'param'=16] {'walker','param'}, use_global_device_ids=true, to_apply=%region_24.30 | all-reduce | flops 64 | bytes 512 | tf_op jit(solution)/shard_map/psum | solution.py:25
  1587.4 53.8 %psum.157 = bf16[256,16]{0,1:T(8,128)(2,1)S(1)} all-reduce(f32[256,16]{0,1:T(8,128)S(1)} %maximum_subtract_fusion.3), channel_id=1, replica_groups=mesh['walker'=16,'param'=16] {'param'}, use_global_device_ids=true, to_apply=%region_25.31 | all-reduce | flops 4096 | bytes 24576 | tf_op jit(solution)/shard_map/psum | solution.py:110
  1645.0 72.8 %reduce-scatter.11.cloned.1.call-done = bf16[256,16]{0,1:T(8,128)(2,1)} async-done(((bf16[4096,16]{0,1:T(8,128)(2,1)}), bf16[256,16]{0,1:T(8,128)(2,1)}) %reduce-scatter.11.cloned.1.call-update) | async-done | bytes 8208 | tf_op jit(solution)/shard_map/reduce_scatter | solution.py:111
  1718.8 77.6 %all-reduce = (f32[32,32]{1,0:T(8,128)}, f32[32,32]{1,0:T(8,128)}) all-reduce(f32[32,32]{1,0:T(8,128)S(1)} %fusion.17, f32[32,32]{1,0:T(8,128)S(1)} %fusion.25), channel_id=1, replica_groups=mesh['walker'=16,'param'=16] {'walker','param'}, use_global_device_ids=true, to_apply=%region_27.33 | all-reduce | flops 2048 | bytes 16384 | tf_op jit(solution)/shard_map/psum | solution.py:25
  (173 shorter events, 320.9 us)
Async XLA Ops:
  7.2 6.3 copy-start
  7.2 560.5 %reduce-scatter.5.cloned.1.call-start = ((), (), s32[]{:S(2)}) async-start(), calls=%async_computation.4 | async-start | bytes 139264 | tf_op jit(solution)/shard_map/reduce_scatter | solution.py:111
  76.9 19.6 %copy-start.2 = (f32[1024,512]{1,0:T(8,128)S(1)}, f32[1024,512]{1,0:T(8,128)}, u32[]{:S(2)}) copy-start(f32[1024,512]{1,0:T(8,128)} %param.18) | copy-start | bytes 6291460
  237.9 121.3 %copy-start.4 = (f32[256]{0:T(256)S(1)}, f32[256]{0:T(256)}, u32[]{:S(2)}) copy-start(f32[256]{0:T(256)} %param.20) | copy-start | bytes 3076
  372.2 870.7 %copy-start.3 = (bf16[4096,256]{1,0:T(8,128)(2,1)}, bf16[4096,256]{1,0:T(8,128)(2,1)S(1)}, u32[]{:S(2)}) copy-start(bf16[4096,256]{1,0:T(8,128)(2,1)S(1)} %get-tuple-element.21) | copy-start | bytes 6291460
  497.7 444.5 %reduce-scatter.7.cloned.1.call-start = ((), (), s32[]{:S(2)}) async-start(), calls=%async_computation.5 | async-start | bytes 139264 | tf_op jit(solution)/shard_map/reduce_scatter | solution.py:111
  869.3 448.0 %reduce-scatter.9.cloned.1.call-start = ((), (), s32[]{:S(2)}) async-start(), calls=%async_computation.6 | async-start | bytes 139264 | tf_op jit(solution)/shard_map/reduce_scatter | solution.py:111
  1244.3 473.5 %reduce-scatter.11.cloned.1.call-start = ((), (), s32[]{:S(2)}) async-start(), calls=%async_computation.7 | async-start | bytes 139264 | tf_op jit(solution)/shard_map/reduce_scatter | solution.py:111
  1548.9 247.5 %copy-start.1 = (f32[1024,512]{1,0:T(8,128)S(1)}, f32[1024,512]{1,0:T(8,128)}, u32[]{:S(2)}) copy-start(f32[1024,512]{1,0:T(8,128)} %param.19) | copy-start | bytes 6291460
Sparse Core Ops, SparseCore 0:
  497.9 69.7 reduce-scatter.4
  869.4 72.8 reduce-scatter.6
  1244.4 72.8 reduce-scatter.8
  1644.3 73.4 reduce-scatter.10
where the time goes:
time: 1810 us; the launch traced here: 1800 us
  blocking collectives  1190 us (66%)
  waiting for transfers between devices  289 us (16%)
  local copies, waits for them, and re-layouts  213 us (12%)
  matrix products  60.8 us (3%)
  other arithmetic  39.5 us (2%)
    psum x11, blocking collectives, dot_sums(): return lax.psum(values, ('walker', 'param'))  831 us
    reduce_scatter x4, waiting for transfers between devices, on_device(): lax.psum_scatter(jnp.dot(derivs, row_images, preferred_element_type=jnp.f...  288 us
    psum x4, blocking collectives, on_device(): row_images = lax.psum(partial_value, 'param').astype(jnp.bfloat16)  212 us
    all_gather x4, blocking collectives, on_device(): fold_piece = lax.all_gather(block_b, 'walker', axis=0, tiled=True)  68.7 us
    psum x1, blocking collectives, on_device(): lax.psum(local_sums.astype(jnp.bfloat16), 'walker').astype(jnp.float32)  58.2 us
  transfers between devices with their start and end apart: 4, of which 4 were waited for; matrix products, arithmetic and copies ran while one was open for 0% of the time, Pallas kernels for 0%

commit v1 on v0

v1 whole, which is shorter than its diff:
```python
import math

import jax
import jax.numpy as jnp
from jax import lax
from jax.sharding import PartitionSpec as P

ITERS = 3
EPS_SHIFT = 0.001
ENERGY_SHIFT = 0.5
HIGHEST = lax.Precision.HIGHEST


def dot_nt(left, right):
    return lax.dot_general(
        left, right, (((1,), (1,)), ((), ())), precision=HIGHEST, preferred_element_type=jnp.float32
    )


def dot_nn(left, right):
    return jnp.dot(left, right, precision=HIGHEST, preferred_element_type=jnp.float32)


def exchange(parts, axis):
    return lax.all_to_all(lax.optimization_barrier(parts), axis, 0, 0)


def to_all(value, axis):
    copies = jnp.broadcast_to(value[None], (lax.axis_size(axis),) + value.shape)
    return exchange(copies, axis)


def by_owner(values, owners):
    rows = values.shape[0]
    return values.reshape(rows, owners, -1).transpose(1, 0, 2)


def pad_columns(values, columns):
    return jnp.pad(values, ((0, 0), (0, columns - values.shape[1])))


def split_in_two(values):
    high = lax.reduce_precision(values, exponent_bits=8, mantissa_bits=7)
    return jnp.concatenate([high, values - high]).astype(jnp.bfloat16)


def forward(vectors, derivs, energy_derivs):
    count = vectors.shape[0]
    halves = split_in_two(vectors)
    images = []
    for table in (derivs, energy_derivs):
        both = jnp.dot(halves, table, preferred_element_type=jnp.float32)
        images.append(both[:count] + both[count:])
    return jnp.concatenate(images)


def build(occupation, inverse_slater, orbitals, hop_orbitals, local_energy, excitations):
    orbital_count = orbitals.shape[1]
    electrons = occupation.shape[0]
    local_walkers = local_energy.shape[0]
    orbital_rows = jnp.take(orbitals, occupation, axis=0)
    hopped_rows = jnp.take(hop_orbitals, occupation, axis=0)
    ratios = jnp.einsum("ikw,kwa->iaw", inverse_slater, orbital_rows, precision=HIGHEST).reshape(
        electrons * orbital_count, local_walkers
    )
    energy_ratios = jnp.einsum(
        "ikw,kwa->iaw", inverse_slater, hopped_rows, precision=HIGHEST
    ).reshape(electrons * orbital_count, local_walkers)
    first = excitations[0] * orbital_count + excitations[2]
    second = excitations[1] * orbital_count + excitations[3]
    cross_one = excitations[0] * orbital_count + excitations[3]
    cross_two = excitations[1] * orbital_count + excitations[2]
    ratio_ia = jnp.take(ratios, first, axis=0)
    ratio_jb = jnp.take(ratios, second, axis=0)
    ratio_ib = jnp.take(ratios, cross_one, axis=0)
    ratio_ja = jnp.take(ratios, cross_two, axis=0)
    energy_ia = jnp.take(energy_ratios, first, axis=0)
    energy_jb = jnp.take(energy_ratios, second, axis=0)
    energy_ib = jnp.take(energy_ratios, cross_one, axis=0)
    energy_ja = jnp.take(energy_ratios, cross_two, axis=0)
    raw = ratio_ia * ratio_jb - ratio_ib * ratio_ja
    energy_raw = (
        local_energy[None, :] * raw
        + energy_ia * ratio_jb
        + ratio_ia * energy_jb
        - energy_ib * ratio_ja
        - ratio_ib * energy_ja
    )
    derivs = raw.astype(jnp.bfloat16)
    energy_derivs = energy_raw.astype(jnp.bfloat16)
    wide = derivs.astype(jnp.float32)
    sums = jnp.stack(
        [
            jnp.sum(wide, axis=1),
            jnp.sum(wide * wide, axis=1),
            jnp.sum(energy_derivs.astype(jnp.float32), axis=1),
        ]
    )
    return derivs, energy_derivs, sums


def inverse_factor(gram):
    lower_factor = jnp.linalg.cholesky(gram)
    return jax.scipy.linalg.solve_triangular(
        lower_factor, jnp.eye(gram.shape[0], dtype=gram.dtype), lower=True
    )


def on_device(
    occupation, inverse_slater, orbitals, hop_orbitals, local_energy, excitations, initial_block
):
    walker_devices = lax.axis_size("walker")
    local_walkers = local_energy.shape[0]
    walkers = local_walkers * walker_devices
    block_rows = excitations.shape[1]
    count = initial_block.shape[1]
    params = block_rows * lax.axis_size("param")
    owned = block_rows // walker_devices
    derivs, energy_derivs, sums = build(
        occupation, inverse_slater, orbitals, hop_orbitals, local_energy, excitations
    )
    start = initial_block.T

    def across_params(images, grams):
        sent = jnp.concatenate([images, pad_columns(grams, local_walkers)])
        total = jnp.sum(to_all(sent, "param"), axis=0)
        return total[: 2 * count], total[2 * count :, : grams.shape[1]]

    images, gram = across_params(
        forward(start, derivs, energy_derivs), dot_nt(start, start)
    )
    factor = inverse_factor(gram)
    totals = jnp.concatenate([dot_nn(factor, images[:count]), dot_nn(factor, images[count:])])
    center_part = jnp.sum(totals, axis=1)
    sent = jnp.concatenate(
        [
            by_owner(sums, walker_devices),
            jnp.broadcast_to(
                jnp.pad(center_part, (0, owned - 2 * count))[None, None], (walker_devices, 1, owned)
            ),
        ],
        axis=1,
    )
    total = jnp.sum(exchange(sent, "walker"), axis=0) / walkers
    means = jnp.stack([total[0], total[2]])
    s_diagonal = total[1] - total[0] * total[0] + EPS_SHIFT
    center = total[3, : 2 * count]

    offset = lax.axis_index("walker") * owned
    block = dot_nn(factor, lax.dynamic_slice_in_dim(start, offset, owned, 1))
    whole = [dot_nn(factor, start)]
    basis = [block]
    all_totals = [totals]
    all_centers = [center]
    all_rows = []
    for iteration in range(ITERS + 1):
        row_images = (totals - center[:, None]).astype(jnp.bfloat16)
        all_rows.append(row_images)
        if iteration == ITERS:
            break
        back = lax.dot_general(
            row_images, derivs, (((1,), (1,)), ((), ())), preferred_element_type=jnp.float32
        )
        inner = lax.dot_general(
            totals[:count],
            row_images.astype(jnp.float32),
            (((1,), (1,)), ((), ())),
            precision=HIGHEST,
        )
        sent = jnp.concatenate(
            [
                by_owner(back, walker_devices),
                jnp.broadcast_to(
                    pad_columns(inner, owned)[None], (walker_devices, count, owned)
                ),
            ],
            axis=1,
        )
        total = jnp.sum(exchange(sent, "walker"), axis=0) / walkers
        inner = total[2 * count :, : 2 * count]
        a_matrix = inner[:, :count] + EPS_SHIFT * jnp.eye(count)
        b_matrix = inner[:, count:] + ENERGY_SHIFT * jnp.eye(count)
        s_image = total[:count] + EPS_SHIFT * block
        h_image = total[count : 2 * count] + ENERGY_SHIFT * block
        rayleigh = jax.scipy.linalg.cho_solve((jnp.linalg.cholesky(a_matrix), True), b_matrix)
        correction = (h_image - dot_nn(rayleigh.T, s_image)) / s_diagonal[None]
        grams = dot_nt(correction, jnp.concatenate(basis + [correction, means]))
        got = to_all(
            jnp.concatenate([correction, pad_columns(grams, 128)], axis=1), "walker"
        )
        grams = jnp.sum(got[:, :, owned : owned + grams.shape[1]], axis=0)
        whole_correction = got[:, :, :owned].transpose(1, 0, 2).reshape(count, block_rows)
        images, grams = across_params(
            forward(whole_correction, derivs, energy_derivs), grams
        )
        earlier = count * (iteration + 1)
        overlap = grams[:, :earlier]
        gram = grams[:, earlier : earlier + count] - dot_nt(overlap, overlap)
        factor = inverse_factor(gram)

        def advance(new, old):
            return dot_nn(factor, new - dot_nn(overlap, old))

        block = advance(correction, jnp.concatenate(basis))
        whole.append(advance(whole_correction, jnp.concatenate(whole)))
        totals = jnp.concatenate(
            [
                advance(images[:count], jnp.concatenate([t[:count] for t in all_totals])),
                advance(images[count:], jnp.concatenate([t[count:] for t in all_totals])),
            ]
        )
        center = jnp.concatenate(
            [
                advance(
                    grams[:, earlier + count + part : earlier + count + part + 1],
                    jnp.concatenate([c[part * count : (part + 1) * count] for c in all_centers])[
                        :, None
                    ],
                )[:, 0]
                for part in range(2)
            ]
        )
        basis.append(block)
        all_totals.append(totals)
        all_centers.append(center)
    lefts = jnp.concatenate([t[:count] for t in all_totals])
    rights = jnp.concatenate(
        [r[:count] for r in all_rows] + [r[count:] for r in all_rows]
    ).astype(jnp.float32)
    proj = jnp.sum(to_all(dot_nt(lefts, rights), "walker"), axis=0) / walkers
    size = lefts.shape[0]
    proj_s = proj[:, :size] + EPS_SHIFT * jnp.eye(size)
    proj_h = proj[:, size:] + ENERGY_SHIFT * jnp.eye(size)
    return (math.sqrt(params) * jnp.concatenate(whole).T, proj_h, proj_s)


def solution(mesh):
    placed = (
        P(None, "walker"),
        P(None, None, "walker"),
        P(),
        P(),
        P("walker"),
        P(None, "param"),
        P("param", None),
    )
    return jax.shard_map(
        on_device,
        mesh=mesh,
        in_specs=placed,
        out_specs=(P("param", None), P(), P()),
        check_vma=False,
    )
```

time: 1810 us -> 501 us (0.28)
  blocking collectives: 1190 us -> 40 us
  waiting for transfers between devices: 289 us -> 90.2 us
  starting transfers between devices: 0.16 us -> 45 us
    psum x16 -> x0, blocking collectives: 1100 us -> none  [the longest x11 831 us: dot_sums(): return lax.psum(values, ('walker', 'param'))]
    reduce_scatter x4 -> x0, waiting for transfers between devices: 288 us -> none  [on_device(): lax.psum_scatter(jnp.dot(derivs, row_images, preferred_element_type=jnp.f...]
    all_to_all x0 -> x9, waiting for transfers between devices: none -> 90.2 us  [exchange(): return lax.all_to_all(lax.optimization_barrier(parts), axis, 0, 0)]
    all_gather x5 -> x0, blocking collectives: 84.9 us -> none  [the longest x4 68.7 us: on_device(): fold_piece = lax.all_gather(block_b, 'walker', axis=0, tiled=True)]
    all_to_all x0 -> x9, starting transfers between devices: none -> 45 us  [exchange(): return lax.all_to_all(lax.optimization_barrier(parts), axis, 0, 0)]
    all_to_all x0 -> x3, blocking collectives: none -> 40 us  [exchange(): return lax.all_to_all(lax.optimization_barrier(parts), axis, 0, 0)]
    dot_general x43 -> x65, matrix products: 58.3 us -> 56.7 us  [the longest x1 17.2 us: build(): jnp.einsum('ikw,kwa->iaw', inverse_slater, hopped_rows, precision=HIGHEST)]
  transfers between devices with their start and end apart: 4 -> 9, of which waited for: 4 -> 9; matrix products, arithmetic and copies ran while one was open for 0% -> 1% of each run, Pallas kernels for 0% -> 0%
where the time goes in v1:
time: 501 us; the launch traced here: 499 us
  local copies, waits for them, and re-layouts  221 us (44%)
  waiting for transfers between devices  90.2 us (18%)
  matrix products  58.5 us (12%)
  starting transfers between devices  45 us (9%)
  other arithmetic  42.7 us (9%)
  blocking collectives  40 us (8%)
    all_to_all x9, waiting for transfers between devices, exchange(): return lax.all_to_all(lax.optimization_barrier(parts), axis, 0, 0)  90.2 us
    all_to_all x9, starting transfers between devices, exchange(): return lax.all_to_all(lax.optimization_barrier(parts), axis, 0, 0)  45 us
    all_to_all x3, blocking collectives, exchange(): return lax.all_to_all(lax.optimization_barrier(parts), axis, 0, 0)  40 us
    gather x1, local copies, waits for them, and re-layouts, build(): ratio_ib = jnp.take(ratios, cross_one, axis=0)  19.6 us
    gather x1, local copies, waits for them, and re-layouts, build(): energy_ia = jnp.take(energy_ratios, first, axis=0)  19.5 us
    gather x1, local copies, waits for them, and re-layouts, build(): ratio_ja = jnp.take(ratios, cross_two, axis=0)  19.5 us
    gather x1, local copies, waits for them, and re-layouts, build(): ratio_ia = jnp.take(ratios, first, axis=0)  19.5 us
    gather x1, local copies, waits for them, and re-layouts, build(): energy_ib = jnp.take(energy_ratios, cross_one, axis=0)  19.5 us
  transfers between devices with their start and end apart: 9, of which 9 were waited for; matrix products, arithmetic and copies ran while one was open for 1% of the time, Pallas kernels for 0%

profile of v1, /device:TPU:1, one launch (start us, length us, event | category | flops | bytes accessed | tf_op | source)
XLA Modules:
  0.0 498.9 jit_solution(1216446000242735209)
XLA Ops:
  6.9 16.8 %gather_fusion = f32[4096,512]{1,0:T(8,128)} fusion(f32[1024,512]{1,0:T(8,128)S(1)} %copy-done, s32[4096]{0:T(1024)S(1)} %broadcast_clamp_fusion), kind=kCustom, calls=%fused_computation.clone | custom fusion | bytes 16793600 | tf_op jit(solution)/shard_map/jit(_take)/gather | solution.py:61
  23.7 17.2 %fusion.13 = f32[16,512,256]{1,0,2:T(8,128)} fusion(f32[16,16,256]{1,0,2:T(8,128)} %copy.328, f32[16,256,512]{2,1,0:T(8,128)} %bitcast.325, pred[16,256]{0,1:T(8,128)(4,1)S(1)} %copy.326), kind=kOutput, calls=%fused_computation.36 | convolution fusion | flops 404750336 | bytes 17043456 | tf_op jit(solution)/shard_map/ikw,kwa->iaw/dot_general | solution.py:63
  40.9 9.9 %copy.407 = f32[16,512,256]{2,1,0:T(8,128)} copy(f32[16,512,256]{1,0,2:T(8,128)} %fusion.13) | data formatting | bytes 16777216 | tf_op jit(solution)/shard_map/reshape | solution.py:63
  50.9 19.5 %gather_fusion.4 = f32[4096,256]{1,0:T(8,128)} fusion(f32[8192,256]{1,0:T(8,128)} %bitcast.316, s32[4096]{0:T(1024)S(1)} %get-tuple-element.37), kind=kCustom, calls=%fused_computation.5.clone | custom fusion | bytes 8404992 | tf_op jit(solution)/shard_map/jit(_take)/gather | solution.py:76
  70.4 19.6 %gather_fusion.3 = f32[4096,256]{1,0:T(8,128)} fusion(f32[8192,256]{1,0:T(8,128)} %bitcast.317, s32[4096]{0:T(1024)S(1)} %get-tuple-element.36), kind=kCustom, calls=%fused_computation.4.clone | custom fusion | bytes 8404992 | tf_op jit(solution)/shard_map/jit(_take)/gather | solution.py:75
  90.0 16.8 %gather_fusion.5 = f32[4096,512]{1,0:T(8,128)} fusion(f32[1024,512]{1,0:T(8,128)S(1)} %copy-done.2, s32[4096]{0:T(1024)S(1)} %broadcast_clamp_fusion), kind=kCustom, calls=%fused_computation.2.clone | custom fusion | bytes 16793600 | tf_op jit(solution)/shard_map/jit(_take)/gather | solution.py:62
  106.8 17.2 %fusion.14 = f32[16,512,256]{1,0,2:T(8,128)} fusion(f32[16,16,256]{1,0,2:T(8,128)} %copy.328, f32[16,256,512]{2,1,0:T(8,128)} %bitcast.324, pred[16,256]{0,1:T(8,128)(4,1)S(1)} %copy.326), kind=kOutput, calls=%fused_computation.37 | convolution fusion | flops 404750336 | bytes 17043456 | tf_op jit(solution)/shard_map/ikw,kwa->iaw/dot_general | solution.py:66
  124.0 9.9 %copy.408 = f32[16,512,256]{2,1,0:T(8,128)} copy(f32[16,512,256]{1,0,2:T(8,128)} %fusion.14) | data formatting | bytes 16777216 | tf_op jit(solution)/shard_map/reshape | solution.py:68
  133.9 19.4 %gather_fusion.9 = f32[4096,256]{1,0:T(8,128)} fusion(f32[8192,256]{1,0:T(8,128)} %bitcast.320, s32[4096]{0:T(1024)S(1)} %get-tuple-element.37), kind=kCustom, calls=%fused_computation.9.clone | custom fusion | bytes 8404992 | tf_op jit(solution)/shard_map/jit(_take)/gather | solution.py:80
  153.4 19.5 %gather_fusion.8 = f32[4096,256]{1,0:T(8,128)} fusion(f32[8192,256]{1,0:T(8,128)} %bitcast.321, s32[4096]{0:T(1024)S(1)} %get-tuple-element.36), kind=kCustom, calls=%fused_computation.8.clone | custom fusion | bytes 8404992 | tf_op jit(solution)/shard_map/jit(_take)/gather | solution.py:79
  172.8 19.4 %gather_fusion.2 = f32[4096,256]{1,0:T(8,128)} fusion(f32[8192,256]{1,0:T(8,128)} %bitcast.318, s32[4096]{0:T(1024)S(1)} %get-tuple-element.35), kind=kCustom, calls=%fused_computation.3.clone | custom fusion | bytes 8404992 | tf_op jit(solution)/shard_map/jit(_take)/gather | solution.py:74
  192.3 19.5 %gather_fusion.7 = f32[4096,256]{1,0:T(8,128)} fusion(f32[8192,256]{1,0:T(8,128)} %bitcast.322, s32[4096]{0:T(1024)S(1)} %get-tuple-element.35), kind=kCustom, calls=%fused_computation.7.clone | custom fusion | bytes 8404992 | tf_op jit(solution)/shard_map/jit(_take)/gather | solution.py:78
  211.7 19.5 %gather_fusion.1 = f32[4096,256]{1,0:T(8,128)} fusion(f32[8192,256]{1,0:T(8,128)} %bitcast.319, s32[4096]{0:T(1024)S(1)} %get-tuple-element.34), kind=kCustom, calls=%fused_computation.1.clone | custom fusion | bytes 8404992 | tf_op jit(solution)/shard_map/jit(_take)/gather | solution.py:73
  231.2 19.5 %gather_fusion.6 = f32[4096,256]{1,0:T(8,128)} fusion(f32[8192,256]{1,0:T(8,128)} %bitcast.323, s32[4096]{0:T(1024)S(1)} %get-tuple-element.34), kind=kCustom, calls=%fused_computation.6.clone | custom fusion | bytes 8404992 | tf_op jit(solution)/shard_map/jit(_take)/gather | solution.py:77
  251.1 14.1 %convert_reduce_fusion = (f32[4096]{0:T(1024)S(1)}, f32[4096]{0:T(1024)S(1)}, bf16[4096,256]{1,0:T(8,128)(2,1)S(1)}, f32[4096]{0:T(1024)S(1)}, bf16[4096,256]{1,0:T(8,128)(2,1)S(1)}) fusion(f32[4096,256]{1,0:T(8,128)} %gather_fusion.4, pred[4096]{0:T(1024)(128)(4,1)S(1)} %get-tuple-element.38, f32[4096,256]{1,0:T(8,128)} %gather_fusion.3, ...), kind=kLoop, calls=%fused_computation.15 | loop fusion | flops 29347840 | bytes 37815296 | tf_op jit(solution)/shard_map/reduce_sum | solution.py:94
  268.1 10.0 %all-to-all-start = ((f32[16,24,256]{2,1,0:T(8,128)}), f32[16,24,256]{2,1,0:T(8,128)S(1)}, u32[]{:S(2)}, u32[]{:S(2)}) async-start(f32[16,24,256]{2,1,0:T(8,128)} %broadcast_in_dim.43), calls=%async_computation | async-start | bytes 786432 | tf_op jit(solution)/shard_map/all_to_all | solution.py:25
  278.2 14.5 %all-to-all-done = f32[16,24,256]{2,1,0:T(8,128)S(1)} async-done(((f32[16,24,256]{2,1,0:T(8,128)}), f32[16,24,256]{2,1,0:T(8,128)S(1)}, u32[]{:S(2)}, u32[]{:S(2)}) %all-to-all-start) | async-done | bytes 393248 | tf_op jit(solution)/shard_map/all_to_all | solution.py:25
  329.4 10.3 %all_to_all.60 = f32[16,8,384]{2,1,0:T(8,128)S(1)} all-to-all(f32[16,8,384]{2,1,0:T(8,128)S(1)} %broadcast_in_dim.46), channel_id=1, replica_groups=mesh['walker'=16,'param'=16] {'walker'}, dimensions={0} | all-to-all | bytes 393216 | tf_op jit(solution)/shard_map/all_to_all | solution.py:25
  342.2 19.7 %all_to_all.61 = f32[16,24,256]{2,1,0:T(8,128)S(1)} all-to-all(f32[16,24,256]{2,1,0:T(8,128)S(1)} %broadcast_in_dim.47), channel_id=1, replica_groups=mesh['walker'=16,'param'=16] {'param'}, dimensions={0} | all-to-all | bytes 786432 | tf_op jit(solution)/shard_map/all_to_all | solution.py:25
  372.6 9.6 %all-to-all-done.5 = f32[16,24,256]{2,1,0:T(8,128)S(1)} async-done(((f32[16,24,256]{2,1,0:T(8,128)}), f32[16,24,256]{2,1,0:T(8,128)S(1)}, u32[]{:S(2)}, u32[]{:S(2)}) %all-to-all-start.5) | async-done | bytes 393248 | tf_op jit(solution)/shard_map/all_to_all | solution.py:25
  386.4 10.0 %all_to_all.62 = f32[16,8,384]{2,1,0:T(8,128)S(1)} all-to-all(f32[16,8,384]{2,1,0:T(8,128)S(1)} %broadcast_in_dim.49), channel_id=1, replica_groups=mesh['walker'=16,'param'=16] {'walker'}, dimensions={0} | all-to-all | bytes 393216 | tf_op jit(solution)/shard_map/all_to_all | solution.py:25
  405.4 13.9 %all-to-all-done.7 = f32[16,24,256]{2,1,0:T(8,128)S(1)} async-done(((f32[16,24,256]{2,1,0:T(8,128)}), f32[16,24,256]{2,1,0:T(8,128)S(1)}, u32[]{:S(2)}, u32[]{:S(2)}) %all-to-all-start.7) | async-done | bytes 393248 | tf_op jit(solution)/shard_map/all_to_all | solution.py:25
  430.2 9.3 %all-to-all-done.8 = f32[16,24,256]{2,1,0:T(8,128)S(1)} async-done(((f32[16,24,256]{2,1,0:T(8,128)}), f32[16,24,256]{2,1,0:T(8,128)S(1)}, u32[]{:S(2)}, u32[]{:S(2)}) %all-to-all-start.8) | async-done | bytes 393248 | tf_op jit(solution)/shard_map/all_to_all | solution.py:25
  465.4 14.0 %all-to-all-done.10 = f32[16,24,256]{2,1,0:T(8,128)S(1)} async-done(((f32[16,24,256]{2,1,0:T(8,128)}), f32[16,24,256]{2,1,0:T(8,128)S(1)}, u32[]{:S(2)}, u32[]{:S(2)}) %all-to-all-start.10) | async-done | bytes 393248 | tf_op jit(solution)/shard_map/all_to_all | solution.py:25
  (268 shorter events, 128.4 us)
Async XLA Ops:
  0.6 6.3 %copy-start = (f32[1024,512]{1,0:T(8,128)S(1)}, f32[1024,512]{1,0:T(8,128)}, u32[]{:S(2)}) copy-start(f32[1024,512]{1,0:T(8,128)} %param.18) | copy-start | bytes 6291460
  70.3 19.6 %copy-start.2 = (f32[1024,512]{1,0:T(8,128)S(1)}, f32[1024,512]{1,0:T(8,128)}, u32[]{:S(2)}) copy-start(f32[1024,512]{1,0:T(8,128)} %param.19) | copy-start | bytes 6291460
  231.2 19.5 %copy-start.5 = (f32[4096,8]{0,1:T(8,128)S(1)}, f32[4096,8]{0,1:T(8,128)}, u32[]{:S(2)}) copy-start(f32[4096,8]{0,1:T(8,128)} %param.22) | copy-start | bytes 393220
  231.2 19.9 %copy-start.6 = (f32[256]{0:T(256)S(1)}, f32[256]{0:T(256)}, u32[]{:S(2)}) copy-start(f32[256]{0:T(256)} %param.20) | copy-start | bytes 3076
  265.2 1.4 copy-start.4
  265.2 159.1 %copy-start.3 = (bf16[4096,256]{1,0:T(8,128)(2,1)}, bf16[4096,256]{1,0:T(8,128)(2,1)S(1)}, u32[]{:S(2)}) copy-start(bf16[4096,256]{1,0:T(8,128)(2,1)S(1)} %get-tuple-element.10) | copy-start | bytes 6291460
  268.1 24.5 %all-to-all-start = ((f32[16,24,256]{2,1,0:T(8,128)}), f32[16,24,256]{2,1,0:T(8,128)S(1)}, u32[]{:S(2)}, u32[]{:S(2)}) async-start(f32[16,24,256]{2,1,0:T(8,128)} %broadcast_in_dim.43), calls=%async_computation | async-start | bytes 786432 | tf_op jit(solution)/shard_map/all_to_all | solution.py:25
  296.7 13.7 %all-to-all-start.1 = ((f32[16,4,256]{2,1,0:T(4,128)}), f32[16,4,256]{2,1,0:T(4,128)S(1)}, u32[]{:S(2)}, u32[]{:S(2)}) async-start(f32[16,4,256]{2,1,0:T(4,128)} %pad_maximum_fusion.15), calls=%async_computation.1 | async-start | bytes 131072 | tf_op jit(solution)/shard_map/all_to_all | solution.py:25
  312.1 13.1 %all-to-all-start.2 = ((f32[16,24,256]{2,1,0:T(8,128)}), f32[16,24,256]{2,1,0:T(8,128)S(1)}, u32[]{:S(2)}, u32[]{:S(2)}) async-start(f32[16,24,256]{2,1,0:T(8,128)} %pad_maximum_fusion), calls=%async_computation.2 | async-start | bytes 786432 | tf_op jit(solution)/shard_map/all_to_all | solution.py:25
  368.3 13.9 %all-to-all-start.5 = ((f32[16,24,256]{2,1,0:T(8,128)}), f32[16,24,256]{2,1,0:T(8,128)S(1)}, u32[]{:S(2)}, u32[]{:S(2)}) async-start(f32[16,24,256]{2,1,0:T(8,128)} %pad_maximum_fusion.1), calls=%async_computation.5 | async-start | bytes 786432 | tf_op jit(solution)/shard_map/all_to_all | solution.py:25
  399.6 19.7 %all-to-all-start.7 = ((f32[16,24,256]{2,1,0:T(8,128)}), f32[16,24,256]{2,1,0:T(8,128)S(1)}, u32[]{:S(2)}, u32[]{:S(2)}) async-start(f32[16,24,256]{2,1,0:T(8,128)} %broadcast_in_dim.50), calls=%async_computation.7 | async-start | bytes 786432 | tf_op jit(solution)/shard_map/all_to_all | solution.py:25
  425.9 13.6 %all-to-all-start.8 = ((f32[16,24,256]{2,1,0:T(8,128)}), f32[16,24,256]{2,1,0:T(8,128)S(1)}, u32[]{:S(2)}, u32[]{:S(2)}) async-start(f32[16,24,256]{2,1,0:T(8,128)} %pad_maximum_fusion.2), calls=%async_computation.8 | async-start | bytes 786432 | tf_op jit(solution)/shard_map/all_to_all | solution.py:25
  444.3 10.4 %all-to-all-start.9 = ((f32[16,8,384]{2,1,0:T(8,128)}), f32[16,8,384]{2,1,0:T(8,128)S(1)}, u32[]{:S(2)}, u32[]{:S(2)}) async-start(f32[16,8,384]{2,1,0:T(8,128)} %broadcast_in_dim.52), calls=%async_computation.9 | async-start | bytes 393216 | tf_op jit(solution)/shard_map/all_to_all | solution.py:25
  454.8 44.1 %copy-start.1 = (f32[1024,512]{1,0:T(8,128)S(1)}, f32[1024,512]{1,0:T(8,128)}, u32[]{:S(2)}) copy-start(f32[1024,512]{1,0:T(8,128)} %param.18) | copy-start | bytes 6291460
  459.7 19.7 %all-to-all-start.10 = ((f32[16,24,256]{2,1,0:T(8,128)}), f32[16,24,256]{2,1,0:T(8,128)S(1)}, u32[]{:S(2)}, u32[]{:S(2)}) async-start(f32[16,24,256]{2,1,0:T(8,128)} %broadcast_in_dim.53), calls=%async_computation.10 | async-start | bytes 786432 | tf_op jit(solution)/shard_map/all_to_all | solution.py:25
  486.0 10.6 %all-to-all-start.11 = ((f32[16,1,2048]{2,1,0:T(1,128)}), f32[16,1,2048]{2,1,0:T(1,128)S(1)}, u32[]{:S(2)}, u32[]{:S(2)}) async-start(f32[16,1,2048]{2,1,0:T(1,128)} %reshape.344), calls=%async_computation.11 | async-start | bytes 262144 | tf_op jit(solution)/shard_map/all_to_all | solution.py:25

commit v2 on v1

--- a/solution.py
+++ b/solution.py
@@ -3,6 +3,8 @@
 import jax
 import jax.numpy as jnp
 from jax import lax
+from jax.experimental import pallas as pl
+from jax.experimental.pallas import tpu as pltpu
 from jax.sharding import PartitionSpec as P
 
 ITERS = 3
@@ -54,40 +56,131 @@
     return jnp.concatenate(images)
 
 
+LANES = 128
+ROWS = 8
+GROUP = 64
+
+
+def build_kernel(
+    place_ref, occupation_ref, inverse_ref, orbitals_ref, hop_ref, energy_ref,
+    derivs_ref, energy_derivs_ref,
+    high_ref, low_ref, sites_ref, rows_ref, wide_ref, table_ref, first_ref, second_ref,
+):
+    electrons, walkers = occupation_ref.shape
+    sites, orbitals = orbitals_ref.shape
+    params = derivs_ref.shape[0]
+    halves = walkers // LANES
+    tiles = orbitals // ROWS
+
+    for half in range(halves):
+        for row in range(electrons * electrons):
+            wide_ref[half, row] = jnp.broadcast_to(
+                inverse_ref[row : row + 1, half * LANES : (half + 1) * LANES], (ROWS, LANES)
+            )
+    for number, source in enumerate((orbitals_ref, hop_ref)):
+        for column in range(0, orbitals, LANES):
+            turned = source[:, column : column + LANES].T
+            high = turned.astype(jnp.bfloat16)
+            where = pl.ds(number * orbitals + column, LANES)
+            high_ref[where, :] = high
+            low_ref[where, :] = (turned - high.astype(jnp.float32)).astype(jnp.bfloat16)
+
+    def pick(electron, carry):
+        occupied = occupation_ref[pl.ds(electron, 1), :]
+        index = lax.broadcasted_iota(jnp.int32, (sites, walkers), 0)
+        sites_ref[...] = jnp.where(index == occupied, 1.0, 0.0).astype(jnp.bfloat16)
+        for row in range(0, 2 * orbitals, 256):
+            where = pl.ds(row, 256)
+            rows_ref[electron, where, :] = jnp.dot(
+                high_ref[where, :], sites_ref[...], preferred_element_type=jnp.float32
+            ) + jnp.dot(low_ref[where, :], sites_ref[...], preferred_element_type=jnp.float32)
+        return carry
+
+    lax.fori_loop(0, electrons, pick, 0)
+
+    def contract(tile, carry):
+        for half in range(halves):
+            lanes = slice(half * LANES, (half + 1) * LANES)
+            plain = [rows_ref[k, pl.ds(pl.multiple_of(tile * ROWS, ROWS), ROWS), lanes] for k in range(electrons)]
+            hopped = [
+                rows_ref[k, pl.ds(pl.multiple_of(orbitals + tile * ROWS, ROWS), ROWS), lanes]
+                for k in range(electrons)
+            ]
+            scale = energy_ref[0:1, lanes] * 0.5
+            for i in range(electrons):
+                weight = wide_ref[half, i * electrons]
+                ratio = weight * plain[0]
+                energy = weight * hopped[0]
+                for k in range(1, electrons):
+                    weight = wide_ref[half, i * electrons + k]
+                    ratio += weight * plain[k]
+                    energy += weight * hopped[k]
+                base = pl.multiple_of((i * tiles + tile) * 4 * ROWS, ROWS)
+                table_ref[pl.ds(base + half, ROWS, stride=4), :] = ratio
+                table_ref[pl.ds(base + 2 + half, ROWS, stride=4), :] = energy + scale * ratio
+        return carry
+
+    lax.fori_loop(0, tiles, contract, 0)
+
+    def pairs(group, carry):
+        for j in range(GROUP):
+
+            def take(which, part):
+                return table_ref[pl.ds(pl.multiple_of(place_ref[which * params + group * GROUP + j], 4) + part * 2, 2), :]
+
+            ia, jb, ib, ja = (take(which, 0) for which in range(4))
+            e_ia, e_jb, e_ib, e_ja = (take(which, 1) for which in range(4))
+            spot = pl.ds(2 * j, 2)
+            first_ref[spot, :] = ia * jb - ib * ja
+            second_ref[spot, :] = (e_ia * jb + ia * e_jb) - (e_ib * ja + ib * e_ja)
+        for source, target in ((first_ref, derivs_ref), (second_ref, energy_derivs_ref)):
+            for row in range(0, GROUP, 2 * ROWS):
+                for half in range(2):
+                    target[
+                        pl.ds(pl.multiple_of(group * GROUP + row, 2 * ROWS), 2 * ROWS),
+                        half * LANES : (half + 1) * LANES,
+                    ] = source[pl.ds(row * 2 + half, 2 * ROWS, stride=2), :].astype(jnp.bfloat16)
+        return carry
+
+    lax.fori_loop(0, params // GROUP, pairs, 0)
+
+
 def build(occupation, inverse_slater, orbitals, hop_orbitals, local_energy, excitations):
-    orbital_count = orbitals.shape[1]
-    electrons = occupation.shape[0]
-    local_walkers = local_energy.shape[0]
-    orbital_rows = jnp.take(orbitals, occupation, axis=0)
-    hopped_rows = jnp.take(hop_orbitals, occupation, axis=0)
-    ratios = jnp.einsum("ikw,kwa->iaw", inverse_slater, orbital_rows, precision=HIGHEST).reshape(
-        electrons * orbital_count, local_walkers
-    )
-    energy_ratios = jnp.einsum(
-        "ikw,kwa->iaw", inverse_slater, hopped_rows, precision=HIGHEST
-    ).reshape(electrons * orbital_count, local_walkers)
-    first = excitations[0] * orbital_count + excitations[2]
-    second = excitations[1] * orbital_count + excitations[3]
-    cross_one = excitations[0] * orbital_count + excitations[3]
-    cross_two = excitations[1] * orbital_count + excitations[2]
-    ratio_ia = jnp.take(ratios, first, axis=0)
-    ratio_jb = jnp.take(ratios, second, axis=0)
-    ratio_ib = jnp.take(ratios, cross_one, axis=0)
-    ratio_ja = jnp.take(ratios, cross_two, axis=0)
-    energy_ia = jnp.take(energy_ratios, first, axis=0)
-    energy_jb = jnp.take(energy_ratios, second, axis=0)
-    energy_ib = jnp.take(energy_ratios, cross_one, axis=0)
-    energy_ja = jnp.take(energy_ratios, cross_two, axis=0)
-    raw = ratio_ia * ratio_jb - ratio_ib * ratio_ja
-    energy_raw = (
-        local_energy[None, :] * raw
-        + energy_ia * ratio_jb
-        + ratio_ia * energy_jb
-        - energy_ib * ratio_ja
-        - ratio_ib * energy_ja
-    )
-    derivs = raw.astype(jnp.bfloat16)
-    energy_derivs = energy_raw.astype(jnp.bfloat16)
+    electrons, walkers = occupation.shape
+    sites, orbital_count = orbitals.shape
+    params = excitations.shape[1]
+
+    def place(electron, orbital):
+        row = electron * orbital_count + orbital
+        return row * 4
+
+    i, j, a, b = excitations
+    places = jnp.concatenate([place(i, a), place(j, b), place(i, b), place(j, a)])
+    vmem = pl.BlockSpec(memory_space=pltpu.VMEM)
+    derivs, energy_derivs = pl.pallas_call(
+        build_kernel,
+        out_shape=[jax.ShapeDtypeStruct((params, walkers), jnp.bfloat16)] * 2,
+        in_specs=[pl.BlockSpec(memory_space=pltpu.SMEM)] + [vmem] * 5,
+        out_specs=[vmem] * 2,
+        scratch_shapes=[
+            pltpu.VMEM((2 * orbital_count, sites), jnp.bfloat16),
+            pltpu.VMEM((2 * orbital_count, sites), jnp.bfloat16),
+            pltpu.VMEM((sites, walkers), jnp.bfloat16),
+            pltpu.VMEM((electrons, 2 * orbital_count, walkers), jnp.float32),
+            pltpu.VMEM((walkers // LANES, electrons * electrons, ROWS, LANES), jnp.float32),
+            pltpu.VMEM((electrons * orbital_count * 4, LANES), jnp.float32),
+            pltpu.VMEM((GROUP * 2, LANES), jnp.float32),
+            pltpu.VMEM((GROUP * 2, LANES), jnp.float32),
+        ],
+        compiler_params=pltpu.CompilerParams(vmem_limit_bytes=60 * 1024 * 1024),
+    )(
+        places,
+        occupation,
+        inverse_slater.reshape(electrons * electrons, walkers),
+        orbitals,
+        hop_orbitals,
+        local_energy[None],
+    )
     wide = derivs.astype(jnp.float32)
     sums = jnp.stack(
         [

time: 501 us -> 300 us (0.60)
  local copies, waits for them, and re-layouts: 221 us -> 7.01 us
  Pallas kernels: 0 us -> 61.9 us
  matrix products: 58.5 us -> 25 us
  other arithmetic: 42.7 us -> 31.8 us
    gather x10 -> x0, local copies, waits for them, and re-layouts: 189 us -> none  [the longest x1 19.6 us: build(): ratio_ib = jnp.take(ratios, cross_one, axis=0)]
    pallas_call x0 -> x1, Pallas kernels: none -> 61.9 us  [build(): pl.pallas_call(build_kernel, out_shape=[jax.ShapeDtypeStruct((params, wal...]
    dot_general x2 -> x0, matrix products: 34.4 us -> none  [the longest x1 17.2 us: build(): jnp.einsum('ikw,kwa->iaw', inverse_slater, hopped_rows, precision=HIGHEST)]
    reshape x2 -> x0, local copies, waits for them, and re-layouts: 19.9 us -> none  [the longest x1 9.95 us: build(): jnp.einsum('ikw,kwa->iaw', inverse_slater, orbital_rows, precision=HIGHEST)]
    reduce_sum x1, other arithmetic: 14.1 us -> 3.28 us  [build(): jnp.sum(wide, axis=1)]
  transfers between devices with their start and end apart: 9 -> 9, of which waited for: 9 -> 9; matrix products, arithmetic and copies ran while one was open for 1% -> 2% of each run, Pallas kernels for 0% -> 0%
where the time goes in v2:
time: 300 us; the launch traced here: 299 us
  waiting for transfers between devices  86.9 us (29%)
  Pallas kernels  61.9 us (21%)
  starting transfers between devices  44.8 us (15%)
  blocking collectives  40.1 us (13%)
  other arithmetic  31.8 us (11%)
  matrix products  25 us (8%)
  local copies, waits for them, and re-layouts  7.01 us (2%)
    all_to_all x9, waiting for transfers between devices, exchange(): return lax.all_to_all(lax.optimization_barrier(parts), axis, 0, 0)  86.9 us
    pallas_call x1, Pallas kernels, build(): pl.pallas_call(build_kernel, out_shape=[jax.ShapeDtypeStruct((params, wal...  61.9 us
    all_to_all x9, starting transfers between devices, exchange(): return lax.all_to_all(lax.optimization_barrier(parts), axis, 0, 0)  44.8 us
    all_to_all x3, blocking collectives, exchange(): return lax.all_to_all(lax.optimization_barrier(parts), axis, 0, 0)  40.1 us
    dot_general x8, matrix products, forward(): both = jnp.dot(halves, table, preferred_element_type=jnp.float32)  9.57 us
    dot_general x41, matrix products, dot_nn(): jnp.dot(left, right, precision=HIGHEST, preferred_element_type=jnp.float32)  8.46 us
  transfers between devices with their start and end apart: 9, of which 9 were waited for; matrix products, arithmetic and copies ran while one was open for 2% of the time, Pallas kernels for 0%

profile of v2, /device:TPU:1, one launch (start us, length us, event | category | flops | bytes accessed | tf_op | source)
XLA Modules:
  0.0 298.8 jit_solution(8817282661537337284)
XLA Ops:
  4.7 61.9 %shard_map.94 = (bf16[4096,256]{1,0:T(8,128)(2,1)}, bf16[4096,256]{1,0:T(8,128)(2,1)}) custom-call(s32[16384]{0:T(1024)} %pad_add_fusion.place_ref, s32[16,256]{1,0:T(8,128)} %occupation_ref.1, f32[256,256]{1,0:T(8,128)} %bitcast.317, f32[1024,512]{1,0:T(8,128)} %orbitals_ref.1, f32[1024,512]{1,0:T(8,128)} %hop_ref.1, f32[1,256]{1,0:T(1,128)} %bitcast.325), custom_call_target="tpu_custom_call" | custom-call | tf_op jit(solution)/shard_map/pallas_call | solution.py:160
  66.5 2.1 fusion.38
  69.9 10.0 %all-to-all-start = ((f32[16,24,256]{2,1,0:T(8,128)}), f32[16,24,256]{2,1,0:T(8,128)S(1)}, u32[]{:S(2)}, u32[]{:S(2)}) async-start(f32[16,24,256]{2,1,0:T(8,128)} %broadcast_in_dim.28), calls=%async_computation | async-start | bytes 786432 | tf_op jit(solution)/shard_map/all_to_all | solution.py:27
  80.0 3.3 %convert_reduce_fusion = (f32[4096]{0:T(1024)S(1)}, f32[4096]{0:T(1024)S(1)}, f32[4096]{0:T(1024)S(1)}) fusion(bf16[4096,256]{1,0:T(8,128)(2,1)S(1)} %copy-done, bf16[4096,256]{1,0:T(8,128)(2,1)} %get-tuple-element.9), kind=kLoop, calls=%fused_computation.1 | loop fusion | flops 6279168 | bytes 4243456 | tf_op jit(solution)/shard_map/reduce_sum | solution.py:187
  83.3 11.2 %all-to-all-done = f32[16,24,256]{2,1,0:T(8,128)S(1)} async-done(((f32[16,24,256]{2,1,0:T(8,128)}), f32[16,24,256]{2,1,0:T(8,128)S(1)}, u32[]{:S(2)}, u32[]{:S(2)}) %all-to-all-start) | async-done | bytes 393248 | tf_op jit(solution)/shard_map/all_to_all | solution.py:27
  98.6 6.7 %all-to-all-start.1 = ((f32[16,4,256]{2,1,0:T(4,128)}), f32[16,4,256]{2,1,0:T(4,128)S(1)}, u32[]{:S(2)}, u32[]{:S(2)}) async-start(f32[16,4,256]{2,1,0:T(4,128)} %pad_maximum_fusion.15), calls=%async_computation.1 | async-start | bytes 131072 | tf_op jit(solution)/shard_map/all_to_all | solution.py:27
  105.3 6.9 %all-to-all-done.1 = f32[16,4,256]{2,1,0:T(4,128)S(1)} async-done(((f32[16,4,256]{2,1,0:T(4,128)}), f32[16,4,256]{2,1,0:T(4,128)S(1)}, u32[]{:S(2)}, u32[]{:S(2)}) %all-to-all-start.1) | async-done | bytes 65568 | tf_op jit(solution)/shard_map/all_to_all | solution.py:27
  114.0 3.6 %all-to-all-start.2 = ((f32[16,24,256]{2,1,0:T(8,128)}), f32[16,24,256]{2,1,0:T(8,128)S(1)}, u32[]{:S(2)}, u32[]{:S(2)}) async-start(f32[16,24,256]{2,1,0:T(8,128)} %pad_maximum_fusion), calls=%async_computation.2 | async-start | bytes 786432 | tf_op jit(solution)/shard_map/all_to_all | solution.py:27
  117.8 9.0 %all-to-all-done.2 = f32[16,24,256]{2,1,0:T(8,128)S(1)} async-done(((f32[16,24,256]{2,1,0:T(8,128)}), f32[16,24,256]{2,1,0:T(8,128)S(1)}, u32[]{:S(2)}, u32[]{:S(2)}) %all-to-all-start.2) | async-done | bytes 393248 | tf_op jit(solution)/shard_map/all_to_all | solution.py:27
  130.9 10.3 %all_to_all.60 = f32[16,8,384]{2,1,0:T(8,128)S(1)} all-to-all(f32[16,8,384]{2,1,0:T(8,128)S(1)} %broadcast_in_dim.31), channel_id=1, replica_groups=mesh['walker'=16,'param'=16] {'walker'}, dimensions={0} | all-to-all | bytes 393216 | tf_op jit(solution)/shard_map/all_to_all | solution.py:27
  143.7 19.8 %all_to_all.61 = f32[16,24,256]{2,1,0:T(8,128)S(1)} all-to-all(f32[16,24,256]{2,1,0:T(8,128)S(1)} %broadcast_in_dim.32), channel_id=1, replica_groups=mesh['walker'=16,'param'=16] {'param'}, dimensions={0} | all-to-all | bytes 786432 | tf_op jit(solution)/shard_map/all_to_all | solution.py:27
  169.9 3.6 %all-to-all-start.5 = ((f32[16,24,256]{2,1,0:T(8,128)}), f32[16,24,256]{2,1,0:T(8,128)S(1)}, u32[]{:S(2)}, u32[]{:S(2)}) async-start(f32[16,24,256]{2,1,0:T(8,128)} %pad_maximum_fusion.1), calls=%async_computation.5 | async-start | bytes 786432 | tf_op jit(solution)/shard_map/all_to_all | solution.py:27
  174.2 9.6 %all-to-all-done.5 = f32[16,24,256]{2,1,0:T(8,128)S(1)} async-done(((f32[16,24,256]{2,1,0:T(8,128)}), f32[16,24,256]{2,1,0:T(8,128)S(1)}, u32[]{:S(2)}, u32[]{:S(2)}) %all-to-all-start.5) | async-done | bytes 393248 | tf_op jit(solution)/shard_map/all_to_all | solution.py:27
  188.0 10.0 %all_to_all.62 = f32[16,8,384]{2,1,0:T(8,128)S(1)} all-to-all(f32[16,8,384]{2,1,0:T(8,128)S(1)} %broadcast_in_dim.34), channel_id=1, replica_groups=mesh['walker'=16,'param'=16] {'walker'}, dimensions={0} | all-to-all | bytes 393216 | tf_op jit(solution)/shard_map/all_to_all | solution.py:27
  201.2 5.1 %all-to-all-start.7 = ((f32[16,24,256]{2,1,0:T(8,128)}), f32[16,24,256]{2,1,0:T(8,128)S(1)}, u32[]{:S(2)}, u32[]{:S(2)}) async-start(f32[16,24,256]{2,1,0:T(8,128)} %broadcast_in_dim.35), calls=%async_computation.7 | async-start | bytes 786432 | tf_op jit(solution)/shard_map/all_to_all | solution.py:27
  207.0 14.0 %all-to-all-done.7 = f32[16,24,256]{2,1,0:T(8,128)S(1)} async-done(((f32[16,24,256]{2,1,0:T(8,128)}), f32[16,24,256]{2,1,0:T(8,128)S(1)}, u32[]{:S(2)}, u32[]{:S(2)}) %all-to-all-start.7) | async-done | bytes 393248 | tf_op jit(solution)/shard_map/all_to_all | solution.py:27
  227.5 3.6 %all-to-all-start.8 = ((f32[16,24,256]{2,1,0:T(8,128)}), f32[16,24,256]{2,1,0:T(8,128)S(1)}, u32[]{:S(2)}, u32[]{:S(2)}) async-start(f32[16,24,256]{2,1,0:T(8,128)} %pad_maximum_fusion.2), calls=%async_computation.8 | async-start | bytes 786432 | tf_op jit(solution)/shard_map/all_to_all | solution.py:27
  231.8 9.3 %all-to-all-done.8 = f32[16,24,256]{2,1,0:T(8,128)S(1)} async-done(((f32[16,24,256]{2,1,0:T(8,128)}), f32[16,24,256]{2,1,0:T(8,128)S(1)}, u32[]{:S(2)}, u32[]{:S(2)}) %all-to-all-start.8) | async-done | bytes 393248 | tf_op jit(solution)/shard_map/all_to_all | solution.py:27
  245.9 3.5 %all-to-all-start.9 = ((f32[16,8,384]{2,1,0:T(8,128)}), f32[16,8,384]{2,1,0:T(8,128)S(1)}, u32[]{:S(2)}, u32[]{:S(2)}) async-start(f32[16,8,384]{2,1,0:T(8,128)} %broadcast_in_dim.37), calls=%async_computation.9 | async-start | bytes 393216 | tf_op jit(solution)/shard_map/all_to_all | solution.py:27
  249.7 6.7 %all-to-all-done.9 = f32[16,8,384]{2,1,0:T(8,128)S(1)} async-done(((f32[16,8,384]{2,1,0:T(8,128)}), f32[16,8,384]{2,1,0:T(8,128)S(1)}, u32[]{:S(2)}, u32[]{:S(2)}) %all-to-all-start.9) | async-done | bytes 196640 | tf_op jit(solution)/shard_map/all_to_all | solution.py:27
  259.6 5.2 %all-to-all-start.10 = ((f32[16,24,256]{2,1,0:T(8,128)}), f32[16,24,256]{2,1,0:T(8,128)S(1)}, u32[]{:S(2)}, u32[]{:S(2)}) async-start(f32[16,24,256]{2,1,0:T(8,128)} %broadcast_in_dim.38), calls=%async_computation.10 | async-start | bytes 786432 | tf_op jit(solution)/shard_map/all_to_all | solution.py:27
  265.3 14.0 %all-to-all-done.10 = f32[16,24,256]{2,1,0:T(8,128)S(1)} async-done(((f32[16,24,256]{2,1,0:T(8,128)}), f32[16,24,256]{2,1,0:T(8,128)S(1)}, u32[]{:S(2)}, u32[]{:S(2)}) %all-to-all-start.10) | async-done | bytes 393248 | tf_op jit(solution)/shard_map/all_to_all | solution.py:27
  285.8 3.5 %all-to-all-start.11 = ((f32[16,1,2048]{2,1,0:T(1,128)}), f32[16,1,2048]{2,1,0:T(1,128)S(1)}, u32[]{:S(2)}, u32[]{:S(2)}) async-start(f32[16,1,2048]{2,1,0:T(1,128)} %reshape.221), calls=%async_computation.11 | async-start | bytes 262144 | tf_op jit(solution)/shard_map/all_to_all | solution.py:27
  290.2 6.3 %all-to-all-done.11 = f32[16,1,2048]{2,1,0:T(1,128)S(1)} async-done(((f32[16,1,2048]{2,1,0:T(1,128)}), f32[16,1,2048]{2,1,0:T(1,128)S(1)}, u32[]{:S(2)}, u32[]{:S(2)}) %all-to-all-start.11) | async-done | bytes 131104 | tf_op jit(solution)/shard_map/all_to_all | solution.py:27
  (235 shorter events, 58.5 us)
Async XLA Ops:
  66.5 2.2 copy-start
  69.9 24.6 %all-to-all-start = ((f32[16,24,256]{2,1,0:T(8,128)}), f32[16,24,256]{2,1,0:T(8,128)S(1)}, u32[]{:S(2)}, u32[]{:S(2)}) async-start(f32[16,24,256]{2,1,0:T(8,128)} %broadcast_in_dim.28), calls=%async_computation | async-start | bytes 786432 | tf_op jit(solution)/shard_map/all_to_all | solution.py:27
  98.6 13.6 %all-to-all-start.1 = ((f32[16,4,256]{2,1,0:T(4,128)}), f32[16,4,256]{2,1,0:T(4,128)S(1)}, u32[]{:S(2)}, u32[]{:S(2)}) async-start(f32[16,4,256]{2,1,0:T(4,128)} %pad_maximum_fusion.15), calls=%async_computation.1 | async-start | bytes 131072 | tf_op jit(solution)/shard_map/all_to_all | solution.py:27
  112.5 5.1 %copy-start.1 = (f32[4096,8]{0,1:T(8,128)S(1)}, f32[4096,8]{0,1:T(8,128)}, u32[]{:S(2)}) copy-start(f32[4096,8]{0,1:T(8,128)} %param.18) | copy-start | bytes 393220
  114.0 12.8 %all-to-all-start.2 = ((f32[16,24,256]{2,1,0:T(8,128)}), f32[16,24,256]{2,1,0:T(8,128)S(1)}, u32[]{:S(2)}, u32[]{:S(2)}) async-start(f32[16,24,256]{2,1,0:T(8,128)} %pad_maximum_fusion), calls=%async_computation.2 | async-start | bytes 786432 | tf_op jit(solution)/shard_map/all_to_all | solution.py:27
  169.9 13.9 %all-to-all-start.5 = ((f32[16,24,256]{2,1,0:T(8,128)}), f32[16,24,256]{2,1,0:T(8,128)S(1)}, u32[]{:S(2)}, u32[]{:S(2)}) async-start(f32[16,24,256]{2,1,0:T(8,128)} %pad_maximum_fusion.1), calls=%async_computation.5 | async-start | bytes 786432 | tf_op jit(solution)/shard_map/all_to_all | solution.py:27
  201.2 19.7 %all-to-all-start.7 = ((f32[16,24,256]{2,1,0:T(8,128)}), f32[16,24,256]{2,1,0:T(8,128)S(1)}, u32[]{:S(2)}, u32[]{:S(2)}) async-start(f32[16,24,256]{2,1,0:T(8,128)} %broadcast_in_dim.35), calls=%async_computation.7 | async-start | bytes 786432 | tf_op jit(solution)/shard_map/all_to_all | solution.py:27
  227.5 13.6 %all-to-all-start.8 = ((f32[16,24,256]{2,1,0:T(8,128)}), f32[16,24,256]{2,1,0:T(8,128)S(1)}, u32[]{:S(2)}, u32[]{:S(2)}) async-start(f32[16,24,256]{2,1,0:T(8,128)} %pad_maximum_fusion.2), calls=%async_computation.8 | async-start | bytes 786432 | tf_op jit(solution)/shard_map/all_to_all | solution.py:27
  245.9 10.4 %all-to-all-start.9 = ((f32[16,8,384]{2,1,0:T(8,128)}), f32[16,8,384]{2,1,0:T(8,128)S(1)}, u32[]{:S(2)}, u32[]{:S(2)}) async-start(f32[16,8,384]{2,1,0:T(8,128)} %broadcast_in_dim.37), calls=%async_computation.9 | async-start | bytes 393216 | tf_op jit(solution)/shard_map/all_to_all | solution.py:27
  259.6 19.7 %all-to-all-start.10 = ((f32[16,24,256]{2,1,0:T(8,128)}), f32[16,24,256]{2,1,0:T(8,128)S(1)}, u32[]{:S(2)}, u32[]{:S(2)}) async-start(f32[16,24,256]{2,1,0:T(8,128)} %broadcast_in_dim.38), calls=%async_computation.10 | async-start | bytes 786432 | tf_op jit(solution)/shard_map/all_to_all | solution.py:27
  285.8 10.6 %all-to-all-start.11 = ((f32[16,1,2048]{2,1,0:T(1,128)}), f32[16,1,2048]{2,1,0:T(1,128)S(1)}, u32[]{:S(2)}, u32[]{:S(2)}) async-start(f32[16,1,2048]{2,1,0:T(1,128)} %reshape.221), calls=%async_computation.11 | async-start | bytes 262144 | tf_op jit(solution)/shard_map/all_to_all | solution.py:27

commit v3 on v2

--- a/solution.py
+++ b/solution.py
@@ -44,6 +44,17 @@
 def split_in_two(values):
     high = lax.reduce_precision(values, exponent_bits=8, mantissa_bits=7)
     return jnp.concatenate([high, values - high]).astype(jnp.bfloat16)
+
+
+def split_in_three(values):
+    high = lax.reduce_precision(values, exponent_bits=8, mantissa_bits=7)
+    rest = values - high
+    middle = lax.reduce_precision(rest, exponent_bits=8, mantissa_bits=7)
+    return jnp.concatenate([high, middle, rest - middle], axis=1).astype(jnp.bfloat16)
+
+
+def joined(thirds, columns):
+    return thirds[:, :columns] + thirds[:, columns : 2 * columns] + thirds[:, 2 * columns : 3 * columns]
 
 
 def forward(vectors, derivs, energy_derivs):
@@ -215,62 +226,64 @@
     start = initial_block.T
 
     def across_params(images, grams):
-        sent = jnp.concatenate([images, pad_columns(grams, local_walkers)])
-        total = jnp.sum(to_all(sent, "param"), axis=0)
-        return total[: 2 * count], total[2 * count :, : grams.shape[1]]
+        sent = jnp.concatenate(
+            [images.astype(jnp.bfloat16), pad_columns(split_in_three(grams), local_walkers)]
+        )
+        total = jnp.sum(to_all(sent, "param").astype(jnp.float32), axis=0)
+        return total[: 2 * count], joined(total[2 * count :], grams.shape[1])
 
     images, gram = across_params(
         forward(start, derivs, energy_derivs), dot_nt(start, start)
     )
     factor = inverse_factor(gram)
     totals = jnp.concatenate([dot_nn(factor, images[:count]), dot_nn(factor, images[count:])])
-    center_part = jnp.sum(totals, axis=1)
-    sent = jnp.concatenate(
-        [
-            by_owner(sums, walker_devices),
-            jnp.broadcast_to(
-                jnp.pad(center_part, (0, owned - 2 * count))[None, None], (walker_devices, 1, owned)
-            ),
-        ],
-        axis=1,
-    )
-    total = jnp.sum(exchange(sent, "walker"), axis=0) / walkers
-    means = jnp.stack([total[0], total[2]])
-    s_diagonal = total[1] - total[0] * total[0] + EPS_SHIFT
-    center = total[3, : 2 * count]
+    center = jnp.mean(totals, axis=1)
 
     offset = lax.axis_index("walker") * owned
     block = dot_nn(factor, lax.dynamic_slice_in_dim(start, offset, owned, 1))
     whole = [dot_nn(factor, start)]
     basis = [block]
     all_totals = [totals]
-    all_centers = [center]
+    all_centers = []
     all_rows = []
+    means = s_diagonal = None
     for iteration in range(ITERS + 1):
         row_images = (totals - center[:, None]).astype(jnp.bfloat16)
-        all_rows.append(row_images)
+        wide_rows = row_images.astype(jnp.float32)
         if iteration == ITERS:
+            all_centers.append(center)
+            all_rows.append(wide_rows)
             break
         back = lax.dot_general(
             row_images, derivs, (((1,), (1,)), ((), ())), preferred_element_type=jnp.float32
         )
-        inner = lax.dot_general(
-            totals[:count],
-            row_images.astype(jnp.float32),
-            (((1,), (1,)), ((), ())),
-            precision=HIGHEST,
-        )
+        inner = dot_nt(totals[:count], wide_rows)
+        if iteration == 0:
+            back = back + center[:, None] * sums[0][None]
+            inner = inner + local_walkers * center[:count, None] * center[None]
+            repeated = jnp.concatenate([inner, local_walkers * center[None]])
+            sent = jnp.concatenate([by_owner(back, walker_devices), by_owner(sums, walker_devices)], axis=1)
+            repeated = pad_columns(repeated, owned)
+        else:
+            sent = by_owner(back.astype(jnp.bfloat16), walker_devices)
+            repeated = pad_columns(split_in_three(inner), owned)
         sent = jnp.concatenate(
-            [
-                by_owner(back, walker_devices),
-                jnp.broadcast_to(
-                    pad_columns(inner, owned)[None], (walker_devices, count, owned)
-                ),
-            ],
-            axis=1,
-        )
-        total = jnp.sum(exchange(sent, "walker"), axis=0) / walkers
-        inner = total[2 * count :, : 2 * count]
+            [sent, jnp.broadcast_to(repeated[None], (walker_devices,) + repeated.shape)], axis=1
+        )
+        total = jnp.sum(exchange(sent, "walker").astype(jnp.float32), axis=0) / walkers
+        if iteration == 0:
+            means = jnp.stack([total[2 * count], total[2 * count + 2]])
+            s_diagonal = total[2 * count + 1] - means[0] * means[0] + EPS_SHIFT
+            inner = total[2 * count + 3 :, : 2 * count]
+            common = inner[count]
+            wide_rows = wide_rows + (center - common)[:, None]
+            center = common
+            inner = inner[:count] - center[:count, None] * center[None]
+            total = total[: 2 * count] - center[:, None] * means[:1]
+        else:
+            inner = joined(total[2 * count :], 2 * count)
+        all_centers.append(center)
+        all_rows.append(wide_rows)
         a_matrix = inner[:, :count] + EPS_SHIFT * jnp.eye(count)
         b_matrix = inner[:, count:] + ENERGY_SHIFT * jnp.eye(count)
         s_image = total[:count] + EPS_SHIFT * block
@@ -315,11 +328,10 @@
         )
         basis.append(block)
         all_totals.append(totals)
-        all_centers.append(center)
     lefts = jnp.concatenate([t[:count] for t in all_totals])
     rights = jnp.concatenate(
         [r[:count] for r in all_rows] + [r[count:] for r in all_rows]
-    ).astype(jnp.float32)
+    )
     proj = jnp.sum(to_all(dot_nt(lefts, rights), "walker"), axis=0) / walkers
     size = lefts.shape[0]
     proj_s = proj[:, :size] + EPS_SHIFT * jnp.eye(size)

time: 300 us -> 275 us (0.917)
  blocking collectives: 40.1 us -> 0 us
  starting transfers between devices: 44.8 us -> 55.7 us
  local copies, waits for them, and re-layouts: 7.01 us -> 13.6 us
  matrix products: 25 us -> 20.5 us
    all_to_all x3 -> x0, blocking collectives: 40.1 us -> none  [exchange(): return lax.all_to_all(lax.optimization_barrier(parts), axis, 0, 0)]
    all_to_all x9 -> x11, starting transfers between devices: 44.8 us -> 55.7 us  [exchange(): return lax.all_to_all(lax.optimization_barrier(parts), axis, 0, 0)]
    dot_general x8, matrix products: 9.57 us -> 4.78 us  [forward(): both = jnp.dot(halves, table, preferred_element_type=jnp.float32)]
    unnamed x17 -> x33, local copies, waits for them, and re-layouts: 1.33 us -> 5.55 us
    all_to_all x9 -> x11, waiting for transfers between devices: 86.9 us -> 88.5 us  [exchange(): return lax.all_to_all(lax.optimization_barrier(parts), axis, 0, 0)]
  transfers between devices with their start and end apart: 9 -> 11, of which waited for: 9 -> 11; matrix products, arithmetic and copies ran while one was open for 2% -> 2% of each run, Pallas kernels for 0% -> 0%
where the time goes in v3:
time: 275 us; the launch traced here: 273 us
  waiting for transfers between devices  88.5 us (32%)
  Pallas kernels  61.9 us (23%)
  starting transfers between devices  55.7 us (20%)
  other arithmetic  31.9 us (12%)
  matrix products  20.5 us (7%)
  local copies, waits for them, and re-layouts  13.6 us (5%)
    all_to_all x11, waiting for transfers between devices, exchange(): return lax.all_to_all(lax.optimization_barrier(parts), axis, 0, 0)  88.5 us
    pallas_call x1, Pallas kernels, build(): pl.pallas_call(build_kernel, out_shape=[jax.ShapeDtypeStruct((params, wal...  61.9 us
    all_to_all x11, starting transfers between devices, exchange(): return lax.all_to_all(lax.optimization_barrier(parts), axis, 0, 0)  55.7 us
    dot_general x41, matrix products, dot_nn(): jnp.dot(left, right, precision=HIGHEST, preferred_element_type=jnp.float32)  8.34 us
    another operation x12, other arithmetic, inverse_factor(): lower_factor = jnp.linalg.cholesky(gram)  5.61 us
    unnamed x33, local copies, waits for them, and re-layouts  5.55 us
  transfers between devices with their start and end apart: 11, of which 11 were waited for; matrix products, arithmetic and copies ran while one was open for 2% of the time, Pallas kernels for 0%

profile of v3, /device:TPU:1, one launch (start us, length us, event | category | flops | bytes accessed | tf_op | source)
XLA Modules:
  0.0 273.3 jit_solution(1340926077203509926)
XLA Ops:
  4.7 61.9 %shard_map.94 = (bf16[4096,256]{1,0:T(8,128)(2,1)}, bf16[4096,256]{1,0:T(8,128)(2,1)}) custom-call(s32[16384]{0:T(1024)} %pad_add_fusion.place_ref, s32[16,256]{1,0:T(8,128)} %occupation_ref.1, f32[256,256]{1,0:T(8,128)} %bitcast.281, f32[1024,512]{1,0:T(8,128)} %orbitals_ref.1, f32[1024,512]{1,0:T(8,128)} %hop_ref.1, f32[1,256]{1,0:T(1,128)} %bitcast.290), custom_call_target="tpu_custom_call" | custom-call | tf_op jit(solution)/shard_map/pallas_call | solution.py:171
  69.9 10.0 %all-to-all-start = ((bf16[16,24,256]{2,1,0:T(8,128)(2,1)}), bf16[16,24,256]{2,1,0:T(8,128)(2,1)S(1)}, u32[]{:S(2)}, u32[]{:S(2)}) async-start(bf16[16,24,256]{2,1,0:T(8,128)(2,1)} %broadcast_in_dim.26), calls=%async_computation | async-start | bytes 393216 | tf_op jit(solution)/shard_map/all_to_all | solution.py:27
  79.9 2.2 convert_reduce_fusion.1
  83.4 6.9 %all-to-all-done = bf16[16,24,256]{2,1,0:T(8,128)(2,1)S(1)} async-done(((bf16[16,24,256]{2,1,0:T(8,128)(2,1)}), bf16[16,24,256]{2,1,0:T(8,128)(2,1)S(1)}, u32[]{:S(2)}, u32[]{:S(2)}) %all-to-all-start) | async-done | bytes 196640 | tf_op jit(solution)/shard_map/all_to_all | solution.py:27
  95.8 6.7 %all-to-all-start.1 = ((f32[16,28,256]{2,1,0:T(8,128)}), f32[16,28,256]{2,1,0:T(8,128)S(1)}, u32[]{:S(2)}, u32[]{:S(2)}) async-start(f32[16,28,256]{2,1,0:T(8,128)} %pad_maximum_fusion), calls=%async_computation.1 | async-start | bytes 1048576 | tf_op jit(solution)/shard_map/all_to_all | solution.py:27
  103.0 10.5 %all-to-all-done.1 = f32[16,28,256]{2,1,0:T(8,128)S(1)} async-done(((f32[16,28,256]{2,1,0:T(8,128)}), f32[16,28,256]{2,1,0:T(8,128)S(1)}, u32[]{:S(2)}, u32[]{:S(2)}) %all-to-all-start.1) | async-done | bytes 458784 | tf_op jit(solution)/shard_map/all_to_all | solution.py:27
  119.2 3.6 %all-to-all-start.2 = ((f32[16,8,384]{2,1,0:T(8,128)}), f32[16,8,384]{2,1,0:T(8,128)S(1)}, u32[]{:S(2)}, u32[]{:S(2)}) async-start(f32[16,8,384]{2,1,0:T(8,128)} %broadcast_in_dim.28), calls=%async_computation.2 | async-start | bytes 393216 | tf_op jit(solution)/shard_map/all_to_all | solution.py:27
  122.9 6.9 %all-to-all-done.2 = f32[16,8,384]{2,1,0:T(8,128)S(1)} async-done(((f32[16,8,384]{2,1,0:T(8,128)}), f32[16,8,384]{2,1,0:T(8,128)S(1)}, u32[]{:S(2)}, u32[]{:S(2)}) %all-to-all-start.2) | async-done | bytes 196640 | tf_op jit(solution)/shard_map/all_to_all | solution.py:27
  132.6 5.9 %all-to-all-start.3 = ((bf16[16,24,256]{2,1,0:T(8,128)(2,1)}), bf16[16,24,256]{2,1,0:T(8,128)(2,1)S(1)}, u32[]{:S(2)}, u32[]{:S(2)}) async-start(bf16[16,24,256]{2,1,0:T(8,128)(2,1)} %broadcast_in_dim.29), calls=%async_computation.3 | async-start | bytes 393216 | tf_op jit(solution)/shard_map/all_to_all | solution.py:27
  138.6 10.3 %all-to-all-done.3 = bf16[16,24,256]{2,1,0:T(8,128)(2,1)S(1)} async-done(((bf16[16,24,256]{2,1,0:T(8,128)(2,1)}), bf16[16,24,256]{2,1,0:T(8,128)(2,1)S(1)}, u32[]{:S(2)}, u32[]{:S(2)}) %all-to-all-start.3) | async-done | bytes 196640 | tf_op jit(solution)/shard_map/all_to_all | solution.py:27
  156.1 3.5 %all-to-all-start.4 = ((bf16[16,24,256]{2,1,0:T(8,128)(2,1)}), bf16[16,24,256]{2,1,0:T(8,128)(2,1)S(1)}, u32[]{:S(2)}, u32[]{:S(2)}) async-start(bf16[16,24,256]{2,1,0:T(8,128)(2,1)} %pad_maximum_fusion.1), calls=%async_computation.4 | async-start | bytes 393216 | tf_op jit(solution)/shard_map/all_to_all | solution.py:27
  160.0 7.1 %all-to-all-done.4 = bf16[16,24,256]{2,1,0:T(8,128)(2,1)S(1)} async-done(((bf16[16,24,256]{2,1,0:T(8,128)(2,1)}), bf16[16,24,256]{2,1,0:T(8,128)(2,1)S(1)}, u32[]{:S(2)}, u32[]{:S(2)}) %all-to-all-start.4) | async-done | bytes 196640 | tf_op jit(solution)/shard_map/all_to_all | solution.py:27
  171.9 3.7 %all-to-all-start.5 = ((f32[16,8,384]{2,1,0:T(8,128)}), f32[16,8,384]{2,1,0:T(8,128)S(1)}, u32[]{:S(2)}, u32[]{:S(2)}) async-start(f32[16,8,384]{2,1,0:T(8,128)} %broadcast_in_dim.31), calls=%async_computation.5 | async-start | bytes 393216 | tf_op jit(solution)/shard_map/all_to_all | solution.py:27
  175.7 6.8 %all-to-all-done.5 = f32[16,8,384]{2,1,0:T(8,128)S(1)} async-done(((f32[16,8,384]{2,1,0:T(8,128)}), f32[16,8,384]{2,1,0:T(8,128)S(1)}, u32[]{:S(2)}, u32[]{:S(2)}) %all-to-all-start.5) | async-done | bytes 196640 | tf_op jit(solution)/shard_map/all_to_all | solution.py:27
  185.3 5.7 %all-to-all-start.6 = ((bf16[16,24,256]{2,1,0:T(8,128)(2,1)}), bf16[16,24,256]{2,1,0:T(8,128)(2,1)S(1)}, u32[]{:S(2)}, u32[]{:S(2)}) async-start(bf16[16,24,256]{2,1,0:T(8,128)(2,1)} %broadcast_in_dim.32), calls=%async_computation.6 | async-start | bytes 393216 | tf_op jit(solution)/shard_map/all_to_all | solution.py:27
  191.4 10.1 %all-to-all-done.6 = bf16[16,24,256]{2,1,0:T(8,128)(2,1)S(1)} async-done(((bf16[16,24,256]{2,1,0:T(8,128)(2,1)}), bf16[16,24,256]{2,1,0:T(8,128)(2,1)S(1)}, u32[]{:S(2)}, u32[]{:S(2)}) %all-to-all-start.6) | async-done | bytes 196640 | tf_op jit(solution)/shard_map/all_to_all | solution.py:27
  208.9 3.5 %all-to-all-start.7 = ((bf16[16,24,256]{2,1,0:T(8,128)(2,1)}), bf16[16,24,256]{2,1,0:T(8,128)(2,1)S(1)}, u32[]{:S(2)}, u32[]{:S(2)}) async-start(bf16[16,24,256]{2,1,0:T(8,128)(2,1)} %pad_maximum_fusion.2), calls=%async_computation.7 | async-start | bytes 393216 | tf_op jit(solution)/shard_map/all_to_all | solution.py:27
  212.7 7.1 %all-to-all-done.7 = bf16[16,24,256]{2,1,0:T(8,128)(2,1)S(1)} async-done(((bf16[16,24,256]{2,1,0:T(8,128)(2,1)}), bf16[16,24,256]{2,1,0:T(8,128)(2,1)S(1)}, u32[]{:S(2)}, u32[]{:S(2)}) %all-to-all-start.7) | async-done | bytes 196640 | tf_op jit(solution)/shard_map/all_to_all | solution.py:27
  224.6 3.6 %all-to-all-start.8 = ((f32[16,8,384]{2,1,0:T(8,128)}), f32[16,8,384]{2,1,0:T(8,128)S(1)}, u32[]{:S(2)}, u32[]{:S(2)}) async-start(f32[16,8,384]{2,1,0:T(8,128)} %broadcast_in_dim.34), calls=%async_computation.8 | async-start | bytes 393216 | tf_op jit(solution)/shard_map/all_to_all | solution.py:27
  228.4 6.9 %all-to-all-done.8 = f32[16,8,384]{2,1,0:T(8,128)S(1)} async-done(((f32[16,8,384]{2,1,0:T(8,128)}), f32[16,8,384]{2,1,0:T(8,128)S(1)}, u32[]{:S(2)}, u32[]{:S(2)}) %all-to-all-start.8) | async-done | bytes 196640 | tf_op jit(solution)/shard_map/all_to_all | solution.py:27
  238.1 5.8 %all-to-all-start.9 = ((bf16[16,24,256]{2,1,0:T(8,128)(2,1)}), bf16[16,24,256]{2,1,0:T(8,128)(2,1)S(1)}, u32[]{:S(2)}, u32[]{:S(2)}) async-start(bf16[16,24,256]{2,1,0:T(8,128)(2,1)} %broadcast_in_dim.35), calls=%async_computation.9 | async-start | bytes 393216 | tf_op jit(solution)/shard_map/all_to_all | solution.py:27
  244.1 10.1 %all-to-all-done.9 = bf16[16,24,256]{2,1,0:T(8,128)(2,1)S(1)} async-done(((bf16[16,24,256]{2,1,0:T(8,128)(2,1)}), bf16[16,24,256]{2,1,0:T(8,128)(2,1)S(1)}, u32[]{:S(2)}, u32[]{:S(2)}) %all-to-all-start.9) | async-done | bytes 196640 | tf_op jit(solution)/shard_map/all_to_all | solution.py:27
  260.3 3.5 %all-to-all-start.10 = ((f32[16,1,2048]{2,1,0:T(1,128)}), f32[16,1,2048]{2,1,0:T(1,128)S(1)}, u32[]{:S(2)}, u32[]{:S(2)}) async-start(f32[16,1,2048]{2,1,0:T(1,128)} %reshape.231), calls=%async_computation.10 | async-start | bytes 262144 | tf_op jit(solution)/shard_map/all_to_all | solution.py:27
  265.3 5.7 %all-to-all-done.10 = f32[16,1,2048]{2,1,0:T(1,128)S(1)} async-done(((f32[16,1,2048]{2,1,0:T(1,128)}), f32[16,1,2048]{2,1,0:T(1,128)S(1)}, u32[]{:S(2)}, u32[]{:S(2)}) %all-to-all-start.10) | async-done | bytes 131104 | tf_op jit(solution)/shard_map/all_to_all | solution.py:27
  (269 shorter events, 63.8 us)
Async XLA Ops:
  66.5 2.2 copy-start.1
  68.7 13.4 %copy-start = (bf16[4096,256]{1,0:T(8,128)(2,1)S(1)}, bf16[4096,256]{1,0:T(8,128)(2,1)}, u32[]{:S(2)}) copy-start(bf16[4096,256]{1,0:T(8,128)(2,1)} %get-tuple-element.8) | copy-start | bytes 6291460
  69.9 20.3 %all-to-all-start = ((bf16[16,24,256]{2,1,0:T(8,128)(2,1)}), bf16[16,24,256]{2,1,0:T(8,128)(2,1)S(1)}, u32[]{:S(2)}, u32[]{:S(2)}) async-start(bf16[16,24,256]{2,1,0:T(8,128)(2,1)} %broadcast_in_dim.26), calls=%async_computation | async-start | bytes 393216 | tf_op jit(solution)/shard_map/all_to_all | solution.py:27
  94.6 7.9 %copy-start.5 = (f32[4096,8]{0,1:T(8,128)S(1)}, f32[4096,8]{0,1:T(8,128)}, u32[]{:S(2)}) copy-start(f32[4096,8]{0,1:T(8,128)} %param.18) | copy-start | bytes 393220
  95.8 17.8 %all-to-all-start.1 = ((f32[16,28,256]{2,1,0:T(8,128)}), f32[16,28,256]{2,1,0:T(8,128)S(1)}, u32[]{:S(2)}, u32[]{:S(2)}) async-start(f32[16,28,256]{2,1,0:T(8,128)} %pad_maximum_fusion), calls=%async_computation.1 | async-start | bytes 1048576 | tf_op jit(solution)/shard_map/all_to_all | solution.py:27
  119.2 10.6 %all-to-all-start.2 = ((f32[16,8,384]{2,1,0:T(8,128)}), f32[16,8,384]{2,1,0:T(8,128)S(1)}, u32[]{:S(2)}, u32[]{:S(2)}) async-start(f32[16,8,384]{2,1,0:T(8,128)} %broadcast_in_dim.28), calls=%async_computation.2 | async-start | bytes 393216 | tf_op jit(solution)/shard_map/all_to_all | solution.py:27
  129.8 1.6 copy-start.2
  132.6 16.3 %all-to-all-start.3 = ((bf16[16,24,256]{2,1,0:T(8,128)(2,1)}), bf16[16,24,256]{2,1,0:T(8,128)(2,1)S(1)}, u32[]{:S(2)}, u32[]{:S(2)}) async-start(bf16[16,24,256]{2,1,0:T(8,128)(2,1)} %broadcast_in_dim.29), calls=%async_computation.3 | async-start | bytes 393216 | tf_op jit(solution)/shard_map/all_to_all | solution.py:27
  156.1 11.0 %all-to-all-start.4 = ((bf16[16,24,256]{2,1,0:T(8,128)(2,1)}), bf16[16,24,256]{2,1,0:T(8,128)(2,1)S(1)}, u32[]{:S(2)}, u32[]{:S(2)}) async-start(bf16[16,24,256]{2,1,0:T(8,128)(2,1)} %pad_maximum_fusion.1), calls=%async_computation.4 | async-start | bytes 393216 | tf_op jit(solution)/shard_map/all_to_all | solution.py:27
  171.9 10.6 %all-to-all-start.5 = ((f32[16,8,384]{2,1,0:T(8,128)}), f32[16,8,384]{2,1,0:T(8,128)S(1)}, u32[]{:S(2)}, u32[]{:S(2)}) async-start(f32[16,8,384]{2,1,0:T(8,128)} %broadcast_in_dim.31), calls=%async_computation.5 | async-start | bytes 393216 | tf_op jit(solution)/shard_map/all_to_all | solution.py:27
  182.5 1.6 copy-start.3
  185.3 16.1 %all-to-all-start.6 = ((bf16[16,24,256]{2,1,0:T(8,128)(2,1)}), bf16[16,24,256]{2,1,0:T(8,128)(2,1)S(1)}, u32[]{:S(2)}, u32[]{:S(2)}) async-start(bf16[16,24,256]{2,1,0:T(8,128)(2,1)} %broadcast_in_dim.32), calls=%async_computation.6 | async-start | bytes 393216 | tf_op jit(solution)/shard_map/all_to_all | solution.py:27
  208.9 11.0 %all-to-all-start.7 = ((bf16[16,24,256]{2,1,0:T(8,128)(2,1)}), bf16[16,24,256]{2,1,0:T(8,128)(2,1)S(1)}, u32[]{:S(2)}, u32[]{:S(2)}) async-start(bf16[16,24,256]{2,1,0:T(8,128)(2,1)} %pad_maximum_fusion.2), calls=%async_computation.7 | async-start | bytes 393216 | tf_op jit(solution)/shard_map/all_to_all | solution.py:27
  224.6 10.6 %all-to-all-start.8 = ((f32[16,8,384]{2,1,0:T(8,128)}), f32[16,8,384]{2,1,0:T(8,128)S(1)}, u32[]{:S(2)}, u32[]{:S(2)}) async-start(f32[16,8,384]{2,1,0:T(8,128)} %broadcast_in_dim.34), calls=%async_computation.8 | async-start | bytes 393216 | tf_op jit(solution)/shard_map/all_to_all | solution.py:27
  235.3 1.6 copy-start.4
  238.1 16.1 %all-to-all-start.9 = ((bf16[16,24,256]{2,1,0:T(8,128)(2,1)}), bf16[16,24,256]{2,1,0:T(8,128)(2,1)S(1)}, u32[]{:S(2)}, u32[]{:S(2)}) async-start(bf16[16,24,256]{2,1,0:T(8,128)(2,1)} %broadcast_in_dim.35), calls=%async_computation.9 | async-start | bytes 393216 | tf_op jit(solution)/shard_map/all_to_all | solution.py:27
  260.3 10.6 %all-to-all-start.10 = ((f32[16,1,2048]{2,1,0:T(1,128)}), f32[16,1,2048]{2,1,0:T(1,128)S(1)}, u32[]{:S(2)}, u32[]{:S(2)}) async-start(f32[16,1,2048]{2,1,0:T(1,128)} %reshape.231), calls=%async_computation.10 | async-start | bytes 262144 | tf_op jit(solution)/shard_map/all_to_all | solution.py:27

commit v4 on v2

v4 whole, which is shorter than its diff:
```python
import functools
import math

import jax
import jax.numpy as jnp
from jax import lax
from jax.experimental import pallas as pl
from jax.experimental.pallas import tpu as pltpu
from jax.sharding import PartitionSpec as P

ITERS = 3
EPS_SHIFT = 0.001
ENERGY_SHIFT = 0.5
HIGHEST = lax.Precision.HIGHEST
LANES = 128
ROWS = 8
GROUP = 64


def build_kernel(
    place_ref, occupation_ref, inverse_ref, orbitals_ref, hop_ref, energy_ref,
    derivs_ref, energy_derivs_ref,
    high_ref, low_ref, sites_ref, rows_ref, wide_ref, table_ref, first_ref, second_ref,
):
    electrons, walkers = occupation_ref.shape
    sites, orbitals = orbitals_ref.shape
    params = derivs_ref.shape[0]
    halves = walkers // LANES
    tiles = orbitals // ROWS

    for half in range(halves):
        for row in range(electrons * electrons):
            wide_ref[half, row] = jnp.broadcast_to(
                inverse_ref[row : row + 1, half * LANES : (half + 1) * LANES], (ROWS, LANES)
            )
    for number, source in enumerate((orbitals_ref, hop_ref)):
        for column in range(0, orbitals, LANES):
            turned = source[:, column : column + LANES].T
            high = turned.astype(jnp.bfloat16)
            where = pl.ds(number * orbitals + column, LANES)
            high_ref[where, :] = high
            low_ref[where, :] = (turned - high.astype(jnp.float32)).astype(jnp.bfloat16)

    def pick(electron, carry):
        occupied = occupation_ref[pl.ds(electron, 1), :]
        index = lax.broadcasted_iota(jnp.int32, (sites, walkers), 0)
        sites_ref[...] = jnp.where(index == occupied, 1.0, 0.0).astype(jnp.bfloat16)
        for row in range(0, 2 * orbitals, 256):
            where = pl.ds(row, 256)
            rows_ref[electron, where, :] = jnp.dot(
                high_ref[where, :], sites_ref[...], preferred_element_type=jnp.float32
            ) + jnp.dot(low_ref[where, :], sites_ref[...], preferred_element_type=jnp.float32)
        return carry

    lax.fori_loop(0, electrons, pick, 0)

    def contract(tile, carry):
        for half in range(halves):
            lanes = slice(half * LANES, (half + 1) * LANES)
            plain = [rows_ref[k, pl.ds(pl.multiple_of(tile * ROWS, ROWS), ROWS), lanes] for k in range(electrons)]
            hopped = [
                rows_ref[k, pl.ds(pl.multiple_of(orbitals + tile * ROWS, ROWS), ROWS), lanes]
                for k in range(electrons)
            ]
            scale = energy_ref[0:1, lanes] * 0.5
            for i in range(electrons):
                weight = wide_ref[half, i * electrons]
                ratio = weight * plain[0]
                energy = weight * hopped[0]
                for k in range(1, electrons):
                    weight = wide_ref[half, i * electrons + k]
                    ratio += weight * plain[k]
                    energy += weight * hopped[k]
                base = pl.multiple_of((i * tiles + tile) * 4 * ROWS, ROWS)
                table_ref[pl.ds(base + half, ROWS, stride=4), :] = ratio
                table_ref[pl.ds(base + 2 + half, ROWS, stride=4), :] = energy + scale * ratio
        return carry

    lax.fori_loop(0, tiles, contract, 0)

    def pairs(group, carry):
        for j in range(GROUP):

            def take(which, part):
                return table_ref[pl.ds(pl.multiple_of(place_ref[which * params + group * GROUP + j], 4) + part * 2, 2), :]

            ia, jb, ib, ja = (take(which, 0) for which in range(4))
            e_ia, e_jb, e_ib, e_ja = (take(which, 1) for which in range(4))
            spot = pl.ds(2 * j, 2)
            first_ref[spot, :] = ia * jb - ib * ja
            second_ref[spot, :] = (e_ia * jb + ia * e_jb) - (e_ib * ja + ib * e_ja)
        for source, target in ((first_ref, derivs_ref), (second_ref, energy_derivs_ref)):
            for row in range(0, GROUP, 2 * ROWS):
                for half in range(2):
                    target[
                        pl.ds(pl.multiple_of(group * GROUP + row, 2 * ROWS), 2 * ROWS),
                        half * LANES : (half + 1) * LANES,
                    ] = source[pl.ds(row * 2 + half, 2 * ROWS, stride=2), :].astype(jnp.bfloat16)
        return carry

    lax.fori_loop(0, params // GROUP, pairs, 0)


def build(occupation, inverse_slater, orbitals, hop_orbitals, local_energy, excitations):
    electrons, walkers = occupation.shape
    sites, orbital_count = orbitals.shape
    params = excitations.shape[1]

    def place(electron, orbital):
        row = electron * orbital_count + orbital
        return row * 4

    i, j, a, b = excitations
    places = jnp.concatenate([place(i, a), place(j, b), place(i, b), place(j, a)])
    vmem = pl.BlockSpec(memory_space=pltpu.VMEM)
    derivs, energy_derivs = pl.pallas_call(
        build_kernel,
        out_shape=[jax.ShapeDtypeStruct((params, walkers), jnp.bfloat16)] * 2,
        in_specs=[pl.BlockSpec(memory_space=pltpu.SMEM)] + [vmem] * 5,
        out_specs=[vmem] * 2,
        scratch_shapes=[
            pltpu.VMEM((2 * orbital_count, sites), jnp.bfloat16),
            pltpu.VMEM((2 * orbital_count, sites), jnp.bfloat16),
            pltpu.VMEM((sites, walkers), jnp.bfloat16),
            pltpu.VMEM((electrons, 2 * orbital_count, walkers), jnp.float32),
            pltpu.VMEM((walkers // LANES, electrons * electrons, ROWS, LANES), jnp.float32),
            pltpu.VMEM((electrons * orbital_count * 4, LANES), jnp.float32),
            pltpu.VMEM((GROUP * 2, LANES), jnp.float32),
            pltpu.VMEM((GROUP * 2, LANES), jnp.float32),
        ],
        compiler_params=pltpu.CompilerParams(vmem_limit_bytes=60 * 1024 * 1024),
    )(
        places,
        occupation,
        inverse_slater.reshape(electrons * electrons, walkers),
        orbitals,
        hop_orbitals,
        local_energy[None],
    )
    wide = derivs.astype(jnp.float32)
    sums = jnp.stack(
        [
            jnp.sum(wide, axis=1),
            jnp.sum(wide * wide, axis=1),
            jnp.sum(energy_derivs.astype(jnp.float32), axis=1),
        ]
    )
    return derivs, energy_derivs, sums


def dot_nt(left, right):
    return lax.dot_general(
        left, right, (((1,), (1,)), ((), ())), precision=HIGHEST, preferred_element_type=jnp.float32
    )


def dot_nn(left, right):
    return jnp.dot(left, right, precision=HIGHEST, preferred_element_type=jnp.float32)


def exchange(parts, axis):
    return lax.all_to_all(parts, axis, 0, 0)


def in_thirds(values):
    high = values.astype(jnp.bfloat16).astype(jnp.float32)
    rest = values - high
    middle = rest.astype(jnp.bfloat16).astype(jnp.float32)
    return high, middle, rest - middle


def lanes_of(shape):
    return lax.broadcasted_iota(jnp.int32, shape, 1)


def eliminate(matrix, right, full):
    count = matrix.shape[0]
    row = lax.broadcasted_iota(jnp.int32, (count, 1), 0)
    for j in range(count):
        pivot = matrix[j : j + 1, j : j + 1]
        scale = matrix[:, j : j + 1] / pivot
        keep = (row != j) if full else (row > j)
        scale = jnp.where(keep, scale, 0.0)
        right = right - scale * right[j : j + 1, :]
        matrix = matrix - scale * matrix[j : j + 1, :]
    diagonal = lanes_of(matrix.shape) == lax.broadcasted_iota(jnp.int32, matrix.shape, 0)
    return right, jnp.sum(jnp.where(diagonal, matrix, 0.0), axis=1, keepdims=True)


def advance_kernel(step, share, *refs):
    if step:
        got_ref, own_ref, state_ref, cents_ref, derivs_ref = refs[:5]
        outs = refs[5:]
    else:
        got_ref, own_ref, sums_ref, derivs_ref = refs[:4]
        outs = refs[4:]
    block_ref, tail_ref, grams_ref, rows_ref, sent_ref = outs
    sources, _, width = got_ref.shape
    walkers = width - LANES
    owned = own_ref.shape[1]
    count = own_ref.shape[0]
    total = got_ref[0].astype(jnp.float32)
    for source in range(1, sources):
        total += got_ref[source].astype(jnp.float32)
    part = total[:, walkers:]
    grams = part[:count] + part[count:] + pltpu.roll(part[:count], LANES // 2, 1)
    lane = lanes_of((count, LANES))
    row = lax.broadcasted_iota(jnp.int32, (count, LANES), 0)
    identity = jnp.where(lane == row + LANES // 2, 1.0, 0.0)
    grams = jnp.where(lane < LANES // 2, grams, 0.0)
    grams_ref[...] = grams
    earlier = count * step
    if step:
        tail = jnp.where(lane < 2, pltpu.roll(grams, LANES - (earlier + count), 1), 0.0) + identity
    else:
        tail = identity
    right = jnp.concatenate([own_ref[...], total[:count, :walkers], total[count:, :walkers], tail], axis=1)
    gram = grams
    if step:
        overlap = grams[:, :earlier]
        right = right - dot_nn(overlap, jnp.concatenate([state_ref[...], cents_ref[...]], axis=1))
        gram = pltpu.roll(grams, LANES - earlier, 1)
        padded = jnp.concatenate([overlap, jnp.zeros((LANES - count, earlier), jnp.float32)])
        gram = gram - dot_nt(overlap, padded)
    right, pivots = eliminate(gram, right, False)
    right = right * lax.rsqrt(pivots)
    plain = right[:, owned : owned + walkers]
    energy = right[:, owned + walkers : owned + 2 * walkers]
    block_ref[...] = right[:, : owned + 2 * walkers]
    tail = right[:, owned + 2 * walkers :]
    if step:
        centers = [tail[:, 0:1], tail[:, 1:2]]
    else:
        centers = [jnp.mean(plain, axis=1, keepdims=True), jnp.mean(energy, axis=1, keepdims=True)]
        tail = jnp.where(lane == 0, centers[0], jnp.where(lane == 1, centers[1], tail))
    tail_ref[...] = tail
    center = jnp.concatenate(centers)
    rows = (jnp.concatenate([plain, energy]) - center).astype(jnp.bfloat16)
    wide = rows.astype(jnp.float32)
    rows_ref[...] = wide
    filled = jnp.concatenate([plain, jnp.zeros((LANES - count, walkers), jnp.float32)])
    if step:
        high, middle, low = in_thirds(dot_nt(wide, filled))
        inner = (high + pltpu.roll(middle, 32, 1) + pltpu.roll(low, 64, 1)).astype(jnp.bfloat16)
    else:
        inner = dot_nt(wide + center, filled)
        inner = inner + jnp.where(lanes_of(inner.shape) == count, walkers * center, 0.0)
        across = dot_nt(jnp.ones((count, walkers), jnp.float32), filled)
    for owner in range(sent_ref.shape[0]):
        where = slice(owner * share, (owner + 1) * share)
        back = lax.dot_general(
            rows, derivs_ref[where, :], (((1,), (1,)), ((), ())), preferred_element_type=jnp.float32
        )
        if step:
            sent_ref[owner, :, :share] = back.astype(jnp.bfloat16)
            sent_ref[owner, :, share:] = inner
        else:
            sent_ref[owner, : 2 * count, :share] = back + center * sums_ref[0:1, where]
            sent_ref[owner, : 2 * count, share:] = inner
            sent_ref[owner, 2 * count :, :share] = sums_ref[:, where]
            sent_ref[owner, 2 * count :, share:] = across


def correct_kernel(step, walkers, *refs):
    if step:
        got_ref, state_ref, stats_ref, own_ref, sent_ref, stack_ref = refs
    else:
        got_ref, state_ref, own_ref, sent_ref, stats_ref, cents_ref, stack_ref = refs
    sources, _, width = got_ref.shape
    owned = width - LANES
    count = own_ref.shape[0]
    earlier = count * (step + 1)
    total = got_ref[0].astype(jnp.float32)
    for source in range(1, sources):
        total += got_ref[source].astype(jnp.float32)
    total = total * (1.0 / walkers)
    images = total[: 2 * count, :owned]
    inner = total[: 2 * count, owned:]
    if step:
        inner = inner + pltpu.roll(inner, LANES - 32, 1) + pltpu.roll(inner, LANES - 64, 1)
        stats = stats_ref[...]
    else:
        mean_o = total[2 * count : 2 * count + 1, :owned]
        mean_h = total[2 * count + 2 : 2 * count + 3, :owned]
        square = total[2 * count + 1 : 2 * count + 2, :owned]
        kind = lax.broadcasted_iota(jnp.int32, (count, owned), 0)
        diagonal = square - mean_o * mean_o + EPS_SHIFT
        stats = jnp.where(
            kind == 0, mean_o, jnp.where(kind == 1, mean_h, jnp.where(kind == 2, diagonal, 0.0))
        )
        stats_ref[...] = stats
        center = inner[:, count : count + 1]
        inner = inner - center * total[2 * count : 2 * count + 1, owned:]
        images = images - center * mean_o
        lane = lanes_of((count, LANES))
        cents_ref[...] = jnp.where(
            lane == 0, center[:count], jnp.where(lane == 1, center[count:], 0.0)
        )
    block = state_ref[earlier - count :, :owned]
    lane = lanes_of((count, LANES))
    unit = jnp.where(lane == lax.broadcasted_iota(jnp.int32, lane.shape, 0), 1.0, 0.0)
    a_matrix = jnp.where(lane < count, inner[:count], 0.0) + EPS_SHIFT * unit
    turned_b = inner[count:] + ENERGY_SHIFT * unit
    s_image = images[:count] + EPS_SHIFT * block
    h_image = images[count:] + ENERGY_SHIFT * block
    solved, pivots = eliminate(a_matrix, s_image, True)
    solved = solved / pivots
    correction = h_image - dot_nn(turned_b[:, :count], solved)
    correction = correction / stats[2:3, :]
    own_ref[...] = correction
    stack_ref[...] = jnp.zeros_like(stack_ref)
    stack_ref[:earlier, :] = state_ref[:, :owned]
    stack_ref[earlier : earlier + count, :] = correction
    stack_ref[earlier + count : earlier + 2 * count, :] = stats
    grams = dot_nt(correction, stack_ref[...])
    for target in range(sent_ref.shape[0]):
        sent_ref[target, :, :owned] = correction
        sent_ref[target, :, owned:] = grams


def project_kernel(got_ref, derivs_ref, energy_ref, sent_ref):
    sources, count, width = got_ref.shape
    owned = width - LANES
    grams = jnp.zeros((count, LANES), jnp.float32)
    plain = energy = None
    for source in range(sources):
        values = got_ref[source]
        grams += values[:, owned:]
        values = values[:, :owned]
        high = values.astype(jnp.bfloat16).astype(jnp.float32)
        both = jnp.concatenate([high, values - high]).astype(jnp.bfloat16)
        where = slice(source * owned, (source + 1) * owned)
        more = [
            jnp.dot(both, table[where, :], preferred_element_type=jnp.float32)
            for table in (derivs_ref, energy_ref)
        ]
        plain, energy = more if plain is None else (plain + more[0], energy + more[1])
    images = jnp.concatenate([plain[:count] + plain[count:], energy[:count] + energy[count:]])
    high, middle, low = in_thirds(jnp.where(lanes_of(grams.shape) < LANES // 2, grams, 0.0))
    side = jnp.concatenate([high + pltpu.roll(low, LANES // 2, 1), middle])
    walkers = images.shape[1]
    for target in range(sent_ref.shape[0]):
        sent_ref[target, :, :walkers] = images.astype(jnp.bfloat16)
        sent_ref[target, :, walkers:] = side.astype(jnp.bfloat16)


def stage(body, outs, args, scratch=()):
    vmem = pl.BlockSpec(memory_space=pltpu.VMEM)
    return pl.pallas_call(
        body,
        out_shape=[jax.ShapeDtypeStruct(shape, dtype) for shape, dtype in outs],
        in_specs=[vmem] * len(args),
        out_specs=[vmem] * len(outs),
        scratch_shapes=list(scratch),
        compiler_params=pltpu.CompilerParams(vmem_limit_bytes=20 * 1024 * 1024),
    )(*args)


def on_device(
    occupation, inverse_slater, orbitals, hop_orbitals, local_energy, excitations, initial_block
):
    walker_devices = lax.axis_size("walker")
    param_devices = lax.axis_size("param")
    local_walkers = local_energy.shape[0]
    walkers = local_walkers * walker_devices
    block_rows = excitations.shape[1]
    count = initial_block.shape[1]
    params = block_rows * param_devices
    owned = block_rows // walker_devices
    f32, bf16 = jnp.float32, jnp.bfloat16
    derivs, energy_derivs, sums = build(
        occupation, inverse_slater, orbitals, hop_orbitals, local_energy, excitations
    )
    sums = jnp.pad(sums, ((0, count - sums.shape[0]), (0, 0)))
    start = initial_block.T
    offset = lax.axis_index("walker") * owned
    own = lax.dynamic_slice_in_dim(start, offset, owned, 1)
    gram = jnp.pad(dot_nt(start, start) / walker_devices, ((0, 0), (0, LANES - count)))
    pieces = jnp.concatenate(
        [start.reshape(count, walker_devices, owned).transpose(1, 0, 2),
         jnp.broadcast_to(gram[None], (walker_devices, count, LANES))],
        axis=2,
    )
    state = cents = stats = None
    wholes, plains, rows = [], [], []
    for step in range(ITERS + 1):
        if step:
            pieces = exchange(sent, "walker")
        (sent,) = stage(
            project_kernel,
            [((param_devices, 2 * count, local_walkers + LANES), bf16)],
            (pieces, derivs, energy_derivs),
        )
        got = exchange(sent, "param")
        outs = [
            ((count, owned + 2 * local_walkers), f32),
            ((count, LANES), f32),
            ((count, LANES), f32),
            ((2 * count, local_walkers), f32),
            ((walker_devices, 2 * count, owned + LANES), bf16)
            if step
            else ((walker_devices, 3 * count, owned + LANES), f32),
        ]
        block, tail, grams, wide, sent = stage(
            functools.partial(advance_kernel, step, owned),
            outs,
            (got, own, state, cents, derivs) if step else (got, own, sums, derivs),
        )
        whole = pieces[:, :, :owned].transpose(1, 0, 2).reshape(count, block_rows)
        if step:
            whole = whole - dot_nn(grams[:, : count * step], jnp.concatenate(wholes))
        wholes.append(dot_nn(tail[:, LANES // 2 : LANES // 2 + count], whole))
        plains.append(block[:, owned : owned + local_walkers])
        rows.append(wide)
        state = block if step == 0 else jnp.concatenate([state, block])
        if step == ITERS:
            break
        got = exchange(sent, "walker")
        outs = [
            ((count, owned), f32),
            ((walker_devices, count, owned + LANES), f32),
        ]
        scratch = [pltpu.VMEM((LANES, owned), f32)]
        if step:
            own, sent = stage(
                functools.partial(correct_kernel, step, walkers), outs, (got, state, stats), scratch
            )
            cents = jnp.concatenate(
                [cents, jnp.where(jnp.arange(LANES) < 2, tail, 0.0)]
            )
        else:
            outs += [((count, owned), f32), ((count, LANES), f32)]
            own, sent, stats, cents = stage(
                functools.partial(correct_kernel, step, walkers), outs, (got, state), scratch
            )
            shift = tail[:, :2] - cents[:, :2]
            rows[0] = wide + shift.T.reshape(2 * count, 1)
    lefts = jnp.concatenate(plains)
    rights = jnp.concatenate([r[:count] for r in rows] + [r[count:] for r in rows])
    proj = dot_nt(lefts, rights)
    proj = exchange(jnp.broadcast_to(proj[None], (walker_devices,) + proj.shape), "walker")
    proj = jnp.sum(proj, axis=0) / walkers
    size = lefts.shape[0]
    proj_s = proj[:, :size] + EPS_SHIFT * jnp.eye(size)
    proj_h = proj[:, size:] + ENERGY_SHIFT * jnp.eye(size)
    return (math.sqrt(params) * jnp.concatenate(wholes).T, proj_h, proj_s)


def solution(mesh):
    placed = (
        P(None, "walker"),
        P(None, None, "walker"),
        P(),
        P(),
        P("walker"),
        P(None, "param"),
        P("param", None),
    )
    return jax.shard_map(
        on_device,
        mesh=mesh,
        in_specs=placed,
        out_specs=(P("param", None), P(), P()),
        check_vma=False,
    )
```

time: 300 us -> 252 us (0.84)
  blocking collectives: 40.1 us -> 0 us
  other arithmetic: 31.8 us -> 8.61 us
  matrix products: 25 us -> 3.65 us
  Pallas kernels: 61.9 us -> 82.3 us
  starting transfers between devices: 44.8 us -> 55.7 us
    all_to_all x3 -> x0, blocking collectives: 40.1 us -> none  [exchange(): return lax.all_to_all(lax.optimization_barrier(parts), axis, 0, 0)]
    pallas_call x0 -> x11, Pallas kernels: none -> 20.3 us  [stage(): pl.pallas_call(body, out_shape=[jax.ShapeDtypeStruct(shape, dtype) for sh...]
    another operation x39 -> x1, other arithmetic: 19.7 us -> 0.06 us  [build(): jnp.stack([jnp.sum(wide, axis=1), jnp.sum(wide * wide, axis=1), jnp.sum(e...]
    dot_general x14 -> x0, matrix products: 11.9 us -> none  [the longest x8 9.57 us: forward(): both = jnp.dot(halves, table, preferred_element_type=jnp.float32)]
    all_to_all x9 -> x11, starting transfers between devices: 44.8 us -> 55.7 us  [exchange(): return lax.all_to_all(parts, axis, 0, 0)]
    unnamed x17 -> x31, local copies, waits for them, and re-layouts: 1.33 us -> 8.94 us
    dot_general x41 -> x7, matrix products: 8.46 us -> 2.12 us  [dot_nn(): jnp.dot(left, right, precision=HIGHEST, preferred_element_type=jnp.float32)]
    broadcast_in_dim x12 -> x2, local copies, waits for them, and re-layouts: 3.27 us -> 0.03 us  [the longest x1 0.02 us: on_device(): jnp.broadcast_to(proj[None], (walker_devices,) + proj.shape)]
  transfers between devices with their start and end apart: 9 -> 11, of which waited for: 9 -> 11; matrix products, arithmetic and copies ran while one was open for 2% -> 3% of each run, Pallas kernels for 0% -> 0%
where the time goes in v4:
time: 252 us; the launch traced here: 250 us
  waiting for transfers between devices  89.2 us (35%)
  Pallas kernels  82.3 us (33%)
  starting transfers between devices  55.7 us (22%)
  local copies, waits for them, and re-layouts  9.72 us (4%)
  other arithmetic  8.61 us (3%)
  matrix products  3.65 us (1%)
    all_to_all x11, waiting for transfers between devices, exchange(): return lax.all_to_all(parts, axis, 0, 0)  89.2 us
    pallas_call x1, Pallas kernels, build(): pl.pallas_call(build_kernel, out_shape=[jax.ShapeDtypeStruct((params, wal...  61.9 us
    all_to_all x11, starting transfers between devices, exchange(): return lax.all_to_all(parts, axis, 0, 0)  55.7 us
    pallas_call x11, Pallas kernels, stage(): pl.pallas_call(body, out_shape=[jax.ShapeDtypeStruct(shape, dtype) for sh...  20.3 us
    unnamed x31, local copies, waits for them, and re-layouts  8.94 us
  transfers between devices with their start and end apart: 11, of which 11 were waited for; matrix products, arithmetic and copies ran while one was open for 3% of the time, Pallas kernels for 0%

profile of v4, /device:TPU:1, one launch (start us, length us, event | category | flops | bytes accessed | tf_op | source)
XLA Modules:
  0.0 250.2 jit_solution(14639190042981670525)
XLA Ops:
  4.7 61.9 %shard_map.94 = (bf16[4096,256]{1,0:T(8,128)(2,1)}, bf16[4096,256]{1,0:T(8,128)(2,1)}) custom-call(s32[16384]{0:T(1024)} %pad_add_fusion.place_ref, s32[16,256]{1,0:T(8,128)} %occupation_ref.1, f32[256,256]{1,0:T(8,128)} %bitcast.41, f32[1024,512]{1,0:T(8,128)} %orbitals_ref.1, f32[1024,512]{1,0:T(8,128)} %hop_ref.1, f32[1,256]{1,0:T(1,128)} %bitcast.49), custom_call_target="tpu_custom_call" | custom-call | tf_op jit(solution)/shard_map/pallas_call | solution.py:116
  71.1 10.0 %all-to-all-start = ((bf16[16,16,384]{2,1,0:T(8,128)(2,1)}), bf16[16,16,384]{2,1,0:T(8,128)(2,1)S(1)}, u32[]{:S(2)}, u32[]{:S(2)}) async-start(bf16[16,16,384]{2,1,0:T(8,128)(2,1)} %shard_map.95), calls=%async_computation | async-start | bytes 393216 | tf_op jit(solution)/shard_map/all_to_all | solution.py:162
  81.1 3.3 %convert_reduce_fusion = (f32[4096]{0:T(1024)S(1)}, f32[4096]{0:T(1024)S(1)}, f32[4096]{0:T(1024)S(1)}) fusion(bf16[4096,256]{1,0:T(8,128)(2,1)S(1)} %copy-done.1, bf16[4096,256]{1,0:T(8,128)(2,1)} %get-tuple-element.32.energy_ref), kind=kLoop, calls=%fused_computation.1 | loop fusion | flops 6279168 | bytes 4243456 | tf_op jit(solution)/shard_map/reduce_sum | solution.py:143
  84.6 6.9 %all-to-all-done.refs_0_ = bf16[16,16,384]{2,1,0:T(8,128)(2,1)S(1)} async-done(((bf16[16,16,384]{2,1,0:T(8,128)(2,1)}), bf16[16,16,384]{2,1,0:T(8,128)(2,1)S(1)}, u32[]{:S(2)}, u32[]{:S(2)}) %all-to-all-start) | async-done | bytes 196640 | tf_op jit(solution)/shard_map/all_to_all | solution.py:162
  93.8 6.8 %all-to-all-start.1 = ((f32[16,24,384]{2,1,0:T(8,128)}), f32[16,24,384]{2,1,0:T(8,128)S(1)}, u32[]{:S(2)}, u32[]{:S(2)}) async-start(f32[16,24,384]{2,1,0:T(8,128)} %get-tuple-element.34), calls=%async_computation.1 | async-start | bytes 1179648 | tf_op jit(solution)/shard_map/all_to_all | solution.py:162
  101.0 11.5 %all-to-all-done.1.refs_0_ = f32[16,24,384]{2,1,0:T(8,128)S(1)} async-done(((f32[16,24,384]{2,1,0:T(8,128)}), f32[16,24,384]{2,1,0:T(8,128)S(1)}, u32[]{:S(2)}, u32[]{:S(2)}) %all-to-all-start.1) | async-done | bytes 589856 | tf_op jit(solution)/shard_map/all_to_all | solution.py:162
  114.2 3.6 %all-to-all-start.2 = ((f32[16,8,384]{2,1,0:T(8,128)}), f32[16,8,384]{2,1,0:T(8,128)S(1)}, u32[]{:S(2)}, u32[]{:S(2)}) async-start(f32[16,8,384]{2,1,0:T(8,128)} %get-tuple-element.36), calls=%async_computation.2 | async-start | bytes 393216 | tf_op jit(solution)/shard_map/all_to_all | solution.py:162
  118.0 6.7 %all-to-all-done.2.got_ref = f32[16,8,384]{2,1,0:T(8,128)S(1)} async-done(((f32[16,8,384]{2,1,0:T(8,128)}), f32[16,8,384]{2,1,0:T(8,128)S(1)}, u32[]{:S(2)}, u32[]{:S(2)}) %all-to-all-start.2) | async-done | bytes 196640 | tf_op jit(solution)/shard_map/all_to_all | solution.py:162
  127.7 5.9 %all-to-all-start.3 = ((bf16[16,16,384]{2,1,0:T(8,128)(2,1)}), bf16[16,16,384]{2,1,0:T(8,128)(2,1)S(1)}, u32[]{:S(2)}, u32[]{:S(2)}) async-start(bf16[16,16,384]{2,1,0:T(8,128)(2,1)} %shard_map.98), calls=%async_computation.3 | async-start | bytes 393216 | tf_op jit(solution)/shard_map/all_to_all | solution.py:162
  133.7 10.3 %all-to-all-done.3.refs_0_ = bf16[16,16,384]{2,1,0:T(8,128)(2,1)S(1)} async-done(((bf16[16,16,384]{2,1,0:T(8,128)(2,1)}), bf16[16,16,384]{2,1,0:T(8,128)(2,1)S(1)}, u32[]{:S(2)}, u32[]{:S(2)}) %all-to-all-start.3) | async-done | bytes 196640 | tf_op jit(solution)/shard_map/all_to_all | solution.py:162
  146.4 3.5 %all-to-all-start.4 = ((bf16[16,16,384]{2,1,0:T(8,128)(2,1)}), bf16[16,16,384]{2,1,0:T(8,128)(2,1)S(1)}, u32[]{:S(2)}, u32[]{:S(2)}) async-start(bf16[16,16,384]{2,1,0:T(8,128)(2,1)} %get-tuple-element.41), calls=%async_computation.4 | async-start | bytes 393216 | tf_op jit(solution)/shard_map/all_to_all | solution.py:162
  150.2 7.2 %all-to-all-done.4.refs_0_ = bf16[16,16,384]{2,1,0:T(8,128)(2,1)S(1)} async-done(((bf16[16,16,384]{2,1,0:T(8,128)(2,1)}), bf16[16,16,384]{2,1,0:T(8,128)(2,1)S(1)}, u32[]{:S(2)}, u32[]{:S(2)}) %all-to-all-start.4) | async-done | bytes 196640 | tf_op jit(solution)/shard_map/all_to_all | solution.py:162
  159.2 3.6 %all-to-all-start.5 = ((f32[16,8,384]{2,1,0:T(8,128)}), f32[16,8,384]{2,1,0:T(8,128)S(1)}, u32[]{:S(2)}, u32[]{:S(2)}) async-start(f32[16,8,384]{2,1,0:T(8,128)} %get-tuple-element.44), calls=%async_computation.5 | async-start | bytes 393216 | tf_op jit(solution)/shard_map/all_to_all | solution.py:162
  162.8 7.0 %all-to-all-done.5.got_ref = f32[16,8,384]{2,1,0:T(8,128)S(1)} async-done(((f32[16,8,384]{2,1,0:T(8,128)}), f32[16,8,384]{2,1,0:T(8,128)S(1)}, u32[]{:S(2)}, u32[]{:S(2)}) %all-to-all-start.5) | async-done | bytes 196640 | tf_op jit(solution)/shard_map/all_to_all | solution.py:162
  172.7 5.7 %all-to-all-start.6 = ((bf16[16,16,384]{2,1,0:T(8,128)(2,1)}), bf16[16,16,384]{2,1,0:T(8,128)(2,1)S(1)}, u32[]{:S(2)}, u32[]{:S(2)}) async-start(bf16[16,16,384]{2,1,0:T(8,128)(2,1)} %shard_map.101), calls=%async_computation.6 | async-start | bytes 393216 | tf_op jit(solution)/shard_map/all_to_all | solution.py:162
  178.8 10.0 %all-to-all-done.6.refs_0_ = bf16[16,16,384]{2,1,0:T(8,128)(2,1)S(1)} async-done(((bf16[16,16,384]{2,1,0:T(8,128)(2,1)}), bf16[16,16,384]{2,1,0:T(8,128)(2,1)S(1)}, u32[]{:S(2)}, u32[]{:S(2)}) %all-to-all-start.6) | async-done | bytes 196640 | tf_op jit(solution)/shard_map/all_to_all | solution.py:162
  191.3 3.5 %all-to-all-start.7 = ((bf16[16,16,384]{2,1,0:T(8,128)(2,1)}), bf16[16,16,384]{2,1,0:T(8,128)(2,1)S(1)}, u32[]{:S(2)}, u32[]{:S(2)}) async-start(bf16[16,16,384]{2,1,0:T(8,128)(2,1)} %get-tuple-element.48), calls=%async_computation.7 | async-start | bytes 393216 | tf_op jit(solution)/shard_map/all_to_all | solution.py:162
  195.1 7.2 %all-to-all-done.7.refs_0_ = bf16[16,16,384]{2,1,0:T(8,128)(2,1)S(1)} async-done(((bf16[16,16,384]{2,1,0:T(8,128)(2,1)}), bf16[16,16,384]{2,1,0:T(8,128)(2,1)S(1)}, u32[]{:S(2)}, u32[]{:S(2)}) %all-to-all-start.7) | async-done | bytes 196640 | tf_op jit(solution)/shard_map/all_to_all | solution.py:162
  204.1 3.7 %all-to-all-start.8 = ((f32[16,8,384]{2,1,0:T(8,128)}), f32[16,8,384]{2,1,0:T(8,128)S(1)}, u32[]{:S(2)}, u32[]{:S(2)}) async-start(f32[16,8,384]{2,1,0:T(8,128)} %get-tuple-element.50), calls=%async_computation.8 | async-start | bytes 393216 | tf_op jit(solution)/shard_map/all_to_all | solution.py:162
  207.8 6.9 %all-to-all-done.8.got_ref = f32[16,8,384]{2,1,0:T(8,128)S(1)} async-done(((f32[16,8,384]{2,1,0:T(8,128)}), f32[16,8,384]{2,1,0:T(8,128)S(1)}, u32[]{:S(2)}, u32[]{:S(2)}) %all-to-all-start.8) | async-done | bytes 196640 | tf_op jit(solution)/shard_map/all_to_all | solution.py:162
  217.6 5.7 %all-to-all-start.9 = ((bf16[16,16,384]{2,1,0:T(8,128)(2,1)}), bf16[16,16,384]{2,1,0:T(8,128)(2,1)S(1)}, u32[]{:S(2)}, u32[]{:S(2)}) async-start(bf16[16,16,384]{2,1,0:T(8,128)(2,1)} %shard_map.104), calls=%async_computation.9 | async-start | bytes 393216 | tf_op jit(solution)/shard_map/all_to_all | solution.py:162
  223.7 10.0 %all-to-all-done.9.refs_0_ = bf16[16,16,384]{2,1,0:T(8,128)(2,1)S(1)} async-done(((bf16[16,16,384]{2,1,0:T(8,128)(2,1)}), bf16[16,16,384]{2,1,0:T(8,128)(2,1)S(1)}, u32[]{:S(2)}, u32[]{:S(2)}) %all-to-all-start.9) | async-done | bytes 196640 | tf_op jit(solution)/shard_map/all_to_all | solution.py:162
  237.3 3.5 %all-to-all-start.10 = ((f32[16,1,2048]{2,1,0:T(1,128)}), f32[16,1,2048]{2,1,0:T(1,128)S(1)}, u32[]{:S(2)}, u32[]{:S(2)}) async-start(f32[16,1,2048]{2,1,0:T(1,128)} %reshape.46), calls=%async_computation.10 | async-start | bytes 262144 | tf_op jit(solution)/shard_map/all_to_all | solution.py:162
  242.3 5.6 %all-to-all-done.10 = f32[16,1,2048]{2,1,0:T(1,128)S(1)} async-done(((f32[16,1,2048]{2,1,0:T(1,128)}), f32[16,1,2048]{2,1,0:T(1,128)S(1)}, u32[]{:S(2)}, u32[]{:S(2)}) %all-to-all-start.10) | async-done | bytes 131104 | tf_op jit(solution)/shard_map/all_to_all | solution.py:162
  (86 shorter events, 39.0 us)
Async XLA Ops:
  66.6 1.6 copy-start
  68.2 1.6 copy-start.2
  69.8 11.3 %copy-start.1 = (bf16[4096,256]{1,0:T(8,128)(2,1)S(1)}, bf16[4096,256]{1,0:T(8,128)(2,1)}, u32[]{:S(2)}) copy-start(bf16[4096,256]{1,0:T(8,128)(2,1)} %get-tuple-element.31.derivs_ref.refs_3_.refs_4_) | copy-start | bytes 6291460
  71.1 20.3 %all-to-all-start = ((bf16[16,16,384]{2,1,0:T(8,128)(2,1)}), bf16[16,16,384]{2,1,0:T(8,128)(2,1)S(1)}, u32[]{:S(2)}, u32[]{:S(2)}) async-start(bf16[16,16,384]{2,1,0:T(8,128)(2,1)} %shard_map.95), calls=%async_computation | async-start | bytes 393216 | tf_op jit(solution)/shard_map/all_to_all | solution.py:162
  81.1 3.3 %copy-start.9 = (f32[4096,8]{0,1:T(8,128)S(1)}, f32[4096,8]{0,1:T(8,128)}, u32[]{:S(2)}) copy-start(f32[4096,8]{0,1:T(8,128)} %param.13) | copy-start | bytes 393220
  93.8 18.6 %all-to-all-start.1 = ((f32[16,24,384]{2,1,0:T(8,128)}), f32[16,24,384]{2,1,0:T(8,128)S(1)}, u32[]{:S(2)}, u32[]{:S(2)}) async-start(f32[16,24,384]{2,1,0:T(8,128)} %get-tuple-element.34), calls=%async_computation.1 | async-start | bytes 1179648 | tf_op jit(solution)/shard_map/all_to_all | solution.py:162
  114.2 10.5 %all-to-all-start.2 = ((f32[16,8,384]{2,1,0:T(8,128)}), f32[16,8,384]{2,1,0:T(8,128)S(1)}, u32[]{:S(2)}, u32[]{:S(2)}) async-start(f32[16,8,384]{2,1,0:T(8,128)} %get-tuple-element.36), calls=%async_computation.2 | async-start | bytes 393216 | tf_op jit(solution)/shard_map/all_to_all | solution.py:162
  124.7 1.6 copy-start.3
  126.3 7.3 %copy-start.7 = (f32[16,8,384]{2,1,0:T(8,128)}, f32[16,8,384]{2,1,0:T(8,128)S(1)}, u32[]{:S(2)}) copy-start(f32[16,8,384]{2,1,0:T(8,128)S(1)} %all-to-all-done.2.got_ref) | copy-start | bytes 589828
  127.7 16.3 %all-to-all-start.3 = ((bf16[16,16,384]{2,1,0:T(8,128)(2,1)}), bf16[16,16,384]{2,1,0:T(8,128)(2,1)S(1)}, u32[]{:S(2)}, u32[]{:S(2)}) async-start(bf16[16,16,384]{2,1,0:T(8,128)(2,1)} %shard_map.98), calls=%async_computation.3 | async-start | bytes 393216 | tf_op jit(solution)/shard_map/all_to_all | solution.py:162
  133.7 16.3 %slice-start.1 = ((f32[16,8,384]{2,1,0:T(8,128)}), f32[16,8,256]{2,1,0:T(8,128)S(1)}, s32[]{:S(2)}) async-start(f32[16,8,384]{2,1,0:T(8,128)} %copy-done.7), calls=%async_computation.12 | async-start | bytes 262144 | tf_op jit(solution)/shard_map/slice | solution.py:409
  146.4 11.0 %all-to-all-start.4 = ((bf16[16,16,384]{2,1,0:T(8,128)(2,1)}), bf16[16,16,384]{2,1,0:T(8,128)(2,1)S(1)}, u32[]{:S(2)}, u32[]{:S(2)}) async-start(bf16[16,16,384]{2,1,0:T(8,128)(2,1)} %get-tuple-element.41), calls=%async_computation.4 | async-start | bytes 393216 | tf_op jit(solution)/shard_map/all_to_all | solution.py:162
  159.2 10.6 %all-to-all-start.5 = ((f32[16,8,384]{2,1,0:T(8,128)}), f32[16,8,384]{2,1,0:T(8,128)S(1)}, u32[]{:S(2)}, u32[]{:S(2)}) async-start(f32[16,8,384]{2,1,0:T(8,128)} %get-tuple-element.44), calls=%async_computation.5 | async-start | bytes 393216 | tf_op jit(solution)/shard_map/all_to_all | solution.py:162
  169.8 1.6 copy-start.4
  171.4 7.4 %copy-start.8 = (f32[16,8,384]{2,1,0:T(8,128)}, f32[16,8,384]{2,1,0:T(8,128)S(1)}, u32[]{:S(2)}) copy-start(f32[16,8,384]{2,1,0:T(8,128)S(1)} %all-to-all-done.5.got_ref) | copy-start | bytes 589828
  172.7 16.1 %all-to-all-start.6 = ((bf16[16,16,384]{2,1,0:T(8,128)(2,1)}), bf16[16,16,384]{2,1,0:T(8,128)(2,1)S(1)}, u32[]{:S(2)}, u32[]{:S(2)}) async-start(bf16[16,16,384]{2,1,0:T(8,128)(2,1)} %shard_map.101), calls=%async_computation.6 | async-start | bytes 393216 | tf_op jit(solution)/shard_map/all_to_all | solution.py:162
  178.8 16.0 %slice-start.2 = ((f32[16,8,384]{2,1,0:T(8,128)}), f32[16,8,256]{2,1,0:T(8,128)S(1)}, s32[]{:S(2)}) async-start(f32[16,8,384]{2,1,0:T(8,128)} %copy-done.8), calls=%async_computation.13 | async-start | bytes 262144 | tf_op jit(solution)/shard_map/slice | solution.py:409
  191.3 11.0 %all-to-all-start.7 = ((bf16[16,16,384]{2,1,0:T(8,128)(2,1)}), bf16[16,16,384]{2,1,0:T(8,128)(2,1)S(1)}, u32[]{:S(2)}, u32[]{:S(2)}) async-start(bf16[16,16,384]{2,1,0:T(8,128)(2,1)} %get-tuple-element.48), calls=%async_computation.7 | async-start | bytes 393216 | tf_op jit(solution)/shard_map/all_to_all | solution.py:162
  204.1 10.6 %all-to-all-start.8 = ((f32[16,8,384]{2,1,0:T(8,128)}), f32[16,8,384]{2,1,0:T(8,128)S(1)}, u32[]{:S(2)}, u32[]{:S(2)}) async-start(f32[16,8,384]{2,1,0:T(8,128)} %get-tuple-element.50), calls=%async_computation.8 | async-start | bytes 393216 | tf_op jit(solution)/shard_map/all_to_all | solution.py:162
  214.7 1.6 copy-start.5
  216.3 7.4 %copy-start.6 = (f32[16,8,384]{2,1,0:T(8,128)}, f32[16,8,384]{2,1,0:T(8,128)S(1)}, u32[]{:S(2)}) copy-start(f32[16,8,384]{2,1,0:T(8,128)S(1)} %all-to-all-done.8.got_ref) | copy-start | bytes 589828
  217.6 16.1 %all-to-all-start.9 = ((bf16[16,16,384]{2,1,0:T(8,128)(2,1)}), bf16[16,16,384]{2,1,0:T(8,128)(2,1)S(1)}, u32[]{:S(2)}, u32[]{:S(2)}) async-start(bf16[16,16,384]{2,1,0:T(8,128)(2,1)} %shard_map.104), calls=%async_computation.9 | async-start | bytes 393216 | tf_op jit(solution)/shard_map/all_to_all | solution.py:162
  223.7 17.0 %slice-start = ((f32[16,8,384]{2,1,0:T(8,128)}), f32[16,8,256]{2,1,0:T(8,128)S(1)}, s32[]{:S(2)}) async-start(f32[16,8,384]{2,1,0:T(8,128)} %copy-done.6), calls=%async_computation.11 | async-start | bytes 262144 | tf_op jit(solution)/shard_map/slice | solution.py:409
  237.3 10.6 %all-to-all-start.10 = ((f32[16,1,2048]{2,1,0:T(1,128)}), f32[16,1,2048]{2,1,0:T(1,128)S(1)}, u32[]{:S(2)}, u32[]{:S(2)}) async-start(f32[16,1,2048]{2,1,0:T(1,128)} %reshape.46), calls=%async_computation.10 | async-start | bytes 262144 | tf_op jit(solution)/shard_map/all_to_all | solution.py:162

commit v5 on v4

--- a/solution.py
+++ b/solution.py
@@ -15,6 +15,7 @@
 LANES = 128
 ROWS = 8
 GROUP = 64
+COPIES = 4
 
 
 def build_kernel(
@@ -78,24 +79,29 @@
 
     lax.fori_loop(0, tiles, contract, 0)
 
+    def turned(value):
+        return jnp.concatenate([value[2:4], value[0:2]])
+
     def pairs(group, carry):
         for j in range(GROUP):
 
-            def take(which, part):
-                return table_ref[pl.ds(pl.multiple_of(place_ref[which * params + group * GROUP + j], 4) + part * 2, 2), :]
-
-            ia, jb, ib, ja = (take(which, 0) for which in range(4))
-            e_ia, e_jb, e_ib, e_ja = (take(which, 1) for which in range(4))
-            spot = pl.ds(2 * j, 2)
+            def take(which):
+                return table_ref[pl.ds(pl.multiple_of(place_ref[which * params + group * GROUP + j], 4), 4), :]
+
+            ia, jb, ib, ja = (take(which) for which in range(4))
+            spot = pl.ds(4 * j, 4)
             first_ref[spot, :] = ia * jb - ib * ja
-            second_ref[spot, :] = (e_ia * jb + ia * e_jb) - (e_ib * ja + ib * e_ja)
-        for source, target in ((first_ref, derivs_ref), (second_ref, energy_derivs_ref)):
+            second_ref[spot, :] = ia * turned(jb) - ib * turned(ja)
+        for source, target, parts in ((first_ref, derivs_ref, 1), (second_ref, energy_derivs_ref, 2)):
             for row in range(0, GROUP, 2 * ROWS):
                 for half in range(2):
+                    value = source[pl.ds(row * 4 + half, 2 * ROWS, stride=4), :]
+                    if parts == 2:
+                        value = value + source[pl.ds(row * 4 + 2 + half, 2 * ROWS, stride=4), :]
                     target[
                         pl.ds(pl.multiple_of(group * GROUP + row, 2 * ROWS), 2 * ROWS),
                         half * LANES : (half + 1) * LANES,
-                    ] = source[pl.ds(row * 2 + half, 2 * ROWS, stride=2), :].astype(jnp.bfloat16)
+                    ] = value.astype(jnp.bfloat16)
         return carry
 
     lax.fori_loop(0, params // GROUP, pairs, 0)
@@ -125,8 +131,8 @@
             pltpu.VMEM((electrons, 2 * orbital_count, walkers), jnp.float32),
             pltpu.VMEM((walkers // LANES, electrons * electrons, ROWS, LANES), jnp.float32),
             pltpu.VMEM((electrons * orbital_count * 4, LANES), jnp.float32),
-            pltpu.VMEM((GROUP * 2, LANES), jnp.float32),
-            pltpu.VMEM((GROUP * 2, LANES), jnp.float32),
+            pltpu.VMEM((GROUP * 4, LANES), jnp.float32),
+            pltpu.VMEM((GROUP * 4, LANES), jnp.float32),
         ],
         compiler_params=pltpu.CompilerParams(vmem_limit_bytes=60 * 1024 * 1024),
     )(
@@ -187,14 +193,17 @@
     return right, jnp.sum(jnp.where(diagonal, matrix, 0.0), axis=1, keepdims=True)
 
 
-def advance_kernel(step, share, *refs):
-    if step:
+def advance_kernel(step, share, last, *refs):
+    if last:
+        got_ref, own_ref, state_ref, cents_ref = refs[:4]
+        rows_refs = refs[4 : 4 + step]
+        tail_ref, grams_ref, sent_ref = refs[4 + step :]
+    elif step:
         got_ref, own_ref, state_ref, cents_ref, derivs_ref = refs[:5]
-        outs = refs[5:]
+        block_ref, tail_ref, grams_ref, rows_ref, sent_ref = refs[5:]
     else:
         got_ref, own_ref, sums_ref, derivs_ref = refs[:4]
-        outs = refs[4:]
-    block_ref, tail_ref, grams_ref, rows_ref, sent_ref = outs
+        block_ref, tail_ref, grams_ref, rows_ref, sent_ref = refs[4:]
     sources, _, width = got_ref.shape
     walkers = width - LANES
     owned = own_ref.shape[1]
@@ -226,7 +235,8 @@
     right = right * lax.rsqrt(pivots)
     plain = right[:, owned : owned + walkers]
     energy = right[:, owned + walkers : owned + 2 * walkers]
-    block_ref[...] = right[:, : owned + 2 * walkers]
+    if not last:
+        block_ref[...] = right[:, : owned + 2 * walkers]
     tail = right[:, owned + 2 * walkers :]
     if step:
         centers = [tail[:, 0:1], tail[:, 1:2]]
@@ -237,6 +247,16 @@
     center = jnp.concatenate(centers)
     rows = (jnp.concatenate([plain, energy]) - center).astype(jnp.bfloat16)
     wide = rows.astype(jnp.float32)
+    if last:
+        lefts = jnp.concatenate([state_ref[:, owned : owned + walkers], plain])
+        every = [ref[...] for ref in rows_refs] + [wide]
+        rights = [value[:count] for value in every] + [value[count:] for value in every]
+        size = 2 * count * len(every)
+        rights = jnp.concatenate(rights + [jnp.zeros((LANES - size, walkers), jnp.float32)])
+        products = dot_nt(lefts, rights)
+        for owner in range(sent_ref.shape[0]):
+            sent_ref[owner] = products
+        return
     rows_ref[...] = wide
     filled = jnp.concatenate([plain, jnp.zeros((LANES - count, walkers), jnp.float32)])
     if step:
@@ -318,41 +338,66 @@
         sent_ref[target, :, owned:] = grams
 
 
-def project_kernel(got_ref, derivs_ref, energy_ref, sent_ref):
+def project_kernel(got_ref, derivs_ref, energy_ref, sent_ref, plain_ref, wide_ref, sems):
     sources, count, width = got_ref.shape
     owned = width - LANES
+    rows = plain_ref.shape[0]
+    chunk = rows // COPIES
+    copies = []
+    for part in range(COPIES):
+        where = pl.ds(part * chunk, chunk)
+        for number, (source, target) in enumerate(((derivs_ref, plain_ref), (energy_ref, wide_ref))):
+            copies.append(
+                pltpu.make_async_copy(source.at[where, :], target.at[where, :], sems.at[part, number])
+            )
+            copies[-1].start()
     grams = jnp.zeros((count, LANES), jnp.float32)
+    for source in range(sources):
+        grams += got_ref[source, :, owned:]
+    high, middle, low = in_thirds(jnp.where(lanes_of(grams.shape) < LANES // 2, grams, 0.0))
+    side = jnp.concatenate([high + pltpu.roll(low, LANES // 2, 1), middle]).astype(jnp.bfloat16)
     plain = energy = None
-    for source in range(sources):
-        values = got_ref[source]
-        grams += values[:, owned:]
-        values = values[:, :owned]
-        high = values.astype(jnp.bfloat16).astype(jnp.float32)
-        both = jnp.concatenate([high, values - high]).astype(jnp.bfloat16)
-        where = slice(source * owned, (source + 1) * owned)
-        more = [
-            jnp.dot(both, table[where, :], preferred_element_type=jnp.float32)
-            for table in (derivs_ref, energy_ref)
-        ]
-        plain, energy = more if plain is None else (plain + more[0], energy + more[1])
+    for part in range(COPIES):
+        copies[2 * part].wait()
+        copies[2 * part + 1].wait()
+        for source in range(part * sources // COPIES, (part + 1) * sources // COPIES):
+            values = got_ref[source, :, :owned]
+            high = values.astype(jnp.bfloat16).astype(jnp.float32)
+            both = jnp.concatenate([high, values - high]).astype(jnp.bfloat16)
+            where = slice(source * owned, (source + 1) * owned)
+            more = [
+                jnp.dot(both, table[where, :], preferred_element_type=jnp.float32)
+                for table in (plain_ref, wide_ref)
+            ]
+            plain, energy = more if plain is None else (plain + more[0], energy + more[1])
     images = jnp.concatenate([plain[:count] + plain[count:], energy[:count] + energy[count:]])
-    high, middle, low = in_thirds(jnp.where(lanes_of(grams.shape) < LANES // 2, grams, 0.0))
-    side = jnp.concatenate([high + pltpu.roll(low, LANES // 2, 1), middle])
+    images = images.astype(jnp.bfloat16)
     walkers = images.shape[1]
     for target in range(sent_ref.shape[0]):
-        sent_ref[target, :, :walkers] = images.astype(jnp.bfloat16)
-        sent_ref[target, :, walkers:] = side.astype(jnp.bfloat16)
-
-
-def stage(body, outs, args, scratch=()):
+        sent_ref[target, :, :walkers] = images
+        sent_ref[target, :, walkers:] = side
+
+
+def finish_kernel(walkers, got_ref, first_ref, second_ref):
+    total = got_ref[0]
+    for source in range(1, got_ref.shape[0]):
+        total += got_ref[source]
+    total = total * (1.0 / walkers)
+    size = first_ref.shape[0]
+    unit = jnp.where(lanes_of(total.shape) == lax.broadcasted_iota(jnp.int32, total.shape, 0), 1.0, 0.0)
+    first_ref[...] = (pltpu.roll(total, LANES - size, 1) + ENERGY_SHIFT * unit)[:, :size]
+    second_ref[...] = (total + EPS_SHIFT * unit)[:, :size]
+
+
+def stage(body, outs, args, scratch=(), outside=0, limit=20):
     vmem = pl.BlockSpec(memory_space=pltpu.VMEM)
     return pl.pallas_call(
         body,
         out_shape=[jax.ShapeDtypeStruct(shape, dtype) for shape, dtype in outs],
-        in_specs=[vmem] * len(args),
+        in_specs=[vmem] * (len(args) - outside) + [pl.BlockSpec(memory_space=pl.ANY)] * outside,
         out_specs=[vmem] * len(outs),
         scratch_shapes=list(scratch),
-        compiler_params=pltpu.CompilerParams(vmem_limit_bytes=20 * 1024 * 1024),
+        compiler_params=pltpu.CompilerParams(vmem_limit_bytes=limit * 1024 * 1024),
     )(*args)
 
 
@@ -382,7 +427,7 @@
         axis=2,
     )
     state = cents = stats = None
-    wholes, plains, rows = [], [], []
+    wholes, rows = [], []
     for step in range(ITERS + 1):
         if step:
             pieces = exchange(sent, "walker")
@@ -390,31 +435,44 @@
             project_kernel,
             [((param_devices, 2 * count, local_walkers + LANES), bf16)],
             (pieces, derivs, energy_derivs),
+            [pltpu.VMEM(derivs.shape, bf16)] * 2 + [pltpu.SemaphoreType.DMA((COPIES, 2))],
+            2,
+            60,
         )
         got = exchange(sent, "param")
-        outs = [
-            ((count, owned + 2 * local_walkers), f32),
-            ((count, LANES), f32),
-            ((count, LANES), f32),
-            ((2 * count, local_walkers), f32),
-            ((walker_devices, 2 * count, owned + LANES), bf16)
-            if step
-            else ((walker_devices, 3 * count, owned + LANES), f32),
-        ]
-        block, tail, grams, wide, sent = stage(
-            functools.partial(advance_kernel, step, owned),
-            outs,
-            (got, own, state, cents, derivs) if step else (got, own, sums, derivs),
-        )
+        last = step == ITERS
+        body = functools.partial(advance_kernel, step, owned, last)
+        if last:
+            tail, grams, sent = stage(
+                body,
+                [
+                    ((count, LANES), f32),
+                    ((count, LANES), f32),
+                    ((walker_devices, count * (ITERS + 1), LANES), f32),
+                ],
+                (got, own, state, cents, *rows),
+            )
+        else:
+            outs = [
+                ((count, owned + 2 * local_walkers), f32),
+                ((count, LANES), f32),
+                ((count, LANES), f32),
+                ((2 * count, local_walkers), f32),
+                ((walker_devices, 2 * count, owned + LANES), bf16)
+                if step
+                else ((walker_devices, 3 * count, owned + LANES), f32),
+            ]
+            block, tail, grams, wide, sent = stage(
+                body, outs, (got, own, state, cents, derivs) if step else (got, own, sums, derivs)
+            )
         whole = pieces[:, :, :owned].transpose(1, 0, 2).reshape(count, block_rows)
         if step:
             whole = whole - dot_nn(grams[:, : count * step], jnp.concatenate(wholes))
         wholes.append(dot_nn(tail[:, LANES // 2 : LANES // 2 + count], whole))
-        plains.append(block[:, owned : owned + local_walkers])
+        if last:
+            break
         rows.append(wide)
         state = block if step == 0 else jnp.concatenate([state, block])
-        if step == ITERS:
-            break
         got = exchange(sent, "walker")
         outs = [
             ((count, owned), f32),
@@ -435,14 +493,12 @@
             )
             shift = tail[:, :2] - cents[:, :2]
             rows[0] = wide + shift.T.reshape(2 * count, 1)
-    lefts = jnp.concatenate(plains)
-    rights = jnp.concatenate([r[:count] for r in rows] + [r[count:] for r in rows])
-    proj = dot_nt(lefts, rights)
-    proj = exchange(jnp.broadcast_to(proj[None], (walker_devices,) + proj.shape), "walker")
-    proj = jnp.sum(proj, axis=0) / walkers
-    size = lefts.shape[0]
-    proj_s = proj[:, :size] + EPS_SHIFT * jnp.eye(size)
-    proj_h = proj[:, size:] + ENERGY_SHIFT * jnp.eye(size)
+    size = count * (ITERS + 1)
+    proj_h, proj_s = stage(
+        functools.partial(finish_kernel, walkers),
+        [((size, size), f32)] * 2,
+        (exchange(sent, "walker"),),
+    )
     return (math.sqrt(params) * jnp.concatenate(wholes).T, proj_h, proj_s)
 
 

time: 252 us -> 252 us (level)
  blocking collectives: 0 us -> 29.1 us
  waiting for transfers between devices: 89.2 us -> 70.7 us
  starting transfers between devices: 55.7 us -> 44.9 us
  Pallas kernels: 82.3 us -> 91.8 us
  local copies, waits for them, and re-layouts: 9.72 us -> 2.53 us
    all_to_all x0 -> x2, blocking collectives: none -> 29.1 us  [exchange(): return lax.all_to_all(parts, axis, 0, 0)]
    all_to_all x11 -> x9, waiting for transfers between devices: 89.2 us -> 70.7 us  [exchange(): return lax.all_to_all(parts, axis, 0, 0)]
    all_to_all x11 -> x9, starting transfers between devices: 55.7 us -> 44.9 us  [exchange(): return lax.all_to_all(parts, axis, 0, 0)]
    pallas_call x11 -> x12, Pallas kernels: 20.3 us -> 30.7 us  [stage(): pl.pallas_call(body, out_shape=[jax.ShapeDtypeStruct(shape, dtype) for sh...]
    unnamed x31 -> x14, local copies, waits for them, and re-layouts: 8.94 us -> 1.38 us
  transfers between devices with their start and end apart: 11 -> 9, of which waited for: 11 -> 9; matrix products, arithmetic and copies ran while one was open for 3% -> 3% of each run, Pallas kernels for 0% -> 0%
where the time goes in v5:
time: 252 us; the launch traced here: 251 us
  Pallas kernels  91.8 us (36%)
  waiting for transfers between devices  70.7 us (28%)
  starting transfers between devices  44.9 us (18%)
  blocking collectives  29.1 us (12%)
  other arithmetic  7.62 us (3%)
  matrix products  3.47 us (1%)
  local copies, waits for them, and re-layouts  2.53 us (1%)
    all_to_all x9, waiting for transfers between devices, exchange(): return lax.all_to_all(parts, axis, 0, 0)  70.7 us
    pallas_call x1, Pallas kernels, build(): pl.pallas_call(build_kernel, out_shape=[jax.ShapeDtypeStruct((params, wal...  61.1 us
    all_to_all x9, starting transfers between devices, exchange(): return lax.all_to_all(parts, axis, 0, 0)  44.9 us
    pallas_call x12, Pallas kernels, stage(): pl.pallas_call(body, out_shape=[jax.ShapeDtypeStruct(shape, dtype) for sh...  30.7 us
    all_to_all x2, blocking collectives, exchange(): return lax.all_to_all(parts, axis, 0, 0)  29.1 us
  transfers between devices with their start and end apart: 9, of which 9 were waited for; matrix products, arithmetic and copies ran while one was open for 3% of the time, Pallas kernels for 0%

profile of v5, /device:TPU:1, one launch (start us, length us, event | category | flops | bytes accessed | tf_op | source)
XLA Modules:
  0.0 251.0 jit_solution(4948010667246021871)
XLA Ops:
  5.4 61.1 %shard_map.94 = (bf16[4096,256]{1,0:T(8,128)(2,1)}, bf16[4096,256]{1,0:T(8,128)(2,1)}) custom-call(s32[16384]{0:T(1024)} %pad_add_fusion.place_ref, s32[16,256]{1,0:T(8,128)} %occupation_ref.1, f32[256,256]{1,0:T(8,128)} %bitcast.40, f32[1024,512]{1,0:T(8,128)} %orbitals_ref.1, f32[1024,512]{1,0:T(8,128)} %hop_ref.1, f32[1,256]{1,0:T(1,128)} %bitcast.48), custom_call_target="tpu_custom_call" | custom-call | tf_op jit(solution)/shard_map/pallas_call | solution.py:122
  66.4 4.2 %shard_map.95 = bf16[16,16,384]{2,1,0:T(8,128)(2,1)} custom-call(f32[16,8,384]{2,1,0:T(8,128)} %pad_maximum_fusion.got_ref, bf16[4096,256]{1,0:T(8,128)(2,1)} %get-tuple-element.32.derivs_ref.refs_3_.refs_4_, bf16[4096,256]{1,0:T(8,128)(2,1)} %get-tuple-element.33.energy_ref), custom_call_target="tpu_custom_call" | custom-call | tf_op jit(solution)/shard_map/pallas_call | solution.py:394
  70.7 10.0 %all-to-all-start = ((bf16[16,16,384]{2,1,0:T(8,128)(2,1)}), bf16[16,16,384]{2,1,0:T(8,128)(2,1)S(1)}, u32[]{:S(2)}, u32[]{:S(2)}) async-start(bf16[16,16,384]{2,1,0:T(8,128)(2,1)} %shard_map.95), calls=%async_computation | async-start | bytes 393216 | tf_op jit(solution)/shard_map/all_to_all | solution.py:168
  84.1 6.9 %all-to-all-done.refs_0_ = bf16[16,16,384]{2,1,0:T(8,128)(2,1)S(1)} async-done(((bf16[16,16,384]{2,1,0:T(8,128)(2,1)}), bf16[16,16,384]{2,1,0:T(8,128)(2,1)S(1)}, u32[]{:S(2)}, u32[]{:S(2)}) %all-to-all-start) | async-done | bytes 196640 | tf_op jit(solution)/shard_map/all_to_all | solution.py:168
  93.0 18.7 %all_to_all.55.refs_0_ = f32[16,24,384]{2,1,0:T(8,128)S(1)} all-to-all(f32[16,24,384]{2,1,0:T(8,128)S(1)} %get-tuple-element.35), channel_id=1, replica_groups=mesh['walker'=16,'param'=16] {'walker'}, dimensions={0} | all-to-all | bytes 1179648 | tf_op jit(solution)/shard_map/all_to_all | solution.py:168
  112.8 10.4 %all_to_all.56.got_ref = f32[16,8,384]{2,1,0:T(8,128)} all-to-all(f32[16,8,384]{2,1,0:T(8,128)S(1)} %get-tuple-element.37), channel_id=1, replica_groups=mesh['walker'=16,'param'=16] {'walker'}, dimensions={0} | all-to-all | bytes 393216 | tf_op jit(solution)/shard_map/all_to_all | solution.py:168
  123.2 4.2 %shard_map.98 = bf16[16,16,384]{2,1,0:T(8,128)(2,1)} custom-call(f32[16,8,384]{2,1,0:T(8,128)} %all_to_all.56.got_ref, bf16[4096,256]{1,0:T(8,128)(2,1)} %get-tuple-element.32.derivs_ref.refs_3_.refs_4_, bf16[4096,256]{1,0:T(8,128)(2,1)} %get-tuple-element.33.energy_ref), custom_call_target="tpu_custom_call" | custom-call | tf_op jit(solution)/shard_map/pallas_call | solution.py:394
  127.4 5.5 %all-to-all-start.3 = ((bf16[16,16,384]{2,1,0:T(8,128)(2,1)}), bf16[16,16,384]{2,1,0:T(8,128)(2,1)S(1)}, u32[]{:S(2)}, u32[]{:S(2)}) async-start(bf16[16,16,384]{2,1,0:T(8,128)(2,1)} %shard_map.98), calls=%async_computation.3 | async-start | bytes 393216 | tf_op jit(solution)/shard_map/all_to_all | solution.py:168
  133.3 10.0 %all-to-all-done.3.refs_0_ = bf16[16,16,384]{2,1,0:T(8,128)(2,1)S(1)} async-done(((bf16[16,16,384]{2,1,0:T(8,128)(2,1)}), bf16[16,16,384]{2,1,0:T(8,128)(2,1)S(1)}, u32[]{:S(2)}, u32[]{:S(2)}) %all-to-all-start.3) | async-done | bytes 196640 | tf_op jit(solution)/shard_map/all_to_all | solution.py:168
  145.7 3.5 %all-to-all-start.4 = ((bf16[16,16,384]{2,1,0:T(8,128)(2,1)}), bf16[16,16,384]{2,1,0:T(8,128)(2,1)S(1)}, u32[]{:S(2)}, u32[]{:S(2)}) async-start(bf16[16,16,384]{2,1,0:T(8,128)(2,1)} %get-tuple-element.42), calls=%async_computation.4 | async-start | bytes 393216 | tf_op jit(solution)/shard_map/all_to_all | solution.py:168
  149.4 7.3 %all-to-all-done.4.refs_0_ = bf16[16,16,384]{2,1,0:T(8,128)(2,1)S(1)} async-done(((bf16[16,16,384]{2,1,0:T(8,128)(2,1)}), bf16[16,16,384]{2,1,0:T(8,128)(2,1)S(1)}, u32[]{:S(2)}, u32[]{:S(2)}) %all-to-all-start.4) | async-done | bytes 196640 | tf_op jit(solution)/shard_map/all_to_all | solution.py:168
  158.5 3.6 %all-to-all-start.5 = ((f32[16,8,384]{2,1,0:T(8,128)}), f32[16,8,384]{2,1,0:T(8,128)S(1)}, u32[]{:S(2)}, u32[]{:S(2)}) async-start(f32[16,8,384]{2,1,0:T(8,128)} %get-tuple-element.45), calls=%async_computation.5 | async-start | bytes 393216 | tf_op jit(solution)/shard_map/all_to_all | solution.py:168
  162.2 6.9 %all-to-all-done.5.got_ref = f32[16,8,384]{2,1,0:T(8,128)S(1)} async-done(((f32[16,8,384]{2,1,0:T(8,128)}), f32[16,8,384]{2,1,0:T(8,128)S(1)}, u32[]{:S(2)}, u32[]{:S(2)}) %all-to-all-start.5) | async-done | bytes 196640 | tf_op jit(solution)/shard_map/all_to_all | solution.py:168
  169.8 4.1 %shard_map.101 = bf16[16,16,384]{2,1,0:T(8,128)(2,1)} custom-call(f32[16,8,384]{2,1,0:T(8,128)} %copy-done.4, bf16[4096,256]{1,0:T(8,128)(2,1)} %get-tuple-element.32.derivs_ref.refs_3_.refs_4_, bf16[4096,256]{1,0:T(8,128)(2,1)} %get-tuple-element.33.energy_ref), custom_call_target="tpu_custom_call" | custom-call | tf_op jit(solution)/shard_map/pallas_call | solution.py:394
  173.9 5.8 %all-to-all-start.6 = ((bf16[16,16,384]{2,1,0:T(8,128)(2,1)}), bf16[16,16,384]{2,1,0:T(8,128)(2,1)S(1)}, u32[]{:S(2)}, u32[]{:S(2)}) async-start(bf16[16,16,384]{2,1,0:T(8,128)(2,1)} %shard_map.101), calls=%async_computation.6 | async-start | bytes 393216 | tf_op jit(solution)/shard_map/all_to_all | solution.py:168
  180.0 10.1 %all-to-all-done.6.refs_0_ = bf16[16,16,384]{2,1,0:T(8,128)(2,1)S(1)} async-done(((bf16[16,16,384]{2,1,0:T(8,128)(2,1)}), bf16[16,16,384]{2,1,0:T(8,128)(2,1)S(1)}, u32[]{:S(2)}, u32[]{:S(2)}) %all-to-all-start.6) | async-done | bytes 196640 | tf_op jit(solution)/shard_map/all_to_all | solution.py:168
  196.3 7.1 %all-to-all-done.7.refs_0_ = bf16[16,16,384]{2,1,0:T(8,128)(2,1)S(1)} async-done(((bf16[16,16,384]{2,1,0:T(8,128)(2,1)}), bf16[16,16,384]{2,1,0:T(8,128)(2,1)S(1)}, u32[]{:S(2)}, u32[]{:S(2)}) %all-to-all-start.7) | async-done | bytes 196640 | tf_op jit(solution)/shard_map/all_to_all | solution.py:168
  205.3 3.6 %all-to-all-start.8 = ((f32[16,8,384]{2,1,0:T(8,128)}), f32[16,8,384]{2,1,0:T(8,128)S(1)}, u32[]{:S(2)}, u32[]{:S(2)}) async-start(f32[16,8,384]{2,1,0:T(8,128)} %get-tuple-element.51), calls=%async_computation.8 | async-start | bytes 393216 | tf_op jit(solution)/shard_map/all_to_all | solution.py:168
  209.2 6.7 %all-to-all-done.8.got_ref = f32[16,8,384]{2,1,0:T(8,128)S(1)} async-done(((f32[16,8,384]{2,1,0:T(8,128)}), f32[16,8,384]{2,1,0:T(8,128)S(1)}, u32[]{:S(2)}, u32[]{:S(2)}) %all-to-all-start.8) | async-done | bytes 196640 | tf_op jit(solution)/shard_map/all_to_all | solution.py:168
  216.6 4.1 %shard_map.104 = bf16[16,16,384]{2,1,0:T(8,128)(2,1)} custom-call(f32[16,8,384]{2,1,0:T(8,128)} %copy-done.5, bf16[4096,256]{1,0:T(8,128)(2,1)} %get-tuple-element.32.derivs_ref.refs_3_.refs_4_, bf16[4096,256]{1,0:T(8,128)(2,1)} %get-tuple-element.33.energy_ref), custom_call_target="tpu_custom_call" | custom-call | tf_op jit(solution)/shard_map/pallas_call | solution.py:394
  220.7 5.8 %all-to-all-start.9 = ((bf16[16,16,384]{2,1,0:T(8,128)(2,1)}), bf16[16,16,384]{2,1,0:T(8,128)(2,1)S(1)}, u32[]{:S(2)}, u32[]{:S(2)}) async-start(bf16[16,16,384]{2,1,0:T(8,128)(2,1)} %shard_map.104), calls=%async_computation.9 | async-start | bytes 393216 | tf_op jit(solution)/shard_map/all_to_all | solution.py:168
  227.7 9.1 %all-to-all-done.9.refs_0_ = bf16[16,16,384]{2,1,0:T(8,128)(2,1)S(1)} async-done(((bf16[16,16,384]{2,1,0:T(8,128)(2,1)}), bf16[16,16,384]{2,1,0:T(8,128)(2,1)S(1)}, u32[]{:S(2)}, u32[]{:S(2)}) %all-to-all-start.9) | async-done | bytes 196640 | tf_op jit(solution)/shard_map/all_to_all | solution.py:168
  238.7 3.5 %all-to-all-start.10 = ((f32[16,32,128]{2,1,0:T(8,128)}), f32[16,32,128]{2,1,0:T(8,128)S(1)}, u32[]{:S(2)}, u32[]{:S(2)}) async-start(f32[16,32,128]{2,1,0:T(8,128)} %get-tuple-element.58), calls=%async_computation.10 | async-start | bytes 524288 | tf_op jit(solution)/shard_map/all_to_all | solution.py:168
  243.8 6.6 %all-to-all-done.10.got_ref = f32[16,32,128]{2,1,0:T(8,128)S(1)} async-done(((f32[16,32,128]{2,1,0:T(8,128)}), f32[16,32,128]{2,1,0:T(8,128)S(1)}, u32[]{:S(2)}, u32[]{:S(2)}) %all-to-all-start.10) | async-done | bytes 262176 | tf_op jit(solution)/shard_map/all_to_all | solution.py:168
  (55 shorter events, 31.2 us)
Async XLA Ops:
  66.4 14.2 %copy-start = (bf16[4096,256]{1,0:T(8,128)(2,1)S(1)}, bf16[4096,256]{1,0:T(8,128)(2,1)}, u32[]{:S(2)}) copy-start(bf16[4096,256]{1,0:T(8,128)(2,1)} %get-tuple-element.32.derivs_ref.refs_3_.refs_4_) | copy-start | bytes 6291460
  70.7 20.3 %all-to-all-start = ((bf16[16,16,384]{2,1,0:T(8,128)(2,1)}), bf16[16,16,384]{2,1,0:T(8,128)(2,1)S(1)}, u32[]{:S(2)}, u32[]{:S(2)}) async-start(bf16[16,16,384]{2,1,0:T(8,128)(2,1)} %shard_map.95), calls=%async_computation | async-start | bytes 393216 | tf_op jit(solution)/shard_map/all_to_all | solution.py:168
  80.7 3.3 %copy-start.3 = (f32[4096,8]{0,1:T(8,128)S(1)}, f32[4096,8]{0,1:T(8,128)}, u32[]{:S(2)}) copy-start(f32[4096,8]{0,1:T(8,128)} %param.13) | copy-start | bytes 393220
  123.2 20.1 %copy-start.1 = (bf16[4096,256]{1,0:T(8,128)(2,1)S(1)}, bf16[4096,256]{1,0:T(8,128)(2,1)}, u32[]{:S(2)}) copy-start(bf16[4096,256]{1,0:T(8,128)(2,1)} %get-tuple-element.32.derivs_ref.refs_3_.refs_4_) | copy-start | bytes 6291460
  127.4 15.9 %all-to-all-start.3 = ((bf16[16,16,384]{2,1,0:T(8,128)(2,1)}), bf16[16,16,384]{2,1,0:T(8,128)(2,1)S(1)}, u32[]{:S(2)}, u32[]{:S(2)}) async-start(bf16[16,16,384]{2,1,0:T(8,128)(2,1)} %shard_map.98), calls=%async_computation.3 | async-start | bytes 393216 | tf_op jit(solution)/shard_map/all_to_all | solution.py:168
  145.7 11.0 %all-to-all-start.4 = ((bf16[16,16,384]{2,1,0:T(8,128)(2,1)}), bf16[16,16,384]{2,1,0:T(8,128)(2,1)S(1)}, u32[]{:S(2)}, u32[]{:S(2)}) async-start(bf16[16,16,384]{2,1,0:T(8,128)(2,1)} %get-tuple-element.42), calls=%async_computation.4 | async-start | bytes 393216 | tf_op jit(solution)/shard_map/all_to_all | solution.py:168
  158.5 10.6 %all-to-all-start.5 = ((f32[16,8,384]{2,1,0:T(8,128)}), f32[16,8,384]{2,1,0:T(8,128)S(1)}, u32[]{:S(2)}, u32[]{:S(2)}) async-start(f32[16,8,384]{2,1,0:T(8,128)} %get-tuple-element.45), calls=%async_computation.5 | async-start | bytes 393216 | tf_op jit(solution)/shard_map/all_to_all | solution.py:168
  162.2 17.4 %slice-start = ((f32[16,8,384]{2,1,0:T(8,128)}), f32[16,8,256]{2,1,0:T(8,128)S(1)}, s32[]{:S(2)}) async-start(f32[16,8,384]{2,1,0:T(8,128)} %all_to_all.56.got_ref), calls=%async_computation.11 | async-start | bytes 262144 | tf_op jit(solution)/shard_map/slice | solution.py:468
  162.2 27.8 %copy-start.2 = (bf16[4096,256]{1,0:T(8,128)(2,1)S(1)}, bf16[4096,256]{1,0:T(8,128)(2,1)}, u32[]{:S(2)}) copy-start(bf16[4096,256]{1,0:T(8,128)(2,1)} %get-tuple-element.32.derivs_ref.refs_3_.refs_4_) | copy-start | bytes 6291460
  169.1 0.7 copy-start.4
  173.9 16.1 %all-to-all-start.6 = ((bf16[16,16,384]{2,1,0:T(8,128)(2,1)}), bf16[16,16,384]{2,1,0:T(8,128)(2,1)S(1)}, u32[]{:S(2)}, u32[]{:S(2)}) async-start(bf16[16,16,384]{2,1,0:T(8,128)(2,1)} %shard_map.101), calls=%async_computation.6 | async-start | bytes 393216 | tf_op jit(solution)/shard_map/all_to_all | solution.py:168
  179.9 29.0 %slice-start.1 = ((f32[16,8,384]{2,1,0:T(8,128)}), f32[16,8,256]{2,1,0:T(8,128)S(1)}, s32[]{:S(2)}) async-start(f32[16,8,384]{2,1,0:T(8,128)} %copy-done.4), calls=%async_computation.12 | async-start | bytes 262144 | tf_op jit(solution)/shard_map/slice | solution.py:468
  192.5 11.0 %all-to-all-start.7 = ((bf16[16,16,384]{2,1,0:T(8,128)(2,1)}), bf16[16,16,384]{2,1,0:T(8,128)(2,1)S(1)}, u32[]{:S(2)}, u32[]{:S(2)}) async-start(bf16[16,16,384]{2,1,0:T(8,128)(2,1)} %get-tuple-element.49), calls=%async_computation.7 | async-start | bytes 393216 | tf_op jit(solution)/shard_map/all_to_all | solution.py:168
  205.3 10.6 %all-to-all-start.8 = ((f32[16,8,384]{2,1,0:T(8,128)}), f32[16,8,384]{2,1,0:T(8,128)S(1)}, u32[]{:S(2)}, u32[]{:S(2)}) async-start(f32[16,8,384]{2,1,0:T(8,128)} %get-tuple-element.51), calls=%async_computation.8 | async-start | bytes 393216 | tf_op jit(solution)/shard_map/all_to_all | solution.py:168
  215.9 0.7 copy-start.5
  220.7 16.1 %all-to-all-start.9 = ((bf16[16,16,384]{2,1,0:T(8,128)(2,1)}), bf16[16,16,384]{2,1,0:T(8,128)(2,1)S(1)}, u32[]{:S(2)}, u32[]{:S(2)}) async-start(bf16[16,16,384]{2,1,0:T(8,128)(2,1)} %shard_map.104), calls=%async_computation.9 | async-start | bytes 393216 | tf_op jit(solution)/shard_map/all_to_all | solution.py:168
  238.7 11.6 %all-to-all-start.10 = ((f32[16,32,128]{2,1,0:T(8,128)}), f32[16,32,128]{2,1,0:T(8,128)S(1)}, u32[]{:S(2)}, u32[]{:S(2)}) async-start(f32[16,32,128]{2,1,0:T(8,128)} %get-tuple-element.58), calls=%async_computation.10 | async-start | bytes 524288 | tf_op jit(solution)/shard_map/all_to_all | solution.py:168

commit v6 on v5

--- a/solution.py
+++ b/solution.py
@@ -15,7 +15,6 @@
 LANES = 128
 ROWS = 8
 GROUP = 64
-COPIES = 4
 
 
 def build_kernel(
@@ -119,7 +118,7 @@
     i, j, a, b = excitations
     places = jnp.concatenate([place(i, a), place(j, b), place(i, b), place(j, a)])
     vmem = pl.BlockSpec(memory_space=pltpu.VMEM)
-    derivs, energy_derivs = pl.pallas_call(
+    return pl.pallas_call(
         build_kernel,
         out_shape=[jax.ShapeDtypeStruct((params, walkers), jnp.bfloat16)] * 2,
         in_specs=[pl.BlockSpec(memory_space=pltpu.SMEM)] + [vmem] * 5,
@@ -134,7 +133,7 @@
             pltpu.VMEM((GROUP * 4, LANES), jnp.float32),
             pltpu.VMEM((GROUP * 4, LANES), jnp.float32),
         ],
-        compiler_params=pltpu.CompilerParams(vmem_limit_bytes=60 * 1024 * 1024),
+        compiler_params=pltpu.CompilerParams(vmem_limit_bytes=49 * 1024 * 1024),
     )(
         places,
         occupation,
@@ -143,15 +142,16 @@
         hop_orbitals,
         local_energy[None],
     )
+
+def walker_sums(derivs, energy_derivs):
     wide = derivs.astype(jnp.float32)
-    sums = jnp.stack(
+    return jnp.stack(
         [
             jnp.sum(wide, axis=1),
             jnp.sum(wide * wide, axis=1),
             jnp.sum(energy_derivs.astype(jnp.float32), axis=1),
         ]
     )
-    return derivs, energy_derivs, sums
 
 
 def dot_nt(left, right):
@@ -338,40 +338,39 @@
         sent_ref[target, :, owned:] = grams
 
 
-def project_kernel(got_ref, derivs_ref, energy_ref, sent_ref, plain_ref, wide_ref, sems):
-    sources, count, width = got_ref.shape
-    owned = width - LANES
-    rows = plain_ref.shape[0]
-    chunk = rows // COPIES
-    copies = []
-    for part in range(COPIES):
-        where = pl.ds(part * chunk, chunk)
-        for number, (source, target) in enumerate(((derivs_ref, plain_ref), (energy_ref, wide_ref))):
-            copies.append(
-                pltpu.make_async_copy(source.at[where, :], target.at[where, :], sems.at[part, number])
-            )
-            copies[-1].start()
+def project_kernel(first, got_ref, derivs_ref, energy_ref, sent_ref):
+    params = derivs_ref.shape[0]
+    if first:
+        count, sources, owned = got_ref.shape[0], 1, params
+    else:
+        sources, count, width = got_ref.shape
+        owned = width - LANES
     grams = jnp.zeros((count, LANES), jnp.float32)
+    plain = energy = None
     for source in range(sources):
-        grams += got_ref[source, :, owned:]
+        if first:
+            values = got_ref[...]
+            grams = jnp.concatenate(
+                [dot_nt(values, values), jnp.zeros((count, LANES - count), jnp.float32)], axis=1
+            )
+        else:
+            values = got_ref[source, :, :owned]
+            grams += got_ref[source, :, owned:]
+        high = values.astype(jnp.bfloat16).astype(jnp.float32)
+        both = jnp.concatenate([high, values - high]).astype(jnp.bfloat16)
+        more = [
+            jnp.dot(
+                both,
+                table[source * owned : (source + 1) * owned, :],
+                preferred_element_type=jnp.float32,
+            )
+            for table in (derivs_ref, energy_ref)
+        ]
+        plain, energy = more if plain is None else (plain + more[0], energy + more[1])
+    images = jnp.concatenate([plain[:count] + plain[count:], energy[:count] + energy[count:]])
+    images = images.astype(jnp.bfloat16)
     high, middle, low = in_thirds(jnp.where(lanes_of(grams.shape) < LANES // 2, grams, 0.0))
     side = jnp.concatenate([high + pltpu.roll(low, LANES // 2, 1), middle]).astype(jnp.bfloat16)
-    plain = energy = None
-    for part in range(COPIES):
-        copies[2 * part].wait()
-        copies[2 * part + 1].wait()
-        for source in range(part * sources // COPIES, (part + 1) * sources // COPIES):
-            values = got_ref[source, :, :owned]
-            high = values.astype(jnp.bfloat16).astype(jnp.float32)
-            both = jnp.concatenate([high, values - high]).astype(jnp.bfloat16)
-            where = slice(source * owned, (source + 1) * owned)
-            more = [
-                jnp.dot(both, table[where, :], preferred_element_type=jnp.float32)
-                for table in (plain_ref, wide_ref)
-            ]
-            plain, energy = more if plain is None else (plain + more[0], energy + more[1])
-    images = jnp.concatenate([plain[:count] + plain[count:], energy[:count] + energy[count:]])
-    images = images.astype(jnp.bfloat16)
     walkers = images.shape[1]
     for target in range(sent_ref.shape[0]):
         sent_ref[target, :, :walkers] = images
@@ -389,15 +388,15 @@
     second_ref[...] = (total + EPS_SHIFT * unit)[:, :size]
 
 
-def stage(body, outs, args, scratch=(), outside=0, limit=20):
+def stage(body, outs, args, scratch=()):
     vmem = pl.BlockSpec(memory_space=pltpu.VMEM)
     return pl.pallas_call(
         body,
         out_shape=[jax.ShapeDtypeStruct(shape, dtype) for shape, dtype in outs],
-        in_specs=[vmem] * (len(args) - outside) + [pl.BlockSpec(memory_space=pl.ANY)] * outside,
+        in_specs=[vmem] * len(args),
         out_specs=[vmem] * len(outs),
         scratch_shapes=list(scratch),
-        compiler_params=pltpu.CompilerParams(vmem_limit_bytes=limit * 1024 * 1024),
+        compiler_params=pltpu.CompilerParams(vmem_limit_bytes=20 * 1024 * 1024),
     )(*args)
 
 
@@ -413,31 +412,23 @@
     params = block_rows * param_devices
     owned = block_rows // walker_devices
     f32, bf16 = jnp.float32, jnp.bfloat16
-    derivs, energy_derivs, sums = build(
+    derivs, energy_derivs = build(
         occupation, inverse_slater, orbitals, hop_orbitals, local_energy, excitations
     )
+    sums = walker_sums(derivs, energy_derivs)
     sums = jnp.pad(sums, ((0, count - sums.shape[0]), (0, 0)))
     start = initial_block.T
     offset = lax.axis_index("walker") * owned
     own = lax.dynamic_slice_in_dim(start, offset, owned, 1)
-    gram = jnp.pad(dot_nt(start, start) / walker_devices, ((0, 0), (0, LANES - count)))
-    pieces = jnp.concatenate(
-        [start.reshape(count, walker_devices, owned).transpose(1, 0, 2),
-         jnp.broadcast_to(gram[None], (walker_devices, count, LANES))],
-        axis=2,
-    )
     state = cents = stats = None
     wholes, rows = [], []
     for step in range(ITERS + 1):
         if step:
             pieces = exchange(sent, "walker")
         (sent,) = stage(
-            project_kernel,
+            functools.partial(project_kernel, step == 0),
             [((param_devices, 2 * count, local_walkers + LANES), bf16)],
-            (pieces, derivs, energy_derivs),
-            [pltpu.VMEM(derivs.shape, bf16)] * 2 + [pltpu.SemaphoreType.DMA((COPIES, 2))],
-            2,
-            60,
+            (pieces if step else start, derivs, energy_derivs),
         )
         got = exchange(sent, "param")
         last = step == ITERS
@@ -465,8 +456,9 @@
             block, tail, grams, wide, sent = stage(
                 body, outs, (got, own, state, cents, derivs) if step else (got, own, sums, derivs)
             )
-        whole = pieces[:, :, :owned].transpose(1, 0, 2).reshape(count, block_rows)
+        whole = start
         if step:
+            whole = pieces[:, :, :owned].transpose(1, 0, 2).reshape(count, block_rows)
             whole = whole - dot_nn(grams[:, : count * step], jnp.concatenate(wholes))
         wholes.append(dot_nn(tail[:, LANES // 2 : LANES // 2 + count], whole))
         if last:

time: 252 us -> 240 us (0.952)
  Pallas kernels: 91.8 us -> 77.9 us
  local copies, waits for them, and re-layouts: 2.53 us -> 7.1 us
    pallas_call x12, Pallas kernels: 30.7 us -> 19.9 us  [stage(): pl.pallas_call(body, out_shape=[jax.ShapeDtypeStruct(shape, dtype) for sh...]
    unnamed x14 -> x20, local copies, waits for them, and re-layouts: 1.38 us -> 6.9 us
    pallas_call x1, Pallas kernels: 61.1 us -> 58 us  [build(): pl.pallas_call(build_kernel, out_shape=[jax.ShapeDtypeStruct((params, wal...]
where the time goes in v6:
time: 240 us; the launch traced here: 239 us
  Pallas kernels  77.9 us (32%)
  waiting for transfers between devices  71.6 us (30%)
  starting transfers between devices  44.8 us (19%)
  blocking collectives  29 us (12%)
  local copies, waits for them, and re-layouts  7.1 us (3%)
  other arithmetic  5.35 us (2%)
    all_to_all x9, waiting for transfers between devices, exchange(): return lax.all_to_all(parts, axis, 0, 0)  71.6 us
    pallas_call x1, Pallas kernels, build(): pl.pallas_call(build_kernel, out_shape=[jax.ShapeDtypeStruct((params, wal...  58 us
    all_to_all x9, starting transfers between devices, exchange(): return lax.all_to_all(parts, axis, 0, 0)  44.8 us
    all_to_all x2, blocking collectives, exchange(): return lax.all_to_all(parts, axis, 0, 0)  29 us
    pallas_call x12, Pallas kernels, stage(): pl.pallas_call(body, out_shape=[jax.ShapeDtypeStruct(shape, dtype) for sh...  19.9 us
    unnamed x20, local copies, waits for them, and re-layouts  6.9 us
  transfers between devices with their start and end apart: 9, of which 9 were waited for; matrix products, arithmetic and copies ran while one was open for 3% of the time, Pallas kernels for 0%

profile of v6, /device:TPU:1, one launch (start us, length us, event | category | flops | bytes accessed | tf_op | source)
XLA Modules:
  0.0 238.9 jit_solution(15434999746009222980)
XLA Ops:
  4.1 58.0 %shard_map.94 = (bf16[4096,256]{1,0:T(8,128)(2,1)S(1)}, bf16[4096,256]{1,0:T(8,128)(2,1)S(1)}) custom-call(s32[16384]{0:T(1024)S(1)} %pad_add_fusion.place_ref, s32[16,256]{1,0:T(8,128)S(1)} %copy-done.7, f32[256,256]{1,0:T(8,128)S(1)} %bitcast.32, f32[1024,512]{1,0:T(8,128)} %orbitals_ref.1, f32[1024,512]{1,0:T(8,128)} %hop_ref.1, f32[1,256]{1,0:T(1,128)S(1)} %bitcast.33), custom_call_target="tpu_custom_call" | custom-call | tf_op jit(solution)/shard_map/pallas_call | solution.py:121
  65.3 10.0 %all-to-all-start = ((bf16[16,16,384]{2,1,0:T(8,128)(2,1)}), bf16[16,16,384]{2,1,0:T(8,128)(2,1)S(1)}, u32[]{:S(2)}, u32[]{:S(2)}) async-start(bf16[16,16,384]{2,1,0:T(8,128)(2,1)} %shard_map.95), calls=%async_computation | async-start | bytes 393216 | tf_op jit(solution)/shard_map/all_to_all | solution.py:168
  75.3 3.3 %convert_reduce_fusion = (f32[4096]{0:T(1024)S(1)}, f32[4096]{0:T(1024)S(1)}, f32[4096]{0:T(1024)S(1)}) fusion(bf16[4096,256]{1,0:T(8,128)(2,1)S(1)} %get-tuple-element.32.derivs_ref.refs_3_.refs_4_, bf16[4096,256]{1,0:T(8,128)(2,1)} %copy-done), kind=kLoop, calls=%fused_computation.1 | loop fusion | flops 6279168 | bytes 4243456 | tf_op jit(solution)/shard_map/reduce_sum | solution.py:150
  78.6 6.9 %all-to-all-done.refs_0_ = bf16[16,16,384]{2,1,0:T(8,128)(2,1)S(1)} async-done(((bf16[16,16,384]{2,1,0:T(8,128)(2,1)}), bf16[16,16,384]{2,1,0:T(8,128)(2,1)S(1)}, u32[]{:S(2)}, u32[]{:S(2)}) %all-to-all-start) | async-done | bytes 196640 | tf_op jit(solution)/shard_map/all_to_all | solution.py:168
  87.6 18.7 %all_to_all.55.refs_0_ = f32[16,24,384]{2,1,0:T(8,128)S(1)} all-to-all(f32[16,24,384]{2,1,0:T(8,128)S(1)} %get-tuple-element.35), channel_id=1, replica_groups=mesh['walker'=16,'param'=16] {'walker'}, dimensions={0} | all-to-all | bytes 1179648 | tf_op jit(solution)/shard_map/all_to_all | solution.py:168
  107.4 10.3 %all_to_all.56.got_ref = f32[16,8,384]{2,1,0:T(8,128)S(1)} all-to-all(f32[16,8,384]{2,1,0:T(8,128)S(1)} %get-tuple-element.37), channel_id=1, replica_groups=mesh['walker'=16,'param'=16] {'walker'}, dimensions={0} | all-to-all | bytes 393216 | tf_op jit(solution)/shard_map/all_to_all | solution.py:168
  119.0 5.5 %all-to-all-start.3 = ((bf16[16,16,384]{2,1,0:T(8,128)(2,1)}), bf16[16,16,384]{2,1,0:T(8,128)(2,1)S(1)}, u32[]{:S(2)}, u32[]{:S(2)}) async-start(bf16[16,16,384]{2,1,0:T(8,128)(2,1)} %shard_map.98), calls=%async_computation.3 | async-start | bytes 393216 | tf_op jit(solution)/shard_map/all_to_all | solution.py:168
  124.8 10.0 %all-to-all-done.3.refs_0_ = bf16[16,16,384]{2,1,0:T(8,128)(2,1)S(1)} async-done(((bf16[16,16,384]{2,1,0:T(8,128)(2,1)}), bf16[16,16,384]{2,1,0:T(8,128)(2,1)S(1)}, u32[]{:S(2)}, u32[]{:S(2)}) %all-to-all-start.3) | async-done | bytes 196640 | tf_op jit(solution)/shard_map/all_to_all | solution.py:168
  134.9 2.4 %shard_map.99 = (f32[8,768]{1,0:T(8,128)S(1)}, f32[8,128]{1,0:T(8,128)S(1)}, f32[8,128]{1,0:T(8,128)S(1)}, f32[16,256]{1,0:T(8,128)S(1)}, bf16[16,16,384]{2,1,0:T(8,128)(2,1)}) custom-call(bf16[16,16,384]{2,1,0:T(8,128)(2,1)S(1)} %all-to-all-done.3.refs_0_, f32[8,256]{1,0:T(8,128)S(1)} %get-tuple-element.38.refs_1_, ...), custom_call_target="tpu_custom_call" | custom-call | tf_op jit(solution)/shard_map/pallas_call | solution.py:393
  137.3 3.5 %all-to-all-start.4 = ((bf16[16,16,384]{2,1,0:T(8,128)(2,1)}), bf16[16,16,384]{2,1,0:T(8,128)(2,1)S(1)}, u32[]{:S(2)}, u32[]{:S(2)}) async-start(bf16[16,16,384]{2,1,0:T(8,128)(2,1)} %get-tuple-element.42), calls=%async_computation.4 | async-start | bytes 393216 | tf_op jit(solution)/shard_map/all_to_all | solution.py:168
  141.0 7.3 %all-to-all-done.4.refs_0_ = bf16[16,16,384]{2,1,0:T(8,128)(2,1)S(1)} async-done(((bf16[16,16,384]{2,1,0:T(8,128)(2,1)}), bf16[16,16,384]{2,1,0:T(8,128)(2,1)S(1)}, u32[]{:S(2)}, u32[]{:S(2)}) %all-to-all-start.4) | async-done | bytes 196640 | tf_op jit(solution)/shard_map/all_to_all | solution.py:168
  150.1 3.6 %all-to-all-start.5 = ((f32[16,8,384]{2,1,0:T(8,128)}), f32[16,8,384]{2,1,0:T(8,128)S(1)}, u32[]{:S(2)}, u32[]{:S(2)}) async-start(f32[16,8,384]{2,1,0:T(8,128)} %get-tuple-element.45), calls=%async_computation.5 | async-start | bytes 393216 | tf_op jit(solution)/shard_map/all_to_all | solution.py:168
  153.8 6.9 %all-to-all-done.5.got_ref = f32[16,8,384]{2,1,0:T(8,128)S(1)} async-done(((f32[16,8,384]{2,1,0:T(8,128)}), f32[16,8,384]{2,1,0:T(8,128)S(1)}, u32[]{:S(2)}, u32[]{:S(2)}) %all-to-all-start.5) | async-done | bytes 196640 | tf_op jit(solution)/shard_map/all_to_all | solution.py:168
  163.6 5.7 %all-to-all-start.6 = ((bf16[16,16,384]{2,1,0:T(8,128)(2,1)}), bf16[16,16,384]{2,1,0:T(8,128)(2,1)S(1)}, u32[]{:S(2)}, u32[]{:S(2)}) async-start(bf16[16,16,384]{2,1,0:T(8,128)(2,1)} %shard_map.101), calls=%async_computation.6 | async-start | bytes 393216 | tf_op jit(solution)/shard_map/all_to_all | solution.py:168
  169.7 10.1 %all-to-all-done.6.refs_0_ = bf16[16,16,384]{2,1,0:T(8,128)(2,1)S(1)} async-done(((bf16[16,16,384]{2,1,0:T(8,128)(2,1)}), bf16[16,16,384]{2,1,0:T(8,128)(2,1)S(1)}, u32[]{:S(2)}, u32[]{:S(2)}) %all-to-all-start.6) | async-done | bytes 196640 | tf_op jit(solution)/shard_map/all_to_all | solution.py:168
  179.7 2.4 %shard_map.102 = (f32[8,768]{1,0:T(8,128)S(1)}, f32[8,128]{1,0:T(8,128)S(1)}, f32[8,128]{1,0:T(8,128)S(1)}, f32[16,256]{1,0:T(8,128)S(1)}, bf16[16,16,384]{2,1,0:T(8,128)(2,1)}) custom-call(bf16[16,16,384]{2,1,0:T(8,128)(2,1)S(1)} %all-to-all-done.6.refs_0_, f32[8,256]{1,0:T(8,128)S(1)} %get-tuple-element.46.refs_1_, ...), custom_call_target="tpu_custom_call" | custom-call | tf_op jit(solution)/shard_map/pallas_call | solution.py:393
  182.2 3.5 %all-to-all-start.7 = ((bf16[16,16,384]{2,1,0:T(8,128)(2,1)}), bf16[16,16,384]{2,1,0:T(8,128)(2,1)S(1)}, u32[]{:S(2)}, u32[]{:S(2)}) async-start(bf16[16,16,384]{2,1,0:T(8,128)(2,1)} %get-tuple-element.49), calls=%async_computation.7 | async-start | bytes 393216 | tf_op jit(solution)/shard_map/all_to_all | solution.py:168
  186.1 7.1 %all-to-all-done.7.refs_0_ = bf16[16,16,384]{2,1,0:T(8,128)(2,1)S(1)} async-done(((bf16[16,16,384]{2,1,0:T(8,128)(2,1)}), bf16[16,16,384]{2,1,0:T(8,128)(2,1)S(1)}, u32[]{:S(2)}, u32[]{:S(2)}) %all-to-all-start.7) | async-done | bytes 196640 | tf_op jit(solution)/shard_map/all_to_all | solution.py:168
  195.0 3.6 %all-to-all-start.8 = ((f32[16,8,384]{2,1,0:T(8,128)}), f32[16,8,384]{2,1,0:T(8,128)S(1)}, u32[]{:S(2)}, u32[]{:S(2)}) async-start(f32[16,8,384]{2,1,0:T(8,128)} %get-tuple-element.51), calls=%async_computation.8 | async-start | bytes 393216 | tf_op jit(solution)/shard_map/all_to_all | solution.py:168
  198.9 6.7 %all-to-all-done.8.got_ref = f32[16,8,384]{2,1,0:T(8,128)S(1)} async-done(((f32[16,8,384]{2,1,0:T(8,128)}), f32[16,8,384]{2,1,0:T(8,128)S(1)}, u32[]{:S(2)}, u32[]{:S(2)}) %all-to-all-start.8) | async-done | bytes 196640 | tf_op jit(solution)/shard_map/all_to_all | solution.py:168
  208.5 5.7 %all-to-all-start.9 = ((bf16[16,16,384]{2,1,0:T(8,128)(2,1)}), bf16[16,16,384]{2,1,0:T(8,128)(2,1)S(1)}, u32[]{:S(2)}, u32[]{:S(2)}) async-start(bf16[16,16,384]{2,1,0:T(8,128)(2,1)} %shard_map.104), calls=%async_computation.9 | async-start | bytes 393216 | tf_op jit(solution)/shard_map/all_to_all | solution.py:168
  214.6 10.0 %all-to-all-done.9.refs_0_ = bf16[16,16,384]{2,1,0:T(8,128)(2,1)S(1)} async-done(((bf16[16,16,384]{2,1,0:T(8,128)(2,1)}), bf16[16,16,384]{2,1,0:T(8,128)(2,1)S(1)}, u32[]{:S(2)}, u32[]{:S(2)}) %all-to-all-start.9) | async-done | bytes 196640 | tf_op jit(solution)/shard_map/all_to_all | solution.py:168
  226.6 3.5 %all-to-all-start.10 = ((f32[16,32,128]{2,1,0:T(8,128)}), f32[16,32,128]{2,1,0:T(8,128)S(1)}, u32[]{:S(2)}, u32[]{:S(2)}) async-start(f32[16,32,128]{2,1,0:T(8,128)} %get-tuple-element.58), calls=%async_computation.10 | async-start | bytes 524288 | tf_op jit(solution)/shard_map/all_to_all | solution.py:168
  231.6 6.6 %all-to-all-done.10.got_ref = f32[16,32,128]{2,1,0:T(8,128)S(1)} async-done(((f32[16,32,128]{2,1,0:T(8,128)}), f32[16,32,128]{2,1,0:T(8,128)S(1)}, u32[]{:S(2)}, u32[]{:S(2)}) %all-to-all-start.10) | async-done | bytes 262176 | tf_op jit(solution)/shard_map/all_to_all | solution.py:168
  (56 shorter events, 26.3 us)
Async XLA Ops:
  1.7 1.0 copy-start.6
  2.7 0.7 copy-start.7
  3.4 0.7 copy-start.8
  4.1 58.0 %copy-start.5 = (f32[4096,8]{0,1:T(8,128)S(1)}, f32[4096,8]{0,1:T(8,128)}, u32[]{:S(2)}) copy-start(f32[4096,8]{0,1:T(8,128)} %param.13) | copy-start | bytes 393220
  63.9 1.4 copy-start
  65.3 20.3 %all-to-all-start = ((bf16[16,16,384]{2,1,0:T(8,128)(2,1)}), bf16[16,16,384]{2,1,0:T(8,128)(2,1)S(1)}, u32[]{:S(2)}, u32[]{:S(2)}) async-start(bf16[16,16,384]{2,1,0:T(8,128)(2,1)} %shard_map.95), calls=%async_computation | async-start | bytes 393216 | tf_op jit(solution)/shard_map/all_to_all | solution.py:168
  85.6 32.1 %copy-start.1 = (bf16[4096,256]{1,0:T(8,128)(2,1)S(1)}, bf16[4096,256]{1,0:T(8,128)(2,1)}, u32[]{:S(2)}) copy-start(bf16[4096,256]{1,0:T(8,128)(2,1)} %copy-done) | copy-start | bytes 6291460
  117.6 36.1 %copy-start.4 = (f32[16,8,384]{2,1,0:T(8,128)}, f32[16,8,384]{2,1,0:T(8,128)S(1)}, u32[]{:S(2)}) copy-start(f32[16,8,384]{2,1,0:T(8,128)S(1)} %all_to_all.56.got_ref) | copy-start | bytes 589828
  119.0 15.9 %all-to-all-start.3 = ((bf16[16,16,384]{2,1,0:T(8,128)(2,1)}), bf16[16,16,384]{2,1,0:T(8,128)(2,1)S(1)}, u32[]{:S(2)}, u32[]{:S(2)}) async-start(bf16[16,16,384]{2,1,0:T(8,128)(2,1)} %shard_map.98), calls=%async_computation.3 | async-start | bytes 393216 | tf_op jit(solution)/shard_map/all_to_all | solution.py:168
  137.3 11.0 %all-to-all-start.4 = ((bf16[16,16,384]{2,1,0:T(8,128)(2,1)}), bf16[16,16,384]{2,1,0:T(8,128)(2,1)S(1)}, u32[]{:S(2)}, u32[]{:S(2)}) async-start(bf16[16,16,384]{2,1,0:T(8,128)(2,1)} %get-tuple-element.42), calls=%async_computation.4 | async-start | bytes 393216 | tf_op jit(solution)/shard_map/all_to_all | solution.py:168
  150.1 10.6 %all-to-all-start.5 = ((f32[16,8,384]{2,1,0:T(8,128)}), f32[16,8,384]{2,1,0:T(8,128)S(1)}, u32[]{:S(2)}, u32[]{:S(2)}) async-start(f32[16,8,384]{2,1,0:T(8,128)} %get-tuple-element.45), calls=%async_computation.5 | async-start | bytes 393216 | tf_op jit(solution)/shard_map/all_to_all | solution.py:168
  160.7 1.6 copy-start.2
  162.3 7.1 %slice-start = ((f32[16,8,384]{2,1,0:T(8,128)}), f32[16,8,256]{2,1,0:T(8,128)S(1)}, s32[]{:S(2)}) async-start(f32[16,8,384]{2,1,0:T(8,128)} %copy-done.4), calls=%async_computation.11 | async-start | bytes 262144 | tf_op jit(solution)/shard_map/slice | solution.py:461
  163.6 16.1 %all-to-all-start.6 = ((bf16[16,16,384]{2,1,0:T(8,128)(2,1)}), bf16[16,16,384]{2,1,0:T(8,128)(2,1)S(1)}, u32[]{:S(2)}, u32[]{:S(2)}) async-start(bf16[16,16,384]{2,1,0:T(8,128)(2,1)} %shard_map.101), calls=%async_computation.6 | async-start | bytes 393216 | tf_op jit(solution)/shard_map/all_to_all | solution.py:168
  182.2 11.0 %all-to-all-start.7 = ((bf16[16,16,384]{2,1,0:T(8,128)(2,1)}), bf16[16,16,384]{2,1,0:T(8,128)(2,1)S(1)}, u32[]{:S(2)}, u32[]{:S(2)}) async-start(bf16[16,16,384]{2,1,0:T(8,128)(2,1)} %get-tuple-element.49), calls=%async_computation.7 | async-start | bytes 393216 | tf_op jit(solution)/shard_map/all_to_all | solution.py:168
  195.0 10.6 %all-to-all-start.8 = ((f32[16,8,384]{2,1,0:T(8,128)}), f32[16,8,384]{2,1,0:T(8,128)S(1)}, u32[]{:S(2)}, u32[]{:S(2)}) async-start(f32[16,8,384]{2,1,0:T(8,128)} %get-tuple-element.51), calls=%async_computation.8 | async-start | bytes 393216 | tf_op jit(solution)/shard_map/all_to_all | solution.py:168
  205.6 1.6 copy-start.3
  208.5 16.1 %all-to-all-start.9 = ((bf16[16,16,384]{2,1,0:T(8,128)(2,1)}), bf16[16,16,384]{2,1,0:T(8,128)(2,1)S(1)}, u32[]{:S(2)}, u32[]{:S(2)}) async-start(bf16[16,16,384]{2,1,0:T(8,128)(2,1)} %shard_map.104), calls=%async_computation.9 | async-start | bytes 393216 | tf_op jit(solution)/shard_map/all_to_all | solution.py:168
  226.6 11.6 %all-to-all-start.10 = ((f32[16,32,128]{2,1,0:T(8,128)}), f32[16,32,128]{2,1,0:T(8,128)S(1)}, u32[]{:S(2)}, u32[]{:S(2)}) async-start(f32[16,32,128]{2,1,0:T(8,128)} %get-tuple-element.58), calls=%async_computation.10 | async-start | bytes 524288 | tf_op jit(solution)/shard_map/all_to_all | solution.py:168

commit v7 on v6

--- a/solution.py
+++ b/solution.py
@@ -14,7 +14,7 @@
 HIGHEST = lax.Precision.HIGHEST
 LANES = 128
 ROWS = 8
-GROUP = 64
+GROUP = 128
 
 
 def build_kernel(
@@ -111,12 +111,11 @@
     sites, orbital_count = orbitals.shape
     params = excitations.shape[1]
 
-    def place(electron, orbital):
-        row = electron * orbital_count + orbital
-        return row * 4
-
-    i, j, a, b = excitations
-    places = jnp.concatenate([place(i, a), place(j, b), place(i, b), place(j, a)])
+    electron_rows = excitations[:2] * (4 * orbital_count)
+    orbital_rows = excitations[2:] * 4
+    places = jnp.concatenate(
+        [electron_rows + orbital_rows, electron_rows + orbital_rows[::-1]]
+    ).reshape(-1)
     vmem = pl.BlockSpec(memory_space=pltpu.VMEM)
     return pl.pallas_call(
         build_kernel,

time: 240 us -> 242 us (level)
    unnamed x20 -> x21, local copies, waits for them, and re-layouts: 6.9 us -> 6.91 us
where the time goes in v7:
time: 242 us; the launch traced here: 240 us
  Pallas kernels  77.8 us (32%)
  waiting for transfers between devices  71.6 us (30%)
  starting transfers between devices  44.8 us (19%)
  blocking collectives  29 us (12%)
  local copies, waits for them, and re-layouts  8.76 us (4%)
  other arithmetic  5.27 us (2%)
    all_to_all x9, waiting for transfers between devices, exchange(): return lax.all_to_all(parts, axis, 0, 0)  71.6 us
    pallas_call x1, Pallas kernels, build(): pl.pallas_call(build_kernel, out_shape=[jax.ShapeDtypeStruct((params, wal...  57.9 us
    all_to_all x9, starting transfers between devices, exchange(): return lax.all_to_all(parts, axis, 0, 0)  44.8 us
    all_to_all x2, blocking collectives, exchange(): return lax.all_to_all(parts, axis, 0, 0)  29 us
    pallas_call x12, Pallas kernels, stage(): pl.pallas_call(body, out_shape=[jax.ShapeDtypeStruct(shape, dtype) for sh...  19.9 us
    unnamed x21, local copies, waits for them, and re-layouts  6.91 us
  transfers between devices with their start and end apart: 9, of which 9 were waited for; matrix products, arithmetic and copies ran while one was open for 3% of the time, Pallas kernels for 0%

profile of v7, /device:TPU:1, one launch (start us, length us, event | category | flops | bytes accessed | tf_op | source)
XLA Modules:
  0.0 240.3 jit_solution(12215014869884195322)
XLA Ops:
  5.7 57.9 %shard_map.94 = (bf16[4096,256]{1,0:T(8,128)(2,1)S(1)}, bf16[4096,256]{1,0:T(8,128)(2,1)S(1)}) custom-call(s32[16384]{0:T(1024)S(1)} %bitcast.31, s32[16,256]{1,0:T(8,128)S(1)} %copy-done.7, f32[256,256]{1,0:T(8,128)S(1)} %bitcast.32, f32[1024,512]{1,0:T(8,128)} %orbitals_ref.1, f32[1024,512]{1,0:T(8,128)} %hop_ref.1, f32[1,256]{1,0:T(1,128)S(1)} %bitcast.33), custom_call_target="tpu_custom_call" | custom-call | tf_op jit(solution)/shard_map/pallas_call | solution.py:120
  66.7 10.0 %all-to-all-start = ((bf16[16,16,384]{2,1,0:T(8,128)(2,1)}), bf16[16,16,384]{2,1,0:T(8,128)(2,1)S(1)}, u32[]{:S(2)}, u32[]{:S(2)}) async-start(bf16[16,16,384]{2,1,0:T(8,128)(2,1)} %shard_map.95), calls=%async_computation | async-start | bytes 393216 | tf_op jit(solution)/shard_map/all_to_all | solution.py:167
  76.7 3.3 %convert_reduce_fusion = (f32[4096]{0:T(1024)S(1)}, f32[4096]{0:T(1024)S(1)}, f32[4096]{0:T(1024)S(1)}) fusion(bf16[4096,256]{1,0:T(8,128)(2,1)S(1)} %get-tuple-element.32.derivs_ref.refs_3_.refs_4_, bf16[4096,256]{1,0:T(8,128)(2,1)} %copy-done), kind=kLoop, calls=%fused_computation.1 | loop fusion | flops 6279168 | bytes 4243456 | tf_op jit(solution)/shard_map/reduce_sum | solution.py:149
  80.1 6.9 %all-to-all-done.refs_0_ = bf16[16,16,384]{2,1,0:T(8,128)(2,1)S(1)} async-done(((bf16[16,16,384]{2,1,0:T(8,128)(2,1)}), bf16[16,16,384]{2,1,0:T(8,128)(2,1)S(1)}, u32[]{:S(2)}, u32[]{:S(2)}) %all-to-all-start) | async-done | bytes 196640 | tf_op jit(solution)/shard_map/all_to_all | solution.py:167
  89.0 18.7 %all_to_all.55.refs_0_ = f32[16,24,384]{2,1,0:T(8,128)S(1)} all-to-all(f32[16,24,384]{2,1,0:T(8,128)S(1)} %get-tuple-element.35), channel_id=1, replica_groups=mesh['walker'=16,'param'=16] {'walker'}, dimensions={0} | all-to-all | bytes 1179648 | tf_op jit(solution)/shard_map/all_to_all | solution.py:167
  108.8 10.3 %all_to_all.56.got_ref = f32[16,8,384]{2,1,0:T(8,128)S(1)} all-to-all(f32[16,8,384]{2,1,0:T(8,128)S(1)} %get-tuple-element.37), channel_id=1, replica_groups=mesh['walker'=16,'param'=16] {'walker'}, dimensions={0} | all-to-all | bytes 393216 | tf_op jit(solution)/shard_map/all_to_all | solution.py:167
  120.4 5.5 %all-to-all-start.3 = ((bf16[16,16,384]{2,1,0:T(8,128)(2,1)}), bf16[16,16,384]{2,1,0:T(8,128)(2,1)S(1)}, u32[]{:S(2)}, u32[]{:S(2)}) async-start(bf16[16,16,384]{2,1,0:T(8,128)(2,1)} %shard_map.98), calls=%async_computation.3 | async-start | bytes 393216 | tf_op jit(solution)/shard_map/all_to_all | solution.py:167
  126.2 10.0 %all-to-all-done.3.refs_0_ = bf16[16,16,384]{2,1,0:T(8,128)(2,1)S(1)} async-done(((bf16[16,16,384]{2,1,0:T(8,128)(2,1)}), bf16[16,16,384]{2,1,0:T(8,128)(2,1)S(1)}, u32[]{:S(2)}, u32[]{:S(2)}) %all-to-all-start.3) | async-done | bytes 196640 | tf_op jit(solution)/shard_map/all_to_all | solution.py:167
  136.3 2.4 %shard_map.99 = (f32[8,768]{1,0:T(8,128)S(1)}, f32[8,128]{1,0:T(8,128)S(1)}, f32[8,128]{1,0:T(8,128)S(1)}, f32[16,256]{1,0:T(8,128)S(1)}, bf16[16,16,384]{2,1,0:T(8,128)(2,1)}) custom-call(bf16[16,16,384]{2,1,0:T(8,128)(2,1)S(1)} %all-to-all-done.3.refs_0_, f32[8,256]{1,0:T(8,128)S(1)} %get-tuple-element.38.refs_1_, ...), custom_call_target="tpu_custom_call" | custom-call | tf_op jit(solution)/shard_map/pallas_call | solution.py:392
  138.7 3.5 %all-to-all-start.4 = ((bf16[16,16,384]{2,1,0:T(8,128)(2,1)}), bf16[16,16,384]{2,1,0:T(8,128)(2,1)S(1)}, u32[]{:S(2)}, u32[]{:S(2)}) async-start(bf16[16,16,384]{2,1,0:T(8,128)(2,1)} %get-tuple-element.42), calls=%async_computation.4 | async-start | bytes 393216 | tf_op jit(solution)/shard_map/all_to_all | solution.py:167
  142.4 7.3 %all-to-all-done.4.refs_0_ = bf16[16,16,384]{2,1,0:T(8,128)(2,1)S(1)} async-done(((bf16[16,16,384]{2,1,0:T(8,128)(2,1)}), bf16[16,16,384]{2,1,0:T(8,128)(2,1)S(1)}, u32[]{:S(2)}, u32[]{:S(2)}) %all-to-all-start.4) | async-done | bytes 196640 | tf_op jit(solution)/shard_map/all_to_all | solution.py:167
  151.5 3.6 %all-to-all-start.5 = ((f32[16,8,384]{2,1,0:T(8,128)}), f32[16,8,384]{2,1,0:T(8,128)S(1)}, u32[]{:S(2)}, u32[]{:S(2)}) async-start(f32[16,8,384]{2,1,0:T(8,128)} %get-tuple-element.45), calls=%async_computation.5 | async-start | bytes 393216 | tf_op jit(solution)/shard_map/all_to_all | solution.py:167
  155.2 6.9 %all-to-all-done.5.got_ref = f32[16,8,384]{2,1,0:T(8,128)S(1)} async-done(((f32[16,8,384]{2,1,0:T(8,128)}), f32[16,8,384]{2,1,0:T(8,128)S(1)}, u32[]{:S(2)}, u32[]{:S(2)}) %all-to-all-start.5) | async-done | bytes 196640 | tf_op jit(solution)/shard_map/all_to_all | solution.py:167
  165.0 5.7 %all-to-all-start.6 = ((bf16[16,16,384]{2,1,0:T(8,128)(2,1)}), bf16[16,16,384]{2,1,0:T(8,128)(2,1)S(1)}, u32[]{:S(2)}, u32[]{:S(2)}) async-start(bf16[16,16,384]{2,1,0:T(8,128)(2,1)} %shard_map.101), calls=%async_computation.6 | async-start | bytes 393216 | tf_op jit(solution)/shard_map/all_to_all | solution.py:167
  171.1 10.1 %all-to-all-done.6.refs_0_ = bf16[16,16,384]{2,1,0:T(8,128)(2,1)S(1)} async-done(((bf16[16,16,384]{2,1,0:T(8,128)(2,1)}), bf16[16,16,384]{2,1,0:T(8,128)(2,1)S(1)}, u32[]{:S(2)}, u32[]{:S(2)}) %all-to-all-start.6) | async-done | bytes 196640 | tf_op jit(solution)/shard_map/all_to_all | solution.py:167
  181.2 2.4 %shard_map.102 = (f32[8,768]{1,0:T(8,128)S(1)}, f32[8,128]{1,0:T(8,128)S(1)}, f32[8,128]{1,0:T(8,128)S(1)}, f32[16,256]{1,0:T(8,128)S(1)}, bf16[16,16,384]{2,1,0:T(8,128)(2,1)}) custom-call(bf16[16,16,384]{2,1,0:T(8,128)(2,1)S(1)} %all-to-all-done.6.refs_0_, f32[8,256]{1,0:T(8,128)S(1)} %get-tuple-element.46.refs_1_, ...), custom_call_target="tpu_custom_call" | custom-call | tf_op jit(solution)/shard_map/pallas_call | solution.py:392
  183.6 3.5 %all-to-all-start.7 = ((bf16[16,16,384]{2,1,0:T(8,128)(2,1)}), bf16[16,16,384]{2,1,0:T(8,128)(2,1)S(1)}, u32[]{:S(2)}, u32[]{:S(2)}) async-start(bf16[16,16,384]{2,1,0:T(8,128)(2,1)} %get-tuple-element.49), calls=%async_computation.7 | async-start | bytes 393216 | tf_op jit(solution)/shard_map/all_to_all | solution.py:167
  187.5 7.1 %all-to-all-done.7.refs_0_ = bf16[16,16,384]{2,1,0:T(8,128)(2,1)S(1)} async-done(((bf16[16,16,384]{2,1,0:T(8,128)(2,1)}), bf16[16,16,384]{2,1,0:T(8,128)(2,1)S(1)}, u32[]{:S(2)}, u32[]{:S(2)}) %all-to-all-start.7) | async-done | bytes 196640 | tf_op jit(solution)/shard_map/all_to_all | solution.py:167
  196.4 3.6 %all-to-all-start.8 = ((f32[16,8,384]{2,1,0:T(8,128)}), f32[16,8,384]{2,1,0:T(8,128)S(1)}, u32[]{:S(2)}, u32[]{:S(2)}) async-start(f32[16,8,384]{2,1,0:T(8,128)} %get-tuple-element.51), calls=%async_computation.8 | async-start | bytes 393216 | tf_op jit(solution)/shard_map/all_to_all | solution.py:167
  200.3 6.7 %all-to-all-done.8.got_ref = f32[16,8,384]{2,1,0:T(8,128)S(1)} async-done(((f32[16,8,384]{2,1,0:T(8,128)}), f32[16,8,384]{2,1,0:T(8,128)S(1)}, u32[]{:S(2)}, u32[]{:S(2)}) %all-to-all-start.8) | async-done | bytes 196640 | tf_op jit(solution)/shard_map/all_to_all | solution.py:167
  209.9 5.7 %all-to-all-start.9 = ((bf16[16,16,384]{2,1,0:T(8,128)(2,1)}), bf16[16,16,384]{2,1,0:T(8,128)(2,1)S(1)}, u32[]{:S(2)}, u32[]{:S(2)}) async-start(bf16[16,16,384]{2,1,0:T(8,128)(2,1)} %shard_map.104), calls=%async_computation.9 | async-start | bytes 393216 | tf_op jit(solution)/shard_map/all_to_all | solution.py:167
  216.0 10.0 %all-to-all-done.9.refs_0_ = bf16[16,16,384]{2,1,0:T(8,128)(2,1)S(1)} async-done(((bf16[16,16,384]{2,1,0:T(8,128)(2,1)}), bf16[16,16,384]{2,1,0:T(8,128)(2,1)S(1)}, u32[]{:S(2)}, u32[]{:S(2)}) %all-to-all-start.9) | async-done | bytes 196640 | tf_op jit(solution)/shard_map/all_to_all | solution.py:167
  228.0 3.5 %all-to-all-start.10 = ((f32[16,32,128]{2,1,0:T(8,128)}), f32[16,32,128]{2,1,0:T(8,128)S(1)}, u32[]{:S(2)}, u32[]{:S(2)}) async-start(f32[16,32,128]{2,1,0:T(8,128)} %get-tuple-element.58), calls=%async_computation.10 | async-start | bytes 524288 | tf_op jit(solution)/shard_map/all_to_all | solution.py:167
  233.0 6.6 %all-to-all-done.10.got_ref = f32[16,32,128]{2,1,0:T(8,128)S(1)} async-done(((f32[16,32,128]{2,1,0:T(8,128)}), f32[16,32,128]{2,1,0:T(8,128)S(1)}, u32[]{:S(2)}, u32[]{:S(2)}) %all-to-all-start.10) | async-done | bytes 262176 | tf_op jit(solution)/shard_map/all_to_all | solution.py:167
  (59 shorter events, 27.9 us)
Async XLA Ops:
  3.3 1.0 copy-start.6
  4.3 0.7 copy-start.7
  5.0 0.7 copy-start.8
  5.7 57.9 %copy-start.5 = (f32[4096,8]{0,1:T(8,128)S(1)}, f32[4096,8]{0,1:T(8,128)}, u32[]{:S(2)}) copy-start(f32[4096,8]{0,1:T(8,128)} %param.13) | copy-start | bytes 393220
  65.4 1.4 copy-start
  66.7 20.3 %all-to-all-start = ((bf16[16,16,384]{2,1,0:T(8,128)(2,1)}), bf16[16,16,384]{2,1,0:T(8,128)(2,1)S(1)}, u32[]{:S(2)}, u32[]{:S(2)}) async-start(bf16[16,16,384]{2,1,0:T(8,128)(2,1)} %shard_map.95), calls=%async_computation | async-start | bytes 393216 | tf_op jit(solution)/shard_map/all_to_all | solution.py:167
  87.0 32.0 %copy-start.1 = (bf16[4096,256]{1,0:T(8,128)(2,1)S(1)}, bf16[4096,256]{1,0:T(8,128)(2,1)}, u32[]{:S(2)}) copy-start(bf16[4096,256]{1,0:T(8,128)(2,1)} %copy-done) | copy-start | bytes 6291460
  119.1 36.1 %copy-start.4 = (f32[16,8,384]{2,1,0:T(8,128)}, f32[16,8,384]{2,1,0:T(8,128)S(1)}, u32[]{:S(2)}) copy-start(f32[16,8,384]{2,1,0:T(8,128)S(1)} %all_to_all.56.got_ref) | copy-start | bytes 589828
  120.4 15.9 %all-to-all-start.3 = ((bf16[16,16,384]{2,1,0:T(8,128)(2,1)}), bf16[16,16,384]{2,1,0:T(8,128)(2,1)S(1)}, u32[]{:S(2)}, u32[]{:S(2)}) async-start(bf16[16,16,384]{2,1,0:T(8,128)(2,1)} %shard_map.98), calls=%async_computation.3 | async-start | bytes 393216 | tf_op jit(solution)/shard_map/all_to_all | solution.py:167
  138.7 11.0 %all-to-all-start.4 = ((bf16[16,16,384]{2,1,0:T(8,128)(2,1)}), bf16[16,16,384]{2,1,0:T(8,128)(2,1)S(1)}, u32[]{:S(2)}, u32[]{:S(2)}) async-start(bf16[16,16,384]{2,1,0:T(8,128)(2,1)} %get-tuple-element.42), calls=%async_computation.4 | async-start | bytes 393216 | tf_op jit(solution)/shard_map/all_to_all | solution.py:167
  151.5 10.6 %all-to-all-start.5 = ((f32[16,8,384]{2,1,0:T(8,128)}), f32[16,8,384]{2,1,0:T(8,128)S(1)}, u32[]{:S(2)}, u32[]{:S(2)}) async-start(f32[16,8,384]{2,1,0:T(8,128)} %get-tuple-element.45), calls=%async_computation.5 | async-start | bytes 393216 | tf_op jit(solution)/shard_map/all_to_all | solution.py:167
  162.1 1.6 copy-start.2
  163.7 7.1 %slice-start = ((f32[16,8,384]{2,1,0:T(8,128)}), f32[16,8,256]{2,1,0:T(8,128)S(1)}, s32[]{:S(2)}) async-start(f32[16,8,384]{2,1,0:T(8,128)} %copy-done.4), calls=%async_computation.11 | async-start | bytes 262144 | tf_op jit(solution)/shard_map/slice | solution.py:460
  165.0 16.1 %all-to-all-start.6 = ((bf16[16,16,384]{2,1,0:T(8,128)(2,1)}), bf16[16,16,384]{2,1,0:T(8,128)(2,1)S(1)}, u32[]{:S(2)}, u32[]{:S(2)}) async-start(bf16[16,16,384]{2,1,0:T(8,128)(2,1)} %shard_map.101), calls=%async_computation.6 | async-start | bytes 393216 | tf_op jit(solution)/shard_map/all_to_all | solution.py:167
  183.6 11.0 %all-to-all-start.7 = ((bf16[16,16,384]{2,1,0:T(8,128)(2,1)}), bf16[16,16,384]{2,1,0:T(8,128)(2,1)S(1)}, u32[]{:S(2)}, u32[]{:S(2)}) async-start(bf16[16,16,384]{2,1,0:T(8,128)(2,1)} %get-tuple-element.49), calls=%async_computation.7 | async-start | bytes 393216 | tf_op jit(solution)/shard_map/all_to_all | solution.py:167
  196.4 10.6 %all-to-all-start.8 = ((f32[16,8,384]{2,1,0:T(8,128)}), f32[16,8,384]{2,1,0:T(8,128)S(1)}, u32[]{:S(2)}, u32[]{:S(2)}) async-start(f32[16,8,384]{2,1,0:T(8,128)} %get-tuple-element.51), calls=%async_computation.8 | async-start | bytes 393216 | tf_op jit(solution)/shard_map/all_to_all | solution.py:167
  207.0 1.6 copy-start.3
  209.9 16.1 %all-to-all-start.9 = ((bf16[16,16,384]{2,1,0:T(8,128)(2,1)}), bf16[16,16,384]{2,1,0:T(8,128)(2,1)S(1)}, u32[]{:S(2)}, u32[]{:S(2)}) async-start(bf16[16,16,384]{2,1,0:T(8,128)(2,1)} %shard_map.104), calls=%async_computation.9 | async-start | bytes 393216 | tf_op jit(solution)/shard_map/all_to_all | solution.py:167
  228.0 11.6 %all-to-all-start.10 = ((f32[16,32,128]{2,1,0:T(8,128)}), f32[16,32,128]{2,1,0:T(8,128)S(1)}, u32[]{:S(2)}, u32[]{:S(2)}) async-start(f32[16,32,128]{2,1,0:T(8,128)} %get-tuple-element.58), calls=%async_computation.10 | async-start | bytes 524288 | tf_op jit(solution)/shard_map/all_to_all | solution.py:167
